TPU v7x, 32 devices: a whole 2x2x4 slice. The times are simulated.
32 devices in a mesh: dp: 4 (over z), fsdp: 8 (over y, x, core).
Axes of the slice: x: 2, y: 2, z: 4, core: 2. Of those that a mesh axis runs over, the one named last changes fastest.
Arguments:
- input_token_ids: int32 [2, 32, 256], P(None, ('dp', 'fsdp')), may hold values from 0 to 50303
- lengths: int32 [2, 32], P(None, ('dp', 'fsdp')), may hold values from 64 to 256, as said below
- scored_slots: int32 [2, 32, 32], P(None, ('dp', 'fsdp')), may hold values from 0 to 255, as said below
- scored_targets: int32 [2, 32, 32], P(None, ('dp', 'fsdp')), may hold values from 0 to 50303
- wte: bfloat16 [50304, 1024], P('fsdp'), may hold values from -0.359375 to 0.359375
- wpe: bfloat16 [256, 1024], replicated, may hold values from -0.359375 to 0.359375
- frozen_attention: bfloat16 [2, 1024, 4096], P(None, 'fsdp'), may hold values from -0.25 to 0.25
- frozen_feed_input: bfloat16 [2, 1024, 4096], P(None, 'fsdp'), may hold values from -0.1875 to 0.1875
- frozen_feed_output: bfloat16 [2, 4096, 1024], P(None, 'fsdp'), may hold values from -0.09375 to 0.09375
- frozen_bias_gain: bfloat16 [2, 13312], P(None, 'fsdp'), as said below
- final_norm_params: bfloat16 [2, 1024], replicated, as said below
- adapter_down: float32 [2, 1024, 12], replicated, may hold values from -0.1875 to 0.1875
- adapter_down_feed: float32 [2, 4096, 4], replicated, may hold values from -0.09375 to 0.09375
- adapter_up: float32 [2, 4, 9216], replicated, may hold values from -0.06 to 0.06
- first_moment_down: float32 [2, 1024, 12], replicated, may hold values from -3.8146973e-05 to 3.8146973e-05
- first_moment_feed: float32 [2, 4096, 4], replicated, may hold values from -3.8146973e-05 to 3.8146973e-05
- first_moment_up: float32 [2, 4, 9216], replicated, may hold values from -3.8146973e-05 to 3.8146973e-05
- second_moment_down: float32 [2, 1024, 12], replicated, may hold values from 3.0517578e-12 to 1.2207031e-11
- second_moment_feed: float32 [2, 4096, 4], replicated, may hold values from 3.0517578e-12 to 1.2207031e-11
- second_moment_up: float32 [2, 4, 9216], replicated, may hold values from 3.0517578e-12 to 1.2207031e-11
- optimizer_step: int32 [1], replicated, may hold values from 2 to 20
Outputs:
- loss: float32 [], replicated
- grad_norm: float32 [], replicated
- new_lora_a: float32 [2, 1024, 12], replicated
- new_lora_a_ff: float32 [2, 4096, 4], replicated
- new_lora_b: float32 [2, 4, 9216], replicated
- new_mom_a: float32 [2, 1024, 12], replicated
- new_mom_a_ff: float32 [2, 4096, 4], replicated
- new_mom_b: float32 [2, 4, 9216], replicated
- new_sq_a: float32 [2, 1024, 12], replicated
- new_sq_a_ff: float32 [2, 4096, 4], replicated
- new_sq_b: float32 [2, 4, 9216], replicated
- row_losses: float32 [2, 32, 32], P(None, ('dp', 'fsdp'))
Inputs may be any that keep to these rules, and one draw needn't show every extreme that they name: `lengths`: each row's live slots; some row holds all 256. `scored_slots`: the first listed position of each row lies under 64; positions may repeat. `frozen_bias_gain`: per layer: biases of the four projections, then the first norm's gain and shift, then the second's. `final_norm_params`: row 0 is the gain, row 1 the shift.
All inputs are finite; a program needn't handle non-finite values.
Results may differ from a plain program's by a relative error of at most 0.008.
Values may be sent and summed in bfloat16 or wider, within the bound.
No kernel may reach another device: no remote copies, remote signals or barrier semaphores. Data moves between devices by JAX's collectives and lax.ppermute only.
A program may use at most 256 MiB of HBM per device.

v0:
```python
from functools import partial

import jax
import jax.numpy as jnp
from jax import lax
from jax.sharding import PartitionSpec as P

MODEL_WIDTH = 1024
H = 16
HD = 64
HIDDEN_UNITS = 4096
ADAPTER_RANK = 4


ADAPTER_SCALE = 8.0
EPS_NORM = 1e-05
BETA_ONE = 0.9
BETA_TWO = 0.999
RATE = 0.02
DECAY = 0.01
EPS_ADAM = 1e-08
CLIP = 0.02
NEGATIVE = -1e30


def joined(x, axis, combine):
    everything = jax.tree.map(lambda part: lax.all_gather(part, axis), x)
    initial = jax.tree.map(lambda part: part[0], everything)

    def turn(k, so_far):
        return combine(so_far, jax.tree.map(lambda part: part[k], everything))

    return lax.fori_loop(1, lax.axis_size(axis), turn, initial)


def product_plain(left, right):
    return jnp.dot(left, right, preferred_element_type=jnp.float32)


def product_left_transposed(left, right):
    return lax.dot_general(
        left, right, (((0,), (0,)), ((), ())), preferred_element_type=jnp.float32
    )


def product_right_transposed(left, right):
    return lax.dot_general(
        left, right, (((1,), (1,)), ((), ())), preferred_element_type=jnp.float32
    )


def norm_fwd(hidden_rows, norm_gain, norm_shift):
    row_mean = jnp.mean(hidden_rows, axis=-1, keepdims=True)
    centered = hidden_rows - row_mean
    inverse_deviation = lax.rsqrt(jnp.mean(centered * centered, axis=-1, keepdims=True) + EPS_NORM)
    normalized_rows = centered * inverse_deviation
    return (normalized_rows * norm_gain + norm_shift, normalized_rows, inverse_deviation)


def norm_backward(gradient_value, normalized_rows, inverse_deviation, norm_gain):
    scaled_rows = gradient_value * norm_gain
    return inverse_deviation * (
        scaled_rows
        - jnp.mean(scaled_rows, axis=-1, keepdims=True)
        - normalized_rows * jnp.mean(scaled_rows * normalized_rows, axis=-1, keepdims=True)
    )


def unpack_tuple(collected_rows, down_width, down_feed, up_maps_every):
    attention_weight, feed_input, feed_output, small = collected_rows
    smallf = small.astype(jnp.float32)
    start = 5 * MODEL_WIDTH + HIDDEN_UNITS
    down_low = down_width.astype(jnp.bfloat16)
    up_low = up_maps_every.astype(jnp.bfloat16)
    return {
        "w_qkv": attention_weight[:, : 3 * MODEL_WIDTH],
        "w_o": attention_weight[:, 3 * MODEL_WIDTH :],
        "w_fc": feed_input,
        "w_fp": feed_output,
        "c_qkv": smallf[: 3 * MODEL_WIDTH],
        "c_o": smallf[3 * MODEL_WIDTH : 4 * MODEL_WIDTH],
        "c_fc": smallf[4 * MODEL_WIDTH : 4 * MODEL_WIDTH + HIDDEN_UNITS],
        "c_fp": smallf[4 * MODEL_WIDTH + HIDDEN_UNITS : start],
        "g_one": smallf[start : start + MODEL_WIDTH],
        "b_one": smallf[start + MODEL_WIDTH : start + 2 * MODEL_WIDTH],
        "g_two": smallf[start + 2 * MODEL_WIDTH : start + 3 * MODEL_WIDTH],
        "b_two": smallf[start + 3 * MODEL_WIDTH : start + 4 * MODEL_WIDTH],
        "d_qkv": down_low[:, :ADAPTER_RANK],
        "d_o": down_low[:, ADAPTER_RANK : 2 * ADAPTER_RANK],
        "d_fc": down_low[:, 2 * ADAPTER_RANK :],
        "d_fp": down_feed.astype(jnp.bfloat16),
        "u_qkv": up_low[:, : 3 * MODEL_WIDTH],
        "u_o": up_low[:, 3 * MODEL_WIDTH : 4 * MODEL_WIDTH],
        "u_fc": up_low[:, 4 * MODEL_WIDTH : 4 * MODEL_WIDTH + HIDDEN_UNITS],
        "u_fp": up_low[:, 4 * MODEL_WIDTH + HIDDEN_UNITS :],
    }


def scores(qkv_low, row_lengths):
    seqs = row_lengths.shape[0]
    seq = qkv_low.shape[0] // seqs
    parts = qkv_low.reshape(seqs, seq, 3, H, HD)
    query = parts[:, :, 0]
    key = parts[:, :, 1]
    value = parts[:, :, 2]
    raw = jnp.einsum("bqhe,bkhe->bhqk", query, key, preferred_element_type=jnp.float32) * HD ** (
        -0.5
    )
    qpos = lax.broadcasted_iota(jnp.int32, (seq, seq), 0)
    kpos = lax.broadcasted_iota(jnp.int32, (seq, seq), 1)
    allowed = (kpos <= qpos)[None, None] & (kpos[None, None] < row_lengths[:, None, None, None])
    return (jnp.where(allowed, raw, NEGATIVE), query, key, value)


def attend(qkv_low, row_lengths):
    masked, query, key, value = scores(qkv_low, row_lengths)
    top = jnp.max(masked, axis=-1, keepdims=True)
    lse = top + jnp.log(jnp.sum(jnp.exp(masked - top), axis=-1, keepdims=True))
    weights = jnp.exp(masked - lse).astype(jnp.bfloat16)
    output_rows = jnp.einsum("bhqk,bkhe->bqhe", weights, value, preferred_element_type=jnp.float32)
    return (output_rows.reshape(qkv_low.shape[0], MODEL_WIDTH).astype(jnp.bfloat16), lse)


def attend_back(d_out, qkv_low, lse, row_lengths):
    masked, query, key, value = scores(qkv_low, row_lengths)
    prob = jnp.exp(masked - lse)
    d_heads = d_out.reshape(query.shape)
    d_prob = jnp.einsum("bqhe,bkhe->bhqk", d_heads, value, preferred_element_type=jnp.float32)
    d_value = jnp.einsum(
        "bhqk,bqhe->bkhe", prob.astype(jnp.bfloat16), d_heads, preferred_element_type=jnp.float32
    )
    d_raw = (prob * (d_prob - jnp.sum(prob * d_prob, axis=-1, keepdims=True))).astype(jnp.bfloat16)
    d_query = jnp.einsum(
        "bhqk,bkhe->bqhe", d_raw, key, preferred_element_type=jnp.float32
    ) * HD ** (-0.5)
    d_key = jnp.einsum(
        "bhqk,bqhe->bkhe", d_raw, query, preferred_element_type=jnp.float32
    ) * HD ** (-0.5)
    return jnp.stack([d_query, d_key, d_value], 2).reshape(qkv_low.shape).astype(jnp.bfloat16)


def layer_forward(hidden_rows, row_lengths, weight_matrix):
    attention_values, a_hat, a_rstd = norm_fwd(
        hidden_rows, weight_matrix["g_one"], weight_matrix["b_one"]
    )
    attention_lowrank = attention_values.astype(jnp.bfloat16)
    up_query_key = product_plain(attention_lowrank, weight_matrix["d_qkv"]).astype(jnp.bfloat16)
    qkv_low = (
        product_plain(attention_lowrank, weight_matrix["w_qkv"])
        + weight_matrix["c_qkv"]
        + ADAPTER_SCALE * product_plain(up_query_key, weight_matrix["u_qkv"])
    ).astype(jnp.bfloat16)
    output_lowrank, lse = attend(qkv_low, row_lengths)
    up_output = product_plain(output_lowrank, weight_matrix["d_o"]).astype(jnp.bfloat16)
    middle_rows = hidden_rows + (
        product_plain(output_lowrank, weight_matrix["w_o"])
        + weight_matrix["c_o"]
        + ADAPTER_SCALE * product_plain(up_output, weight_matrix["u_o"])
    )
    feed_values, m_hat, m_rstd = norm_fwd(
        middle_rows, weight_matrix["g_two"], weight_matrix["b_two"]
    )
    feed_lowrank = feed_values.astype(jnp.bfloat16)
    up_feed_input = product_plain(feed_lowrank, weight_matrix["d_fc"]).astype(jnp.bfloat16)
    prenorm_rows = (
        product_plain(feed_lowrank, weight_matrix["w_fc"])
        + weight_matrix["c_fc"]
        + ADAPTER_SCALE * product_plain(up_feed_input, weight_matrix["u_fc"])
    )
    gradient_lowrank = jax.nn.gelu(prenorm_rows, approximate=True).astype(jnp.bfloat16)
    up_feed_output = product_plain(gradient_lowrank, weight_matrix["d_fp"]).astype(jnp.bfloat16)
    output_rows = middle_rows + (
        product_plain(gradient_lowrank, weight_matrix["w_fp"])
        + weight_matrix["c_fp"]
        + ADAPTER_SCALE * product_plain(up_feed_output, weight_matrix["u_fp"])
    )
    saved = (
        a_hat,
        a_rstd,
        attention_lowrank,
        up_query_key,
        qkv_low,
        lse,
        output_lowrank,
        up_output,
        m_hat,
        m_rstd,
        feed_lowrank,
        up_feed_input,
        prenorm_rows,
        gradient_lowrank,
        up_feed_output,
    )
    return (output_rows, saved)


def layer_backward(gradient_value, row_lengths, weight_matrix, saved):
    (
        a_hat,
        a_rstd,
        attention_lowrank,
        up_query_key,
        qkv_low,
        lse,
        output_lowrank,
        up_output,
        m_hat,
        m_rstd,
        feed_lowrank,
        up_feed_input,
        prenorm_rows,
        gradient_lowrank,
        up_feed_output,
    ) = saved
    feed_gradient = gradient_value.astype(jnp.bfloat16)
    up_map_feed_output = ADAPTER_SCALE * product_left_transposed(up_feed_output, feed_gradient)
    up_gradient_feed_output = (
        ADAPTER_SCALE * product_right_transposed(feed_gradient, weight_matrix["u_fp"])
    ).astype(jnp.bfloat16)
    down_fp = product_left_transposed(gradient_lowrank, up_gradient_feed_output)
    d_act = product_right_transposed(
        feed_gradient, weight_matrix["w_fp"]
    ) + product_right_transposed(up_gradient_feed_output, weight_matrix["d_fp"])
    prenorm_gradient = jax.vjp(partial(jax.nn.gelu, approximate=True), prenorm_rows)[1](d_act)[
        0
    ].astype(jnp.bfloat16)
    up_map_feed_input = ADAPTER_SCALE * product_left_transposed(up_feed_input, prenorm_gradient)
    up_gradient_feed_input = (
        ADAPTER_SCALE * product_right_transposed(prenorm_gradient, weight_matrix["u_fc"])
    ).astype(jnp.bfloat16)
    down_fc = product_left_transposed(feed_lowrank, up_gradient_feed_input)
    d_mid = product_right_transposed(
        prenorm_gradient, weight_matrix["w_fc"]
    ) + product_right_transposed(up_gradient_feed_input, weight_matrix["d_fc"])
    grad_mid = gradient_value + norm_backward(d_mid, m_hat, m_rstd, weight_matrix["g_two"])
    attention_gradient = grad_mid.astype(jnp.bfloat16)
    up_map_output = ADAPTER_SCALE * product_left_transposed(up_output, attention_gradient)
    up_gradient_output = (
        ADAPTER_SCALE * product_right_transposed(attention_gradient, weight_matrix["u_o"])
    ).astype(jnp.bfloat16)
    down_o = product_left_transposed(output_lowrank, up_gradient_output)
    d_heads = (
        product_right_transposed(attention_gradient, weight_matrix["w_o"])
        + product_right_transposed(up_gradient_output, weight_matrix["d_o"])
    ).astype(jnp.bfloat16)
    query_key_gradient = attend_back(d_heads, qkv_low, lse, row_lengths)
    up_map_query_key = ADAPTER_SCALE * product_left_transposed(up_query_key, query_key_gradient)
    up_gradient_query_key = (
        ADAPTER_SCALE * product_right_transposed(query_key_gradient, weight_matrix["u_qkv"])
    ).astype(jnp.bfloat16)
    down_qkv = product_left_transposed(attention_lowrank, up_gradient_query_key)
    d_norm = product_right_transposed(
        query_key_gradient, weight_matrix["w_qkv"]
    ) + product_right_transposed(up_gradient_query_key, weight_matrix["d_qkv"])
    grad_in = grad_mid + norm_backward(d_norm, a_hat, a_rstd, weight_matrix["g_one"])
    down_all = jnp.concatenate([down_qkv, down_o, down_fc], 1)
    up_maps_every = jnp.concatenate(
        [up_map_query_key, up_map_output, up_map_feed_input, up_map_feed_output], 1
    )
    return (grad_in, (down_all, down_fp, up_maps_every))


def combine_stats(first, second):
    return (jnp.logaddexp(first[0], second[0]), first[1] + second[1])


def moment_update(weight, first, second, gradient_value, scale_factor, step_number):
    clipped = gradient_value * scale_factor
    first_new = BETA_ONE * first + (1.0 - BETA_ONE) * clipped
    second_new = BETA_TWO * second + (1.0 - BETA_TWO) * clipped * clipped
    first_hat = first_new / (1.0 - BETA_ONE**step_number)
    second_hat = second_new / (1.0 - BETA_TWO**step_number)
    weight_new = weight - RATE * (first_hat / (jnp.sqrt(second_hat) + EPS_ADAM) + DECAY * weight)
    return (weight_new, first_new, second_new)


def body(
    input_token_ids,
    lengths,
    scored_slots,
    scored_targets,
    wte,
    wpe,
    frozen_attention,
    frozen_feed_input,
    frozen_feed_output,
    frozen_bias_gain,
    final_norm_params,
    adapter_down,
    adapter_down_feed,
    adapter_up,
    first_moment_down,
    first_moment_feed,
    first_moment_up,
    second_moment_down,
    second_moment_feed,
    second_moment_up,
    optimizer_step,
):
    vocab_rows = wte.shape[0]
    vocab_start = lax.axis_index("fsdp") * vocab_rows
    micro, seqs, seq = input_token_ids.shape
    rows_dev = seqs * seq
    picks = scored_slots.shape[2]
    layers = frozen_attention.shape[0]
    gain_final = final_norm_params[0].astype(jnp.float32)
    shift_final = final_norm_params[1].astype(jnp.float32)
    places = jnp.tile(wpe.astype(jnp.float32), (seqs, 1))
    zero_value = jnp.zeros((), jnp.float32)
    running_totals = (
        jnp.zeros_like(adapter_down),
        jnp.zeros_like(adapter_down_feed),
        jnp.zeros_like(adapter_up),
        zero_value,
        zero_value,
    )
    position_losses = []
    for micro_step in range(micro):
        row_lengths = lengths[micro_step]
        valid = (scored_slots[micro_step] < row_lengths[:, None]).astype(jnp.int32)
        ids_all, tgt_all, valid_all = (
            lax.all_gather(input_token_ids[micro_step], "fsdp", axis=0, tiled=True),
            lax.all_gather(scored_targets[micro_step], "fsdp", axis=0, tiled=True),
            lax.all_gather(valid, "fsdp", axis=0, tiled=True),
        )
        ids_flat = ids_all.reshape(-1)
        local = ids_flat - vocab_start
        inside = (local >= 0) & (local < vocab_rows)
        picked = jnp.take(wte, jnp.clip(local, 0, vocab_rows - 1), axis=0).astype(jnp.float32)
        hidden_rows = (
            lax.psum_scatter(
                jnp.where(inside[:, None], picked, 0.0).astype(jnp.bfloat16),
                "fsdp",
                scatter_dimension=0,
                tiled=True,
            ).astype(jnp.float32)
            + places
        )
        input_rows = []
        gathered_all = []
        for layer_index in range(layers):
            collected_rows = (
                lax.all_gather(frozen_attention[layer_index], "fsdp", axis=0, tiled=True),
                lax.all_gather(frozen_feed_input[layer_index], "fsdp", axis=0, tiled=True),
                lax.all_gather(frozen_feed_output[layer_index], "fsdp", axis=0, tiled=True),
                lax.all_gather(frozen_bias_gain[layer_index], "fsdp", axis=0, tiled=True),
            )
            gathered_all.append(collected_rows)
            input_rows.append(hidden_rows)
            hidden_rows, unused = layer_forward(
                hidden_rows,
                row_lengths,
                unpack_tuple(
                    collected_rows,
                    adapter_down[layer_index],
                    adapter_down_feed[layer_index],
                    adapter_up[layer_index],
                ),
            )
        h_val, h_hat, h_rstd = norm_fwd(hidden_rows, gain_final, shift_final)
        h_low = h_val.astype(jnp.bfloat16)
        row_index = (
            scored_slots[micro_step] + jnp.arange(seqs, dtype=jnp.int32)[:, None] * seq
        ).reshape(-1)
        chosen = h_low[row_index]
        logits = product_right_transposed(lax.all_gather(chosen, "fsdp", axis=0, tiled=True), wte)
        tgt_local = tgt_all.reshape(-1) - vocab_start
        columns = lax.broadcasted_iota(jnp.int32, logits.shape, 1)
        hit = columns == tgt_local[:, None]
        top = jnp.max(logits, axis=-1)
        part_lse = top + jnp.log(jnp.sum(jnp.exp(logits - top[:, None]), axis=-1))
        part_tgt = jnp.sum(jnp.where(hit, logits, 0.0), axis=-1)
        whole_lse, whole_tgt = joined((part_lse, part_tgt), "fsdp", combine_stats)
        mask_all = valid_all.reshape(-1).astype(jnp.float32)
        d_logits = (
            (jnp.exp(logits - whole_lse[:, None]) - hit.astype(jnp.float32)) * mask_all[:, None]
        ).astype(jnp.bfloat16)
        d_chosen = lax.psum_scatter(
            product_plain(d_logits, wte), "fsdp", scatter_dimension=0, tiled=True
        )
        own_terms = lax.dynamic_slice_in_dim(
            (whole_lse - whole_tgt) * mask_all, lax.axis_index("fsdp") * seqs * picks, seqs * picks
        )
        position_losses.append(own_terms.reshape(seqs, picks))
        d_hidden = jnp.zeros((rows_dev, MODEL_WIDTH), jnp.float32).at[row_index].add(d_chosen)
        gradient_value = norm_backward(d_hidden, h_hat, h_rstd, gain_final)
        down_list = [None] * layers
        ff_list = [None] * layers
        up_list = [None] * layers
        for layer_index in reversed(range(layers)):
            collected_rows = (
                lax.all_gather(frozen_attention[layer_index], "fsdp", axis=0, tiled=True),
                lax.all_gather(frozen_feed_input[layer_index], "fsdp", axis=0, tiled=True),
                lax.all_gather(frozen_feed_output[layer_index], "fsdp", axis=0, tiled=True),
                lax.all_gather(frozen_bias_gain[layer_index], "fsdp", axis=0, tiled=True),
            )
            packed_tuple = unpack_tuple(
                collected_rows,
                adapter_down[layer_index],
                adapter_down_feed[layer_index],
                adapter_up[layer_index],
            )
            unused, saved = layer_forward(input_rows[layer_index], row_lengths, packed_tuple)
            gradient_value, parts = layer_backward(gradient_value, row_lengths, packed_tuple, saved)
            down_list[layer_index], ff_list[layer_index], up_list[layer_index] = parts
        batch_sums = (
            jnp.stack(down_list),
            jnp.stack(ff_list),
            jnp.stack(up_list),
            jnp.sum(own_terms),
            jnp.sum(valid.astype(jnp.float32)),
        )
        batch_sums = lax.psum(
            (batch_sums[0], batch_sums[1], batch_sums[2], batch_sums[3], batch_sums[4]),
            ("dp", "fsdp"),
        )
        running_totals = jax.tree.map(jnp.add, running_totals, batch_sums)
    grad_a, grad_ff, grad_b, loss_total, count = running_totals
    gradient_tree = [grad_a / count, grad_ff / count, grad_b / count]
    norm = jnp.sqrt(sum((jnp.sum(g * g) for g in gradient_tree)))
    scale_factor = jnp.minimum(1.0, CLIP / (norm + 1e-06))
    step_number = optimizer_step[0].astype(jnp.float32)
    updated_down, updated_first_down, updated_second_down = moment_update(
        adapter_down,
        first_moment_down,
        second_moment_down,
        gradient_tree[0],
        scale_factor,
        step_number,
    )
    updated_feed, updated_first_feed, updated_second_feed = moment_update(
        adapter_down_feed,
        first_moment_feed,
        second_moment_feed,
        gradient_tree[1],
        scale_factor,
        step_number,
    )
    updated_up, updated_first_up, updated_second_up = moment_update(
        adapter_up, first_moment_up, second_moment_up, gradient_tree[2], scale_factor, step_number
    )
    return (
        loss_total / count,
        norm,
        updated_down,
        updated_feed,
        updated_up,
        updated_first_down,
        updated_first_feed,
        updated_first_up,
        updated_second_down,
        updated_second_feed,
        updated_second_up,
        jnp.stack(position_losses),
    )


def solution(mesh):
    in_specs = (
        P(None, ("dp", "fsdp"), None),
        P(None, ("dp", "fsdp")),
        P(None, ("dp", "fsdp"), None),
        P(None, ("dp", "fsdp"), None),
        P("fsdp", None),
        P(),
        P(None, "fsdp", None),
        P(None, "fsdp", None),
        P(None, "fsdp", None),
        P(None, "fsdp"),
        P(),
        P(),
        P(),
        P(),
        P(),
        P(),
        P(),
        P(),
        P(),
        P(),
        P(),
    )
    out_specs = (
        P(),
        P(),
        P(),
        P(),
        P(),
        P(),
        P(),
        P(),
        P(),
        P(),
        P(),
        P(None, ("dp", "fsdp"), None),
    )
    return jax.shard_map(body, mesh=mesh, in_specs=in_specs, out_specs=out_specs, check_vma=False)
```

profile of v0, /device:TPU:0, one launch (start us, length us, event | category | flops | bytes accessed | tf_op | source)
XLA Modules:
  0.0 994.3 jit_solution(16568715871185683584)
XLA Ops:
  7.9 10.3 %all-gather.14 = s32[8,1,256]{2,1,0:T(1,128)S(1)} all-gather(s32[1,1,256]{2,1,0:T(1,128)S(1)} %get-tuple-element.437), channel_id=16, replica_groups=mesh['dp'=4,'fsdp'=8] {'fsdp'}, dimensions={0}, use_global_device_ids=true | all-gather | bytes 9216 | tf_op jit(solution)/shard_map/all_gather | solution.py:322
  18.3 8.9 all-gather
  27.3 17.3 %gather_fusion.3 = bf16[2048,1024]{1,0:T(8,128)(2,1)} fusion(bf16[6288,1024]{1,0:T(8,128)(2,1)} %param.31, s32[2048]{0:T(1024)S(1)} %fusion.261), kind=kCustom, calls=%fused_computation.1.clone | custom fusion | bytes 8396800 | tf_op jit(solution)/shard_map/jit(_take)/gather | solution.py:329
  48.8 17.3 %gather_fusion.2 = bf16[2048,1024]{1,0:T(8,128)(2,1)} fusion(bf16[6288,1024]{1,0:T(8,128)(2,1)} %param.31, s32[2048]{0:T(1024)S(1)} %fusion.260), kind=kCustom, calls=%fused_computation.clone | custom fusion | bytes 8396800 | tf_op jit(solution)/shard_map/jit(_take)/gather | solution.py:329
  66.1 4.2 select_convert_fusion.1
  82.3 7.9 all-gather.5
  92.1 9.4 all-gather.1
  106.8 7.5 all-gather.19
  115.0 9.0 all-gather.17
  124.6 7.5 all-gather.13
  134.0 9.2 all-gather.11
  144.7 11.0 %reduce-scatter.5.cloned.1.call-done = bf16[256,1024]{1,0:T(8,128)(2,1)} async-done(((bf16[2048,1024]{1,0:T(8,128)(2,1)}), bf16[256,1024]{1,0:T(8,128)(2,1)}) %reduce-scatter.5.cloned.1.call-update) | async-done | bytes 524304 | tf_op jit(solution)/shard_map/reduce_scatter | solution.py:331
  162.0 50.0 %all-gather.31.cloned.1.call-done = bf16[1,1024,4096]{2,1,0:T(8,128)(2,1)} async-done(((bf16[1,128,4096]{2,1,0:T(8,128)(2,1)}), bf16[1,1024,4096]{2,1,0:T(8,128)(2,1)}) %all-gather.31.cloned.1.call-update) | async-done | bytes 8388624 | tf_op jit(solution)/shard_map/all_gather | solution.py:343
  212.0 4.7 fusion.101
  224.4 4.2 fusion.104
  246.7 21.5 %all-gather.33.cloned.1.call-done = bf16[1,1024,4096]{2,1,0:T(8,128)(2,1)} async-done(((bf16[1,128,4096]{2,1,0:T(8,128)(2,1)}), bf16[1,1024,4096]{2,1,0:T(8,128)(2,1)}) %all-gather.33.cloned.1.call-update) | async-done | bytes 8388624 | tf_op jit(solution)/shard_map/all_gather | solution.py:344
  268.2 5.7 fusion.43
  280.5 43.8 %all-gather.35.cloned.1.call-done = bf16[1,4096,1024]{2,1,0:T(8,128)(2,1)} async-done(((bf16[1,512,1024]{2,1,0:T(8,128)(2,1)}), bf16[1,4096,1024]{2,1,0:T(8,128)(2,1)}) %all-gather.35.cloned.1.call-update) | async-done | bytes 8388624 | tf_op jit(solution)/shard_map/all_gather | solution.py:345
  324.3 6.4 fusion.161
  332.0 6.8 fusion.40
  347.5 33.0 %all-gather.37.cloned.1.call-done = bf16[1,1024,4096]{2,1,0:T(8,128)(2,1)} async-done(((bf16[1,128,4096]{2,1,0:T(8,128)(2,1)}), bf16[1,1024,4096]{2,1,0:T(8,128)(2,1)}) %all-gather.37.cloned.1.call-update) | async-done | bytes 8388624 | tf_op jit(solution)/shard_map/all_gather | solution.py:343
  380.5 4.6 fusion.95
  389.8 5.1 fusion.92
  415.7 21.1 %all-gather.39.cloned.1.call-done = bf16[1,1024,4096]{2,1,0:T(8,128)(2,1)} async-done(((bf16[1,128,4096]{2,1,0:T(8,128)(2,1)}), bf16[1,1024,4096]{2,1,0:T(8,128)(2,1)}) %all-gather.39.cloned.1.call-update) | async-done | bytes 8388624 | tf_op jit(solution)/shard_map/all_gather | solution.py:344
  436.8 5.9 fusion.49
  448.8 44.3 %all-gather.41.cloned.1.call-done = bf16[1,4096,1024]{2,1,0:T(8,128)(2,1)} async-done(((bf16[1,512,1024]{2,1,0:T(8,128)(2,1)}), bf16[1,4096,1024]{2,1,0:T(8,128)(2,1)}) %all-gather.41.cloned.1.call-update) | async-done | bytes 8388624 | tf_op jit(solution)/shard_map/all_gather | solution.py:345
  493.1 6.3 fusion.167
  500.5 5.9 fusion.46
  517.7 9.8 all-gather.15
  527.5 7.1 fusion.368
  539.0 8.0 all-gather.22
  547.6 8.8 all-gather.23
  559.0 8.9 all-gather.9
  567.9 6.8 fusion.367
  579.1 8.9 all-gather.20
  587.9 7.9 all-gather.21
  595.9 5.8 while.35
  601.7 11.2 %fusion.109 = f32[256,1024]{1,0:T(8,128)} fusion(bf16[6288,1024]{1,0:T(8,128)(2,1)} %param.31, f32[256,6288]{0,1:T(8,128)} %copy-done.40, f32[256]{0:T(256)S(1)} %copy-done.188, f32[256]{0:T(256)S(1)} %get-tuple-element.281, s32[256]{0:T(256)S(1)} %copy-done.193), kind=kOutput, calls=%fused_computation.171 | convolution fusion | flops 3306381312 | bytes 20368384 | tf_op jit(solution)/shard_map/dot_general | solution.py:37
  613.6 11.4 %fusion.108 = f32[256,1024]{1,0:T(8,128)} fusion(bf16[6288,1024]{1,0:T(8,128)(2,1)} %param.31, f32[256,6288]{0,1:T(8,128)} %copy-done.39, f32[256]{0:T(256)S(1)} %copy-done.189, f32[256]{0:T(256)S(1)} %get-tuple-element.279, s32[256]{0:T(256)S(1)} %copy-done.191), kind=kOutput, calls=%fused_computation.170 | convolution fusion | flops 3306381312 | bytes 20368384 | tf_op jit(solution)/shard_map/dot_general | solution.py:37
  628.1 21.1 %reduce-scatter.11.cloned.1.call-done = f32[32,1024]{1,0:T(8,128)} async-done(((f32[256,1024]{1,0:T(8,128)}), f32[32,1024]{1,0:T(8,128)}) %reduce-scatter.11.cloned.1.call-update) | async-done | bytes 131088 | tf_op jit(solution)/shard_map/reduce_scatter | solution.py:378
  651.4 36.9 %reduce-scatter.9.cloned.1.call-done = f32[32,1024]{1,0:T(8,128)} async-done(((f32[256,1024]{1,0:T(8,128)}), f32[32,1024]{1,0:T(8,128)}) %reduce-scatter.9.cloned.1.call-update) | async-done | bytes 131088 | tf_op jit(solution)/shard_map/reduce_scatter | solution.py:378
  697.9 5.9 fusion.2
  709.9 7.9 fusion
  717.7 5.9 fusion.79
  781.8 5.9 fusion.18
  787.7 5.3 fusion.58
  841.6 39.4 %all-reduce = (f32[]{:T(128)}, f32[]{:T(128)}) all-reduce(f32[]{:T(128)S(6)} %add.972, f32[]{:T(128)S(6)} %add.973), channel_id=1, replica_groups=mesh['dp'=4,'fsdp'=8] {'dp','fsdp'}, use_global_device_ids=true, to_apply=%region_21.23 | all-reduce | flops 2 | bytes 16 | tf_op jit(solution)/shard_map/psum | solution.py:413
  882.9 84.2 %all-reduce.4.cloned.1.call-done = (f32[2,1024,12]{1,2,0:T(8,128)}, f32[2,4096,4]{1,2,0:T(4,128)}, f32[2,4,9216]{2,1,0:T(4,128)}) async-done(((f32[2,1024,12]{1,2,0:T(8,128)}, f32[2,4096,4]{1,2,0:T(4,128)}, f32[2,4,9216]{2,1,0:T(4,128)}), (f32[2,1024,12]{1,2,0:T(8,128)}, f32[2,4096,4]{1,2,0:T(4,128)}, f32[2,4,9216]{2,1,0:T(4,128)})) %all-reduce.4.cloned.1.call-update) | async-done | bytes 524304 | tf_op jit(solution)/shard_map/psum | solution.py:413
  (824 shorter events, 277.4 us)
Async XLA Ops:
  7.2 137.5 %reduce-scatter.7.cloned.1.call-start = ((), (), s32[]{:S(2)}) async-start(), calls=%async_computation.5 | async-start | bytes 4718592 | tf_op jit(solution)/shard_map/reduce_scatter | solution.py:331
  48.7 107.0 %reduce-scatter.5.cloned.1.call-start = ((), (), s32[]{:S(2)}) async-start(), calls=%async_computation.4 | async-start | bytes 4718592 | tf_op jit(solution)/shard_map/reduce_scatter | solution.py:331
  70.3 141.7 %all-gather.31.cloned.1.call-start = ((), (), s32[]{:S(2)}) async-start(), calls=%async_computation.8 | async-start | bytes 9437184 | tf_op jit(solution)/shard_map/all_gather | solution.py:343
  73.6 194.6 %all-gather.33.cloned.1.call-start = ((), (), s32[]{:S(2)}) async-start(), calls=%async_computation.9 | async-start | bytes 9437184 | tf_op jit(solution)/shard_map/all_gather | solution.py:344
  76.8 67.0 %copy-start.170 = (bf16[2,1024]{1,0:T(2,128)(2,1)S(1)}, bf16[2,1024]{1,0:T(2,128)(2,1)}, u32[]{:S(2)}) copy-start(bf16[2,1024]{1,0:T(2,128)(2,1)} %param.37) | copy-start | bytes 12292
  76.8 67.6 %copy-start.75 = (f32[2,4096,4]{1,2,0:T(4,128)S(1)}, f32[2,4096,4]{1,2,0:T(4,128)}, u32[]{:S(2)}) copy-start(f32[2,4096,4]{1,2,0:T(4,128)} %param.39) | copy-start | bytes 393220
  76.8 67.6 %copy-start.77 = (f32[2,1024,12]{1,0,2:T(2,128)S(1)}, f32[2,1024,12]{1,0,2:T(2,128)}, u32[]{:S(2)}) copy-start(f32[2,1024,12]{1,0,2:T(2,128)} %param.38) | copy-start | bytes 294916
  76.8 67.7 %copy-start.73 = (f32[2,4,9216]{2,1,0:T(4,128)S(1)}, f32[2,4,9216]{2,1,0:T(4,128)}, u32[]{:S(2)}) copy-start(f32[2,4,9216]{2,1,0:T(4,128)} %param.40) | copy-start | bytes 884740
  76.8 78.8 %copy-start.20 = (bf16[256,1024]{1,0:T(8,128)(2,1)S(1)}, bf16[256,1024]{1,0:T(8,128)(2,1)}, u32[]{:S(2)}) copy-start(bf16[256,1024]{1,0:T(8,128)(2,1)} %param.32) | copy-start | bytes 1572868
  76.9 247.5 %all-gather.35.cloned.1.call-start = ((), (), s32[]{:S(2)}) async-start(), calls=%async_computation.10 | async-start | bytes 9437184 | tf_op jit(solution)/shard_map/all_gather | solution.py:345
  80.2 300.4 %all-gather.37.cloned.1.call-start = ((), (), s32[]{:S(2)}) async-start(), calls=%async_computation.11 | async-start | bytes 9437184 | tf_op jit(solution)/shard_map/all_gather | solution.py:343
  80.7 356.1 %all-gather.39.cloned.1.call-start = ((), (), s32[]{:S(2)}) async-start(), calls=%async_computation.12 | async-start | bytes 9437184 | tf_op jit(solution)/shard_map/all_gather | solution.py:344
  81.5 411.6 %all-gather.41.cloned.1.call-start = ((), (), s32[]{:S(2)}) async-start(), calls=%async_computation.13 | async-start | bytes 9437184 | tf_op jit(solution)/shard_map/all_gather | solution.py:345
  82.2 567.0 %reduce-scatter.11.cloned.1.call-start = ((), (), s32[]{:S(2)}) async-start(), calls=%async_computation.7 | async-start | bytes 1179648 | tf_op jit(solution)/shard_map/reduce_scatter | solution.py:378
  103.4 41.1 %copy-start.197 = (s32[32]{0:T(128)}, s32[32]{0:T(128)S(1)}, u32[]{:S(2)}) copy-start(s32[32]{0:T(128)S(1)} %get-tuple-element.446) | copy-start | bytes 388
  103.4 41.1 %copy-start.198 = (s32[32]{0:T(128)}, s32[32]{0:T(128)S(1)}, u32[]{:S(2)}) copy-start(s32[32]{0:T(128)S(1)} %get-tuple-element.445) | copy-start | bytes 388
  144.6 186.9 %copy-start.71 = (bf16[1024,12]{0,1:T(8,128)(2,1)}, bf16[1024,12]{0,1:T(8,128)(2,1)S(1)}, u32[]{:S(2)}) copy-start(bf16[1024,12]{0,1:T(8,128)(2,1)S(1)} %get-tuple-element.410) | copy-start | bytes 73732
  144.7 201.3 %copy-start.69 = (bf16[4,9216]{1,0:T(4,128)(2,1)}, bf16[4,9216]{1,0:T(4,128)(2,1)S(1)}, u32[]{:S(2)}) copy-start(bf16[4,9216]{1,0:T(4,128)(2,1)S(1)} %get-tuple-element.408) | copy-start | bytes 221188
  160.9 55.9 %copy-start.49 = (bf16[256,1024]{1,0:T(8,128)(2,1)}, bf16[256,1024]{1,0:T(8,128)(2,1)S(1)}, u32[]{:S(2)}) copy-start(bf16[256,1024]{1,0:T(8,128)(2,1)S(1)} %get-tuple-element.405) | copy-start | bytes 1572868
  160.9 55.9 %copy-start.51 = (bf16[256,1024]{1,0:T(8,128)(2,1)}, bf16[256,1024]{1,0:T(8,128)(2,1)S(1)}, u32[]{:S(2)}) copy-start(bf16[256,1024]{1,0:T(8,128)(2,1)S(1)} %get-tuple-element.406) | copy-start | bytes 1572868
  161.1 59.6 %copy-start.127 = (bf16[256,4]{0,1:T(4,128)(2,1)}, bf16[256,4]{0,1:T(4,128)(2,1)S(1)}, u32[]{:S(2)}) copy-start(bf16[256,4]{0,1:T(4,128)(2,1)S(1)} %convolution_convert_fusion.13) | copy-start | bytes 6148
  244.1 101.8 %copy-start.10 = (f32[256,1024]{1,0:T(8,128)}, f32[256,1024]{1,0:T(8,128)S(1)}, u32[]{:S(2)}) copy-start(f32[256,1024]{1,0:T(8,128)S(1)} %get-tuple-element.458) | copy-start | bytes 3145732
  245.0 85.7 %copy-start.12 = (f32[256,1024]{1,0:T(8,128)}, f32[256,1024]{1,0:T(8,128)S(1)}, u32[]{:S(2)}) copy-start(f32[256,1024]{1,0:T(8,128)S(1)} %get-tuple-element.454) | copy-start | bytes 3145732
  273.9 50.4 %copy-start.186 = (f32[1,1024]{1,0:T(1,128)S(1)}, f32[1,1024]{1,0:T(1,128)}, u32[]{:S(2)}) copy-start(f32[1,1024]{1,0:T(1,128)} %get-tuple-element.417) | copy-start | bytes 12292
  346.0 34.5 %copy-start.175 = (f32[1,3072]{1,0:T(1,128)S(1)}, f32[1,3072]{1,0:T(1,128)}, u32[]{:S(2)}) copy-start(f32[1,3072]{1,0:T(1,128)} %slice.526) | copy-start | bytes 36868
  346.5 61.6 %copy-start.8 = (f32[256,1024]{1,0:T(8,128)}, f32[256,1024]{1,0:T(8,128)S(1)}, u32[]{:S(2)}) copy-start(f32[256,1024]{1,0:T(8,128)S(1)} %get-tuple-element.466) | copy-start | bytes 3145732
  346.5 38.6 %copy-start.115 = (f32[256]{0:T(256)}, f32[256]{0:T(256)S(1)}, u32[]{:S(2)}) copy-start(f32[256]{0:T(256)S(1)} %broadcast_multiply_fusion.23) | copy-start | bytes 3076
  346.8 38.3 %copy-start.158 = (f32[256]{0:T(256)}, f32[256]{0:T(256)S(1)}, u32[]{:S(2)}) copy-start(f32[256]{0:T(256)S(1)} %add_rsqrt_fusion.2) | copy-start | bytes 3076
  346.8 38.3 %copy-start.156 = (f32[256]{0:T(256)}, f32[256]{0:T(256)S(1)}, u32[]{:S(2)}) copy-start(f32[256]{0:T(256)S(1)} %add_rsqrt_fusion.7) | copy-start | bytes 3076
  347.3 37.8 %copy-start.59 = (bf16[256,1024]{1,0:T(8,128)(2,1)}, bf16[256,1024]{1,0:T(8,128)(2,1)S(1)}, u32[]{:S(2)}) copy-start(bf16[256,1024]{1,0:T(8,128)(2,1)S(1)} %get-tuple-element.427) | copy-start | bytes 1572868
  347.3 42.5 %copy-start.57 = (bf16[256,1024]{1,0:T(8,128)(2,1)}, bf16[256,1024]{1,0:T(8,128)(2,1)S(1)}, u32[]{:S(2)}) copy-start(bf16[256,1024]{1,0:T(8,128)(2,1)S(1)} %get-tuple-element.428) | copy-start | bytes 1572868
  347.5 37.6 %copy-start.141 = (bf16[256,4]{0,1:T(4,128)(2,1)}, bf16[256,4]{0,1:T(4,128)(2,1)S(1)}, u32[]{:S(2)}) copy-start(bf16[256,4]{0,1:T(4,128)(2,1)S(1)} %convolution_convert_fusion.10) | copy-start | bytes 6148
  415.7 90.7 %copy-start.182 = (bf16[256,4]{0,1:T(4,128)(2,1)}, bf16[256,4]{0,1:T(4,128)(2,1)S(1)}, u32[]{:S(2)}) copy-start(bf16[256,4]{0,1:T(4,128)(2,1)S(1)} %convolution_convert_fusion.14) | copy-start | bytes 6148
  442.8 50.4 %copy-start.185 = (f32[1,1024]{1,0:T(1,128)S(1)}, f32[1,1024]{1,0:T(1,128)}, u32[]{:S(2)}) copy-start(f32[1,1024]{1,0:T(1,128)} %get-tuple-element.411) | copy-start | bytes 12292
  448.8 50.7 %copy-start.147 = (bf16[256,4]{0,1:T(4,128)(2,1)}, bf16[256,4]{0,1:T(4,128)(2,1)S(1)}, u32[]{:S(2)}) copy-start(bf16[256,4]{0,1:T(4,128)(2,1)S(1)} %convolution_convert_fusion.20) | copy-start | bytes 6148
  613.0 75.3 %reduce-scatter.9.cloned.1.call-start = ((), (), s32[]{:S(2)}) async-start(), calls=%async_computation.6 | async-start | bytes 1179648 | tf_op jit(solution)/shard_map/reduce_scatter | solution.py:378
  613.5 77.1 %copy-start.124 = (f32[256]{0:T(256)S(1)}, f32[256]{0:T(256)}, u32[]{:S(2)}) copy-start(f32[256]{0:T(256)} %copy-done.123) | copy-start | bytes 3076
  613.5 77.1 %copy-start.126 = (f32[256]{0:T(256)S(1)}, f32[256]{0:T(256)}, u32[]{:S(2)}) copy-start(f32[256]{0:T(256)} %copy-done.125) | copy-start | bytes 3076
  613.5 77.1 %copy-start.172 = (f32[256]{0:T(256)S(1)}, f32[256]{0:T(256)}, u32[]{:S(2)}) copy-start(f32[256]{0:T(256)} %copy-done.171) | copy-start | bytes 3076
  613.5 77.1 %copy-start.174 = (f32[256]{0:T(256)S(1)}, f32[256]{0:T(256)}, u32[]{:S(2)}) copy-start(f32[256]{0:T(256)} %copy-done.173) | copy-start | bytes 3076
  624.9 342.1 %all-reduce.4.cloned.1.call-start = ((), (), s32[]{:S(2)}) async-start(), calls=%async_computation.14 | async-start | bytes 1114112 | tf_op jit(solution)/shard_map/psum | solution.py:413
  829.1 146.7 %copy-start.78 = (f32[2,1024,12]{1,0,2:T(2,128)S(1)}, f32[2,1024,12]{1,0,2:T(2,128)}, u32[]{:S(2)}) copy-start(f32[2,1024,12]{1,0,2:T(2,128)} %param.38) | copy-start | bytes 294916
  830.3 149.5 %copy-start.76 = (f32[2,4096,4]{1,2,0:T(4,128)S(1)}, f32[2,4096,4]{1,2,0:T(4,128)}, u32[]{:S(2)}) copy-start(f32[2,4096,4]{1,2,0:T(4,128)} %param.39) | copy-start | bytes 393220
  830.3 151.9 %copy-start.74 = (f32[2,4,9216]{2,1,0:T(4,128)S(1)}, f32[2,4,9216]{2,1,0:T(4,128)}, u32[]{:S(2)}) copy-start(f32[2,4,9216]{2,1,0:T(4,128)} %param.40) | copy-start | bytes 884740
  830.3 151.9 %copy-start.79 = (f32[2,4,9216]{2,1,0:T(4,128)S(1)}, f32[2,4,9216]{2,1,0:T(4,128)}, u32[]{:S(2)}) copy-start(f32[2,4,9216]{2,1,0:T(4,128)} %param.46) | copy-start | bytes 884740
  830.3 151.9 %copy-start.80 = (f32[2,4,9216]{2,1,0:T(4,128)S(1)}, f32[2,4,9216]{2,1,0:T(4,128)}, u32[]{:S(2)}) copy-start(f32[2,4,9216]{2,1,0:T(4,128)} %param.43) | copy-start | bytes 884740
  830.8 148.9 %copy-start.91 = (f32[2,4096,4]{1,2,0:T(4,128)S(1)}, f32[2,4096,4]{1,2,0:T(4,128)}, u32[]{:S(2)}) copy-start(f32[2,4096,4]{1,2,0:T(4,128)} %param.45) | copy-start | bytes 393220
  830.8 148.9 %copy-start.92 = (f32[2,4096,4]{1,2,0:T(4,128)S(1)}, f32[2,4096,4]{1,2,0:T(4,128)}, u32[]{:S(2)}) copy-start(f32[2,4096,4]{1,2,0:T(4,128)} %param.42) | copy-start | bytes 393220
  (189 other events, 1115.7 us)
Sparse Core Ops, SparseCore 0:
  48.8 51.7 reduce-scatter.6
  104.3 51.3 reduce-scatter.4
  157.6 54.3 all-gather.30
  213.8 54.3 all-gather.32
  269.9 54.3 all-gather.34
  326.1 54.3 all-gather.36
  382.4 54.3 all-gather.38
  438.7 54.3 all-gather.40
  613.1 36.0 reduce-scatter.10
  652.2 36.0 reduce-scatter.8
  839.0 127.9 all-reduce.3
where the time goes:
time: 1000 us; the launch traced here: 994 us
  waiting for transfers between devices  369 us (37%)
  matrix products  274 us (27%)
  blocking collectives  161 us (16%)
  local copies, waits for them, and re-layouts  89.3 us (9%)
  other arithmetic  72.8 us (7%)
  between operations  26.6 us (3%)
    dot_general x50, matrix products, product_plain(): return jnp.dot(left, right, preferred_element_type=jnp.float32)  121 us
    all_gather x2, waiting for transfers between devices, body(): lax.all_gather(frozen_feed_output[layer_index], 'fsdp', axis=0, tiled=True)  88.1 us
    dot_general x44, matrix products, product_right_transposed(): lax.dot_general(left, right, (((1,), (1,)), ((), ())), preferred_element_...  85.6 us
    psum x1, waiting for transfers between devices, body(): lax.psum((batch_sums[0], batch_sums[1], batch_sums[2], batch_sums[3], bat...  84.2 us
    all_gather x2, waiting for transfers between devices, body(): lax.all_gather(frozen_attention[layer_index], 'fsdp', axis=0, tiled=True)  83 us
    reduce_scatter x2, waiting for transfers between devices, body(): lax.psum_scatter(product_plain(d_logits, wte), 'fsdp', scatter_dimension=...  57.9 us
    all_gather x2, waiting for transfers between devices, body(): lax.all_gather(frozen_feed_input[layer_index], 'fsdp', axis=0, tiled=True)  42.6 us
    psum x1, blocking collectives, body(): lax.psum((batch_sums[0], batch_sums[1], batch_sums[2], batch_sums[3], bat...  39.4 us
  transfers between devices with their start and end apart: 11, of which 10 were waited for; matrix products, arithmetic and copies ran while one was open for 18% of the time, Pallas kernels for 0%

commit v1 on v0

v1 whole, which is shorter than its diff:
```python
from functools import partial

import jax
import jax.numpy as jnp
from jax import lax
from jax.experimental import pallas as pl
from jax.experimental.pallas import tpu as pltpu
from jax.sharding import PartitionSpec as P

MODEL_WIDTH = 1024
H = 16
HD = 64
HIDDEN_UNITS = 4096
ADAPTER_RANK = 4


ADAPTER_SCALE = 8.0
EPS_NORM = 1e-05
BETA_ONE = 0.9
BETA_TWO = 0.999
RATE = 0.02
DECAY = 0.01
EPS_ADAM = 1e-08
CLIP = 0.02
NEGATIVE = -1e30


def product_plain(left, right):
    return jnp.dot(left, right, preferred_element_type=jnp.float32)


def product_left_transposed(left, right):
    return lax.dot_general(
        left, right, (((0,), (0,)), ((), ())), preferred_element_type=jnp.float32
    )


def product_right_transposed(left, right):
    return lax.dot_general(
        left, right, (((1,), (1,)), ((), ())), preferred_element_type=jnp.float32
    )


def norm_fwd(hidden_rows, norm_gain, norm_shift):
    row_mean = jnp.mean(hidden_rows, axis=-1, keepdims=True)
    centered = hidden_rows - row_mean
    inverse_deviation = lax.rsqrt(jnp.mean(centered * centered, axis=-1, keepdims=True) + EPS_NORM)
    normalized_rows = centered * inverse_deviation
    return (normalized_rows * norm_gain + norm_shift, normalized_rows, inverse_deviation)


def norm_backward(gradient_value, normalized_rows, inverse_deviation, norm_gain):
    scaled_rows = gradient_value * norm_gain
    return inverse_deviation * (
        scaled_rows
        - jnp.mean(scaled_rows, axis=-1, keepdims=True)
        - normalized_rows * jnp.mean(scaled_rows * normalized_rows, axis=-1, keepdims=True)
    )


def moment_update(weight, first, second, gradient_value, scale_factor, step_number):
    clipped = gradient_value * scale_factor
    first_new = BETA_ONE * first + (1.0 - BETA_ONE) * clipped
    second_new = BETA_TWO * second + (1.0 - BETA_TWO) * clipped * clipped
    first_hat = first_new / (1.0 - BETA_ONE**step_number)
    second_hat = second_new / (1.0 - BETA_TWO**step_number)
    weight_new = weight - RATE * (first_hat / (jnp.sqrt(second_hat) + EPS_ADAM) + DECAY * weight)
    return (weight_new, first_new, second_new)


CAPACITY = 80


def attention_scores(query, key, query_slots, row_lengths):
    raw = jnp.einsum("bqhe,bkhe->bhqk", query, key, preferred_element_type=jnp.float32) * HD ** (
        -0.5
    )
    kpos = jnp.arange(key.shape[1], dtype=jnp.int32)[None, None, :]
    allowed = (kpos <= query_slots[:, :, None]) & (kpos < row_lengths[:, None, None])
    return jnp.where(allowed[:, None], raw, NEGATIVE)


def attend(query, key, value, query_slots, row_lengths):
    masked = attention_scores(query, key, query_slots, row_lengths)
    top = jnp.max(masked, axis=-1, keepdims=True)
    lse = top + jnp.log(jnp.sum(jnp.exp(masked - top), axis=-1, keepdims=True))
    weights = jnp.exp(masked - lse).astype(jnp.bfloat16)
    output = jnp.einsum("bhqk,bkhe->bqhe", weights, value, preferred_element_type=jnp.float32)
    return (output.reshape(-1, MODEL_WIDTH).astype(jnp.bfloat16), lse)


def attend_back(d_heads, query, key, value, lse, query_slots, row_lengths):
    masked = attention_scores(query, key, query_slots, row_lengths)
    prob = jnp.exp(masked - lse)
    d_heads = d_heads.reshape(query.shape)
    d_prob = jnp.einsum("bqhe,bkhe->bhqk", d_heads, value, preferred_element_type=jnp.float32)
    d_value = jnp.einsum(
        "bhqk,bqhe->bkhe", prob.astype(jnp.bfloat16), d_heads, preferred_element_type=jnp.float32
    )
    d_raw = (prob * (d_prob - jnp.sum(prob * d_prob, axis=-1, keepdims=True))).astype(jnp.bfloat16)
    d_query = jnp.einsum(
        "bhqk,bkhe->bqhe", d_raw, key, preferred_element_type=jnp.float32
    ) * HD ** (-0.5)
    d_key = jnp.einsum(
        "bhqk,bqhe->bkhe", d_raw, query, preferred_element_type=jnp.float32
    ) * HD ** (-0.5)

    def flat(part):
        return part.reshape(-1, MODEL_WIDTH).astype(jnp.bfloat16)

    return flat(d_query), flat(d_key), flat(d_value)


def projection(rows_low, weight, bias, down, up):
    inner = product_plain(rows_low, down).astype(jnp.bfloat16)
    return (
        product_plain(rows_low, weight) + bias + ADAPTER_SCALE * product_plain(inner, up),
        inner,
    )


def projection_back(gradient_low, rows_low, inner, weight, down, up, into_rows=True):
    grad_up = ADAPTER_SCALE * product_left_transposed(inner, gradient_low)
    d_inner = (ADAPTER_SCALE * product_right_transposed(gradient_low, up)).astype(jnp.bfloat16)
    grad_down = product_left_transposed(d_inner, rows_low)
    d_rows = None
    if into_rows:
        d_rows = product_right_transposed(gradient_low, weight) + product_right_transposed(
            d_inner, down
        )
    return grad_down, grad_up, d_rows


def feed_forward(middle_rows, weights):
    feed_values, m_hat, m_rstd = norm_fwd(middle_rows, weights["g_two"], weights["b_two"])
    feed_low = feed_values.astype(jnp.bfloat16)
    prenorm, um = projection(
        feed_low, weights["w_fc"], weights["c_fc"], weights["d_fc"], weights["u_fc"]
    )
    act_low = jax.nn.gelu(prenorm, approximate=True).astype(jnp.bfloat16)
    branch, ug = projection(
        act_low, weights["w_fp"], weights["c_fp"], weights["d_fp"], weights["u_fp"]
    )
    return middle_rows + branch, (m_hat, m_rstd, feed_low, um, prenorm, act_low, ug)


def feed_backward(gradient_value, weights, saved):
    m_hat, m_rstd, feed_low, um, prenorm, act_low, ug = saved
    grad_dfp, grad_ufp, d_act = projection_back(
        gradient_value.astype(jnp.bfloat16),
        act_low,
        ug,
        weights["w_fp"],
        weights["d_fp"],
        weights["u_fp"],
    )
    d_pre = jax.vjp(partial(jax.nn.gelu, approximate=True), prenorm)[1](d_act)[0].astype(
        jnp.bfloat16
    )
    grad_dfc, grad_ufc, d_feed = projection_back(
        d_pre, feed_low, um, weights["w_fc"], weights["d_fc"], weights["u_fc"]
    )
    grad_mid = gradient_value + norm_backward(d_feed, m_hat, m_rstd, weights["g_two"])
    return grad_mid, (grad_dfp, grad_ufp, grad_dfc, grad_ufc)


def unpack(small, down, down_feed, up):
    smallf = small.astype(jnp.float32)
    start = 5 * MODEL_WIDTH + HIDDEN_UNITS
    down_low = down.astype(jnp.bfloat16)
    up_low = up.astype(jnp.bfloat16)
    return {
        "c_qkv": smallf[: 3 * MODEL_WIDTH],
        "c_o": smallf[3 * MODEL_WIDTH : 4 * MODEL_WIDTH],
        "c_fc": smallf[4 * MODEL_WIDTH : 4 * MODEL_WIDTH + HIDDEN_UNITS],
        "c_fp": smallf[4 * MODEL_WIDTH + HIDDEN_UNITS : start],
        "g_one": smallf[start : start + MODEL_WIDTH],
        "b_one": smallf[start + MODEL_WIDTH : start + 2 * MODEL_WIDTH],
        "g_two": smallf[start + 2 * MODEL_WIDTH : start + 3 * MODEL_WIDTH],
        "b_two": smallf[start + 3 * MODEL_WIDTH : start + 4 * MODEL_WIDTH],
        "d_qkv": down_low[:, :ADAPTER_RANK],
        "d_o": down_low[:, ADAPTER_RANK : 2 * ADAPTER_RANK],
        "d_fc": down_low[:, 2 * ADAPTER_RANK :],
        "d_fp": down_feed.astype(jnp.bfloat16),
        "u_qkv": up_low[:, : 3 * MODEL_WIDTH],
        "u_o": up_low[:, 3 * MODEL_WIDTH : 4 * MODEL_WIDTH],
        "u_fc": up_low[:, 4 * MODEL_WIDTH : 4 * MODEL_WIDTH + HIDDEN_UNITS],
        "u_fp": up_low[:, 4 * MODEL_WIDTH + HIDDEN_UNITS :],
    }


def lookup(table, ids, needed):
    shards = lax.axis_size("fsdp")
    total = ids.shape[0]
    order = jnp.arange(total, dtype=jnp.int32)
    owner = ids // table.shape[0]
    local = ids - owner * table.shape[0]
    same = (ids[:, None] == ids[None, :]) & needed[None, :]
    first = jnp.min(jnp.where(same, order[None, :], total), axis=1)
    leads = needed & (first == order)
    rank = jnp.sum(
        (leads & (owner[:, None] == owner[None, :]) & (order[None, :] < first[:, None])).astype(
            jnp.int32
        ),
        axis=1,
    )
    rounds = (jnp.max(jnp.where(needed, rank, 0)) + CAPACITY) // CAPACITY

    spots = jnp.arange(shards * CAPACITY, dtype=jnp.int32)

    def serve(turn):
        place = jnp.where(
            needed & (rank // CAPACITY == turn), owner * CAPACITY + rank % CAPACITY, -1
        )
        asked = jnp.sum(
            jnp.where(leads[:, None] & (place[:, None] == spots[None, :]), local[:, None], 0), axis=0
        ).reshape(shards, CAPACITY)
        message = jnp.concatenate([asked, jnp.full((shards, 1), rounds, jnp.int32)], 1)
        got = lax.all_to_all(message, "fsdp", 0, 0, tiled=True)
        sent = table.at[got[:, :CAPACITY].reshape(-1)].get(mode="promise_in_bounds")
        back = lax.all_to_all(sent, "fsdp", 0, 0, tiled=True)
        pick = (place[:, None] == spots[None, :]).astype(jnp.bfloat16)
        return product_plain(pick, back), jnp.max(got[:, CAPACITY])

    found, most = serve(0)
    groups = lax.axis_size("dp")
    others = [
        lax.ppermute(most, "dp", [(i, (i + k) % groups) for i in range(groups)])
        for k in range(1, groups)
    ]
    for other in others:
        most = jnp.maximum(most, other)
    return lax.fori_loop(1, most, lambda turn, so_far: so_far + serve(turn)[0], found)


def swap(part, bit):
    return lax.ppermute(part, "fsdp", [(i, i ^ bit) for i in range(lax.axis_size("fsdp"))])


def tie(parts, before):
    parts, _ = lax.optimization_barrier((parts, before))
    return parts


def place_kernel(places, rows, *refs):
    pieces, out = refs[:-1], refs[-1]
    me = lax.axis_index("fsdp")
    for (offset, first), piece in zip(places, pieces):
        start = pl.multiple_of(jnp.bitwise_xor(me, offset) * rows + first, 16)
        out[pl.ds(start, piece.shape[0]), :] = piece[...]


def placed(pieces, rows):
    places = tuple((offset, first) for offset, first, _ in pieces)
    arrays = [array for _, _, array in pieces]
    columns = arrays[0].shape[1]
    height = rows * lax.axis_size("fsdp")
    tile = columns // 4
    return pl.pallas_call(
        partial(place_kernel, places, rows),
        out_shape=jax.ShapeDtypeStruct((height, columns), arrays[0].dtype),
        grid=(columns // tile,),
        in_specs=[pl.BlockSpec((a.shape[0], tile), lambda j: (0, j)) for a in arrays],
        out_specs=pl.BlockSpec((height, tile), lambda j: (0, j)),
        compiler_params=pltpu.CompilerParams(vmem_limit_bytes=32 * 2**20),
        cost_estimate=pl.CostEstimate(
            flops=0, bytes_accessed=4 * height * columns, transcendentals=0
        ),
    )(*arrays)


def gather_units(units):
    if lax.axis_size("fsdp") != 8:
        return [lax.all_gather(unit, "fsdp", axis=0, tiled=True) for unit in units]
    wholes = []
    near = ()
    waiting = None
    for unit in list(units) + [None]:
        done = near
        if unit is not None:
            own = tie(unit, near)
            near = (swap(own, 2), swap(own, 4))
        if waiting is not None:
            before, (one, two) = waiting
            rows = before.shape[0]
            half = rows // 2
            far = (swap(one[:half], 4), swap(two[half:], 2))
            wholes.append(
                placed(
                    [
                        (0, 0, before),
                        (1, 0, swap(before, 1)),
                        (2, 0, one),
                        (3, 0, swap(one, 1)),
                        (4, 0, two),
                        (5, 0, swap(two, 1)),
                        (6, 0, far[0]),
                        (6, half, far[1]),
                        (7, 0, swap(far[0], 1)),
                        (7, half, swap(far[1], 1)),
                    ],
                    rows,
                )
            )
        waiting = (own, near)
    return wholes


def everywhere(part):
    shards = lax.axis_size("fsdp")
    return lax.all_to_all(
        jnp.tile(part, (shards,) + (1,) * (part.ndim - 1)), "fsdp", 0, 0, tiled=True
    )


def owned_parts(parts):
    shards = lax.axis_size("fsdp")
    rows = parts.shape[0] // shards
    return lax.all_to_all(parts, "fsdp", 0, 0, tiled=True).reshape(
        (shards, rows) + parts.shape[1:]
    )


def split_feed_forward(middle_rows, weights):
    feed_values, m_hat, m_rstd = norm_fwd(middle_rows, weights["g_two"], weights["b_two"])
    feed_low = everywhere(feed_values.astype(jnp.bfloat16))
    prenorm, um = projection(
        feed_low, weights["w_fc"], weights["c_fc"], weights["d_fc"], weights["u_fc"]
    )
    act_low = jax.nn.gelu(prenorm, approximate=True).astype(jnp.bfloat16)
    branch, ug = projection(act_low, weights["w_fp"], 0.0, weights["d_fp"], weights["u_fp"])
    branch = jnp.sum(owned_parts(branch.astype(jnp.bfloat16)).astype(jnp.float32), axis=0)
    return (
        middle_rows + (branch + weights["c_fp"]),
        (m_hat, m_rstd, feed_low, um, prenorm, act_low, ug),
    )


def split_feed_backward(gradient_value, weights, saved):
    m_hat, m_rstd, feed_low, um, prenorm, act_low, ug = saved
    grad_dfp, grad_ufp, d_act = projection_back(
        everywhere(gradient_value.astype(jnp.bfloat16)),
        act_low,
        ug,
        weights["w_fp"],
        weights["d_fp"],
        weights["u_fp"],
    )
    d_pre = jax.vjp(partial(jax.nn.gelu, approximate=True), prenorm)[1](d_act)[0].astype(
        jnp.bfloat16
    )
    grad_dfc, grad_ufc, d_feed = projection_back(
        d_pre, feed_low, um, weights["w_fc"], weights["d_fc"], weights["u_fc"]
    )
    d_feed = jnp.sum(owned_parts(d_feed.astype(jnp.bfloat16)).astype(jnp.float32), axis=0)
    grad_mid = gradient_value + norm_backward(d_feed, m_hat, m_rstd, weights["g_two"])
    return grad_mid, (grad_dfp, grad_ufp, grad_dfc, grad_ufc)


def summed_everywhere(gradients, extras):
    shards = lax.axis_size("fsdp")
    groups = lax.axis_size("dp")
    rows, columns = gradients.shape
    width = columns // shards
    blocks = gradients.reshape(rows, shards, width).transpose(1, 0, 2)
    tail = jnp.zeros((rows, 128), jnp.float32).at[0, : extras.shape[0]].set(extras)
    blocks = jnp.concatenate([blocks, jnp.tile(tail[None], (shards, 1, 1))], 2)
    block = jnp.sum(owned_parts(blocks.reshape(shards * rows, -1)), axis=0)
    others = [
        lax.ppermute(block, "dp", [(i, (i + k) % groups) for i in range(groups)])
        for k in range(1, groups)
    ]
    stacked = jnp.stack([block] + others)
    order = (lax.axis_index("dp") - jnp.arange(groups)) % groups
    ranks = (order[None, :] == jnp.arange(groups)[:, None])[:, :, None, None]
    total = jnp.sum(jnp.sum(jnp.where(ranks, stacked[None], 0.0), axis=1), axis=0)
    whole = everywhere(total).reshape(shards, rows, width + 128)
    return (
        whole[:, :, :width].transpose(1, 0, 2).reshape(rows, columns),
        whole[0, 0, width : width + extras.shape[0]],
    )


def body(
    input_token_ids,
    lengths,
    scored_slots,
    scored_targets,
    wte,
    wpe,
    frozen_attention,
    frozen_feed_input,
    frozen_feed_output,
    frozen_bias_gain,
    final_norm_params,
    adapter_down,
    adapter_down_feed,
    adapter_up,
    first_moment_down,
    first_moment_feed,
    first_moment_up,
    second_moment_down,
    second_moment_feed,
    second_moment_up,
    optimizer_step,
):
    micro, seqs, seq = input_token_ids.shape
    rows = micro * seqs
    picks = scored_slots.shape[2]
    layers = frozen_attention.shape[0]
    last = layers - 1
    shards = lax.axis_size("fsdp")
    row_lengths = lengths.reshape(rows)
    slots = scored_slots.reshape(rows, picks)
    valid = slots < row_lengths[:, None]
    mask = valid.reshape(-1).astype(jnp.float32)
    all_slots = jnp.tile(jnp.arange(seq, dtype=jnp.int32)[None], (rows, 1))
    gain_final = final_norm_params[0].astype(jnp.float32)
    shift_final = final_norm_params[1].astype(jnp.float32)

    me = lax.axis_index("fsdp")
    small_all = everywhere(frozen_bias_gain[None]).transpose(1, 0, 2).reshape(layers, -1)
    weights = [
        unpack(small_all[layer], adapter_down[layer], adapter_down_feed[layer], adapter_up[layer])
        for layer in range(layers)
    ]
    units = []
    for layer in range(layers):
        units.append(frozen_attention[layer])
        if layer < last:
            units += [frozen_feed_input[layer], frozen_feed_output[layer]]
    wholes = gather_units(units)
    for layer in range(layers):
        attention = wholes[3 * layer]
        weights[layer]["w_qkv"] = attention[:, : 3 * MODEL_WIDTH]
        weights[layer]["w_o"] = attention[:, 3 * MODEL_WIDTH :]
        if layer < last:
            weights[layer]["w_fc"] = wholes[3 * layer + 1]
            weights[layer]["w_fp"] = wholes[3 * layer + 2]
    share = HIDDEN_UNITS // shards
    own_units = partial(lax.dynamic_slice_in_dim, start_index=me * share, slice_size=share)
    weights[last]["w_fc"] = lax.all_to_all(
        tie(frozen_feed_input[last], wholes[2]), "fsdp", 1, 0, tiled=True
    )
    weights[last]["w_fp"] = frozen_feed_output[last]
    weights[last]["c_fc"] = own_units(weights[last]["c_fc"])
    weights[last]["d_fp"] = own_units(weights[last]["d_fp"])
    weights[last]["u_fc"] = own_units(weights[last]["u_fc"], axis=1)

    useful = jnp.max(jnp.where(valid, slots, -1), axis=1)
    needed = jnp.concatenate([(all_slots <= useful[:, None]).reshape(-1), valid.reshape(-1)])
    ids = jnp.concatenate([input_token_ids.reshape(-1), scored_targets.reshape(-1)])
    looked_up = lookup(wte, ids, needed)
    hidden = looked_up[: rows * seq] + jnp.tile(wpe.astype(jnp.float32), (rows, 1))
    target_rows = looked_up[rows * seq :]

    def heads(part):
        return part.reshape(rows, -1, H, HD)

    saved_layers = []
    for layer in range(last):
        w = weights[layer]
        values, a_hat, a_rstd = norm_fwd(hidden, w["g_one"], w["b_one"])
        a_low = values.astype(jnp.bfloat16)
        qkv, ua = projection(a_low, w["w_qkv"], w["c_qkv"], w["d_qkv"], w["u_qkv"])
        qkv_low = qkv.astype(jnp.bfloat16)
        query, key, value = (heads(part) for part in jnp.split(qkv_low, 3, axis=1))
        o_low, lse = attend(query, key, value, all_slots, row_lengths)
        branch, uo = projection(o_low, w["w_o"], w["c_o"], w["d_o"], w["u_o"])
        middle = hidden + branch
        hidden, feed_saved = feed_forward(middle, w)
        saved_layers.append((a_hat, a_rstd, a_low, ua, query, key, value, lse, o_low, uo, feed_saved))

    w = weights[last]
    values, a_hat, a_rstd = norm_fwd(hidden, w["g_one"], w["b_one"])
    a_low = values.astype(jnp.bfloat16)
    picked = (slots[:, :, None] == all_slots[:, None, :]).astype(jnp.bfloat16)
    flat_index = (slots + seq * jnp.arange(rows, dtype=jnp.int32)[:, None]).reshape(-1)
    a_sel = jnp.einsum(
        "rps,rsd->rpd",
        picked,
        a_low.reshape(rows, seq, -1),
        preferred_element_type=jnp.bfloat16,
    ).reshape(rows * picks, -1)
    hidden_sel = jnp.take(hidden, flat_index, axis=0)
    split = MODEL_WIDTH
    kv, ua = projection(
        a_low, w["w_qkv"][:, split:], w["c_qkv"][split:], w["d_qkv"], w["u_qkv"][:, split:]
    )
    q_sel, ua_sel = projection(
        a_sel, w["w_qkv"][:, :split], w["c_qkv"][:split], w["d_qkv"], w["u_qkv"][:, :split]
    )
    kv_low = kv.astype(jnp.bfloat16)
    key, value = heads(kv_low[:, :split]), heads(kv_low[:, split:])
    query = heads(q_sel.astype(jnp.bfloat16))
    o_low, lse = attend(query, key, value, slots, row_lengths)
    branch, uo = projection(o_low, w["w_o"], w["c_o"], w["d_o"], w["u_o"])
    middle = hidden_sel + branch
    final, feed_saved = split_feed_forward(middle, w)

    h_val, h_hat, h_rstd = norm_fwd(final, gain_final, shift_final)
    h_low = h_val.astype(jnp.bfloat16)
    h_all = everywhere(h_low)
    logits = product_right_transposed(h_all, wte)
    top = jnp.max(logits, axis=-1, keepdims=True)
    weight_low = jnp.exp(logits - top).astype(jnp.bfloat16)
    part_sum = jnp.sum(jnp.exp(logits - top), axis=-1, keepdims=True)
    part_rows = product_plain(weight_low, wte).astype(jnp.bfloat16)
    got_rows = owned_parts(part_rows)
    got_stats = owned_parts(jnp.concatenate([top, part_sum], 1))
    whole_top = jnp.max(got_stats[:, :, 0], axis=0)
    whole_lse = whole_top + jnp.log(
        jnp.sum(got_stats[:, :, 1] * jnp.exp(got_stats[:, :, 0] - whole_top), axis=0)
    )
    shares = jnp.exp(got_stats[:, :, 0] - whole_lse)
    target_logit = jnp.sum(h_low.astype(jnp.float32) * target_rows, axis=-1)
    own_terms = (whole_lse - target_logit) * mask
    d_hidden = mask[:, None] * (
        jnp.sum(got_rows.astype(jnp.float32) * shares[:, :, None], axis=0) - target_rows
    )
    gradient = norm_backward(d_hidden, h_hat, h_rstd, gain_final)

    grads = [None] * layers
    gradient, feed_grads = split_feed_backward(gradient, w, feed_saved)
    grad_do, grad_uo, d_heads = projection_back(
        gradient.astype(jnp.bfloat16), o_low, uo, w["w_o"], w["d_o"], w["u_o"]
    )
    d_query, d_key, d_value = attend_back(
        d_heads.astype(jnp.bfloat16), query, key, value, lse, slots, row_lengths
    )
    grad_dq, grad_uq, d_sel = projection_back(
        d_query, a_sel, ua_sel, w["w_qkv"][:, :split], w["d_qkv"], w["u_qkv"][:, :split]
    )
    d_kv = jnp.concatenate([d_key, d_value], 1)
    grad_dkv, grad_ukv, d_all = projection_back(
        d_kv, a_low, ua, w["w_qkv"][:, split:], w["d_qkv"], w["u_qkv"][:, split:]
    )
    own_first = jnp.zeros((ADAPTER_RANK, HIDDEN_UNITS), jnp.float32)
    grads[last] = [
        grad_dq + grad_dkv,
        grad_do,
        feed_grads[2],
        lax.dynamic_update_slice_in_dim(own_first, feed_grads[0], me * share, 1),
        grad_uq,
        grad_ukv,
        grad_uo,
        lax.dynamic_update_slice_in_dim(own_first, feed_grads[3], me * share, 1),
        feed_grads[1],
    ]
    spread = jnp.einsum(
        "rps,rpd->rsd",
        picked.astype(jnp.float32),
        jnp.concatenate([d_sel, gradient], 1).reshape(rows, picks, -1),
        precision=lax.Precision.HIGHEST,
    ).reshape(rows * seq, -1)
    gradient = spread[:, MODEL_WIDTH:] + norm_backward(
        d_all + spread[:, :MODEL_WIDTH], a_hat, a_rstd, w["g_one"]
    )

    for layer in reversed(range(last)):
        w = weights[layer]
        a_hat, a_rstd, a_low, ua, query, key, value, lse, o_low, uo, feed_saved = saved_layers[layer]
        gradient, feed_grads = feed_backward(gradient, w, feed_saved)
        grad_do, grad_uo, d_heads = projection_back(
            gradient.astype(jnp.bfloat16), o_low, uo, w["w_o"], w["d_o"], w["u_o"]
        )
        d_qkv = jnp.concatenate(
            attend_back(
                d_heads.astype(jnp.bfloat16), query, key, value, lse, all_slots, row_lengths
            ),
            1,
        )
        grad_dqkv, grad_uqkv, d_norm = projection_back(
            d_qkv, a_low, ua, w["w_qkv"], w["d_qkv"], w["u_qkv"], into_rows=layer > 0
        )
        if layer > 0:
            gradient = gradient + norm_backward(d_norm, a_hat, a_rstd, w["g_one"])
        grads[layer] = [
            grad_dqkv,
            grad_do,
            feed_grads[2],
            feed_grads[0],
            grad_uqkv,
            grad_uo,
            feed_grads[3],
            feed_grads[1],
        ]

    gradients = jnp.concatenate([jnp.concatenate(parts, 1) for parts in grads], 0)
    gradients, totals = summed_everywhere(
        gradients, jnp.stack([jnp.sum(own_terms), jnp.sum(mask)])
    )
    loss_total, count = totals[0], totals[1]
    gradients = gradients / count
    norm = jnp.sqrt(jnp.sum(gradients * gradients))
    by_layer = gradients.reshape(layers, ADAPTER_RANK, -1)
    gradient_tree = [
        by_layer[:, :, : 3 * MODEL_WIDTH]
        .reshape(layers, ADAPTER_RANK, 3, MODEL_WIDTH)
        .transpose(0, 3, 2, 1)
        .reshape(layers, MODEL_WIDTH, 3 * ADAPTER_RANK),
        by_layer[:, :, 3 * MODEL_WIDTH : 3 * MODEL_WIDTH + HIDDEN_UNITS].transpose(0, 2, 1),
        by_layer[:, :, 3 * MODEL_WIDTH + HIDDEN_UNITS :],
    ]
    scale_factor = jnp.minimum(1.0, CLIP / (norm + 1e-06))
    step_number = optimizer_step[0].astype(jnp.float32)
    updated = [
        moment_update(weight, first, second, gradient_value, scale_factor, step_number)
        for weight, first, second, gradient_value in zip(
            (adapter_down, adapter_down_feed, adapter_up),
            (first_moment_down, first_moment_feed, first_moment_up),
            (second_moment_down, second_moment_feed, second_moment_up),
            gradient_tree,
        )
    ]
    return (
        loss_total / count,
        norm,
        *(part[0] for part in updated),
        *(part[1] for part in updated),
        *(part[2] for part in updated),
        own_terms.reshape(micro, seqs, picks),
    )


def solution(mesh):
    in_specs = (
        P(None, ("dp", "fsdp"), None),
        P(None, ("dp", "fsdp")),
        P(None, ("dp", "fsdp"), None),
        P(None, ("dp", "fsdp"), None),
        P("fsdp", None),
        P(),
        P(None, "fsdp", None),
        P(None, "fsdp", None),
        P(None, "fsdp", None),
        P(None, "fsdp"),
        P(),
        P(),
        P(),
        P(),
        P(),
        P(),
        P(),
        P(),
        P(),
        P(),
        P(),
    )
    out_specs = (
        P(),
        P(),
        P(),
        P(),
        P(),
        P(),
        P(),
        P(),
        P(),
        P(),
        P(),
        P(None, ("dp", "fsdp"), None),
    )
    return jax.shard_map(body, mesh=mesh, in_specs=in_specs, out_specs=out_specs, check_vma=False)
```

time: 1000 us -> 669 us (0.67)
  waiting for transfers between devices: 369 us -> 127 us
  blocking collectives: 161 us -> 17.8 us
  starting transfers between devices: 0.44 us -> 80.5 us
  matrix products: 274 us -> 204 us
  local copies, waits for them, and re-layouts: 89.3 us -> 136 us
  between operations: 26.6 us -> 11.5 us
  Pallas kernels: 0 us -> 14.6 us
    all_gather x6 -> x0, waiting for transfers between devices: 214 us -> none  [the longest x2 88.1 us: body(): lax.all_gather(frozen_feed_output[layer_index], 'fsdp', axis=0, tiled=True)]
    all_gather x14 -> x0, blocking collectives: 122 us -> none  [the longest x4 33.6 us: joined(): everything = jax.tree.map(lambda part: lax.all_gather(part, axis), x)]
    psum x1 -> x0, waiting for transfers between devices: 84.2 us -> none  [body(): lax.psum((batch_sums[0], batch_sums[1], batch_sums[2], batch_sums[3], bat...]
    all_to_all x0 -> x12, waiting for transfers between devices: none -> 69.8 us  [the longest x5 35.8 us: owned_parts(): lax.all_to_all(parts, 'fsdp', 0, 0, tiled=True)]
    reduce_scatter x4 -> x0, waiting for transfers between devices: 68.9 us -> none  [the longest x2 57.9 us: body(): lax.psum_scatter(product_plain(d_logits, wte), 'fsdp', scatter_dimension=...]
    ppermute x0 -> x42, waiting for transfers between devices: none -> 57.1 us  [the longest x36 51.7 us: swap(): lax.ppermute(part, 'fsdp', [(i, i ^ bit) for i in range(lax.axis_size('fs...]
    all_to_all x0 -> x12, starting transfers between devices: none -> 48.4 us  [the longest x5 20.7 us: owned_parts(): lax.all_to_all(parts, 'fsdp', 0, 0, tiled=True)]
    reshape x0 -> x19, local copies, waits for them, and re-layouts: none -> 44.5 us  [the longest x11 33.4 us: heads(): return part.reshape(rows, -1, H, HD)]
  transfers between devices with their start and end apart: 11 -> 54, of which waited for: 10 -> 20; matrix products, arithmetic and copies ran while one was open for 18% -> 32% of each run, Pallas kernels for 0% -> 2%
where the time goes in v1:
time: 669 us; the launch traced here: 658 us
  matrix products  204 us (30%)
  local copies, waits for them, and re-layouts  136 us (20%)
  waiting for transfers between devices  127 us (19%)
  starting transfers between devices  80.5 us (12%)
  other arithmetic  66.7 us (10%)
  blocking collectives  17.8 us (3%)
  Pallas kernels  14.6 us (2%)
  between operations  11.5 us (2%)
    dot_general x29, matrix products, product_plain(): return jnp.dot(left, right, preferred_element_type=jnp.float32)  79 us
    dot_general x25, matrix products, product_right_transposed(): lax.dot_general(left, right, (((1,), (1,)), ((), ())), preferred_element_...  75.8 us
    ppermute x36, waiting for transfers between devices, swap(): lax.ppermute(part, 'fsdp', [(i, i ^ bit) for i in range(lax.axis_size('fs...  51.7 us
    all_to_all x5, waiting for transfers between devices, owned_parts(): lax.all_to_all(parts, 'fsdp', 0, 0, tiled=True)  35.8 us
    reshape x11, local copies, waits for them, and re-layouts, heads(): return part.reshape(rows, -1, H, HD)  33.4 us
    all_to_all x4, waiting for transfers between devices, everywhere(): lax.all_to_all(jnp.tile(part, (shards,) + (1,) * (part.ndim - 1)), 'fsdp'...  32.4 us
    ppermute x36, starting transfers between devices, swap(): lax.ppermute(part, 'fsdp', [(i, i ^ bit) for i in range(lax.axis_size('fs...  22.3 us
    unnamed x300, local copies, waits for them, and re-layouts  21.9 us
  transfers between devices with their start and end apart: 54, of which 20 were waited for; matrix products, arithmetic and copies ran while one was open for 32% of the time, Pallas kernels for 2%

profile of v1, /device:TPU:0, one launch (start us, length us, event | category | flops | bytes accessed | tf_op | source)
XLA Modules:
  0.0 658.2 jit_solution(15127388374831713480)
XLA Ops:
  36.6 10.8 %gather_fusion.1 = bf16[640,1024]{1,0:T(8,128)(2,1)} fusion(bf16[6288,1024]{1,0:T(8,128)(2,1)} %param.29, s32[1024]{0:T(1024)S(1)} %pad_clamp_fusion.2), kind=kCustom, calls=%fused_computation.1 | custom fusion | bytes 2624000 | tf_op jit(solution)/shard_map/gather | solution.py:220
  47.4 4.4 all-to-all-start.3
  79.6 3.9 fusion.53
  86.3 22.5 %collective-permute-done.8.refs_6_ = bf16[64,4096]{1,0:T(8,128)(2,1)} collective-permute-done((bf16[64,4096]{1,0:T(8,128)(2,1)}, bf16[64,4096]{1,0:T(8,128)(2,1)}, u32[]{:S(2)}, u32[]{:S(2)}) %collective-permute-start.8) | collective-permute-done | bytes 524320 | tf_op jit(solution)/shard_map/ppermute | solution.py:237
  116.1 3.8 shard_map.292
  120.0 3.7 add_convert_fusion
  125.5 4.0 reshape.1009
  133.0 4.0 reshape.1008
  137.1 3.6 copy.248
  147.0 4.0 reshape.1010
  151.1 3.7 copy.225
  154.8 5.7 fusion.58
  170.0 7.2 %collective-permute-done.17.refs_6_ = bf16[64,4096]{1,0:T(8,128)(2,1)S(1)} collective-permute-done((bf16[64,4096]{1,0:T(8,128)(2,1)S(1)}, bf16[64,4096]{1,0:T(8,128)(2,1)S(1)}, u32[]{:S(2)}, u32[]{:S(2)}) %collective-permute-start.17) | collective-permute-done | bytes 524320 | tf_op jit(solution)/shard_map/ppermute | solution.py:237
  180.2 9.8 %collective-permute-done.18.refs_7_ = bf16[64,4096]{1,0:T(8,128)(2,1)S(1)} collective-permute-done((bf16[64,4096]{1,0:T(8,128)(2,1)S(1)}, bf16[64,4096]{1,0:T(8,128)(2,1)S(1)}, u32[]{:S(2)}, u32[]{:S(2)}) %collective-permute-start.18) | collective-permute-done | bytes 524320 | tf_op jit(solution)/shard_map/ppermute | solution.py:237
  193.4 4.6 fusion.152
  207.0 12.4 %multiply_convert_fusion.1 = (bf16[512,4096]{1,0:T(8,128)(2,1)}, f32[512,4096]{1,0:T(8,128)}) fusion(f32[512,4096]{1,0:T(8,128)} %fusion.152, f32[4096]{0:T(1024)S(1)} %copy-done.115, bf16[512,1024]{1,0:T(8,128)(2,1)S(1)} %add_convert_fusion.7, bf16[1024,4096]{1,0:T(8,128)(2,1)S(1)} %shard_map.293), kind=kOutput, calls=%fused_computation.32 | convolution fusion | flops 4320133120 | bytes 30425088 | tf_op jit(solution)/shard_map/dot_general | solution.py:29
  219.5 8.8 %collective-permute-done.31.refs_2_ = bf16[128,4096]{1,0:T(8,128)(2,1)} collective-permute-done((bf16[128,4096]{1,0:T(8,128)(2,1)S(1)}, bf16[128,4096]{1,0:T(8,128)(2,1)}, u32[]{:S(2)}, u32[]{:S(2)}) %collective-permute-start.31) | collective-permute-done | bytes 1048608 | tf_op jit(solution)/shard_map/ppermute | solution.py:237
  239.0 3.9 shard_map.294
  242.9 4.8 fusion.242
  253.7 4.4 all-to-all-start.6
  263.5 3.6 shard_map.295
  271.0 5.9 add_convert_fusion.1
  296.6 4.2 all-to-all-start.5
  307.2 9.0 %all-to-all-done.5 = bf16[8,64,1024]{2,1,0:T(8,128)(2,1)} async-done(((bf16[8,64,1024]{2,1,0:T(8,128)(2,1)}), bf16[8,64,1024]{2,1,0:T(8,128)(2,1)}, u32[]{:S(2)}, u32[]{:S(2)}) %all-to-all-start.5) | async-done | bytes 1048608 | tf_op jit(solution)/shard_map/all_to_all | solution.py:311
  326.4 4.6 all-to-all-start.7
  332.4 14.1 %all-to-all-done.7 = bf16[8,64,1024]{2,1,0:T(8,128)(2,1)} async-done(((bf16[8,64,1024]{2,1,0:T(8,128)(2,1)}), bf16[8,64,1024]{2,1,0:T(8,128)(2,1)}, u32[]{:S(2)}, u32[]{:S(2)}) %all-to-all-start.7) | async-done | bytes 1048608 | tf_op jit(solution)/shard_map/all_to_all | solution.py:319
  351.3 17.8 %all_to_all.154 = bf16[8,64,1024]{2,1,0:T(8,128)(2,1)S(1)} all-to-all(bf16[8,64,1024]{2,1,0:T(8,128)(2,1)S(1)} %tile.25), channel_id=1, replica_groups=mesh['dp'=4,'fsdp'=8] {'fsdp'}, dimensions={0} | all-to-all | bytes 2097152 | tf_op jit(solution)/shard_map/all_to_all | solution.py:311
  369.1 15.2 %fusion.245 = (f32[512]{0:T(512)}, f32[512,6288]{0,1:T(8,128)}) fusion(bf16[512,1024]{1,0:T(8,128)(2,1)S(1)} %bitcast.329, bf16[6288,1024]{1,0:T(8,128)(2,1)} %get-tuple-element.537), kind=kOutput, calls=%fused_computation.422 | convolution fusion | flops 6596664832 | bytes 26806272 | tf_op jit(solution)/shard_map/dot_general | solution.py:39
  385.6 7.0 %fusion.8 = f32[512]{0:T(512)} fusion(f32[512,6288]{0,1:T(8,128)} %get-tuple-element.390, f32[512]{0:T(512)} %get-tuple-element.389), kind=kLoop, calls=%fused_computation.21 | loop fusion | flops 6438400 | bytes 12881920 | tf_op jit(solution)/shard_map/reduce_sum | solution.py:507
  396.6 3.9 all-to-all-start.10
  400.5 14.6 %fusion.50 = bf16[512,1024]{1,0:T(8,128)(2,1)} fusion(bf16[6288,1024]{1,0:T(8,128)(2,1)} %get-tuple-element.537, f32[512,6288]{0,1:T(8,128)} %get-tuple-element.390, f32[512]{0:T(512)} %get-tuple-element.389), kind=kOutput, calls=%fused_computation.97 | convolution fusion | flops 6600409088 | bytes 26806272 | tf_op jit(solution)/shard_map/dot_general | solution.py:29
  415.0 4.2 all-to-all-start.9
  428.8 5.9 all-to-all-done.9
  439.6 4.2 all-to-all-start.11
  445.2 14.1 %all-to-all-done.11 = bf16[8,64,1024]{2,1,0:T(8,128)(2,1)} async-done(((bf16[8,64,1024]{2,1,0:T(8,128)(2,1)}), bf16[8,64,1024]{2,1,0:T(8,128)(2,1)}, u32[]{:S(2)}, u32[]{:S(2)}) %all-to-all-start.11) | async-done | bytes 1048608 | tf_op jit(solution)/shard_map/all_to_all | solution.py:311
  468.8 4.4 all-to-all-start.12
  482.6 5.8 all-to-all-done.12
  518.3 4.5 fusion.150
  522.8 16.4 %fusion.16 = bf16[512,4096]{1,0:T(8,128)(2,1)} fusion(f32[512,4096]{1,0:T(8,128)} %get-tuple-element.380, f32[512,4096]{1,0:T(8,128)} %fusion.150, bf16[4096,1024]{1,0:T(8,128)(2,1)} %copy-done.3, f32[512,1024]{1,0:T(8,128)S(1)} %slice_add_fusion.1), kind=kOutput, calls=%fused_computation.29 | convolution fusion | flops 4339531776 | bytes 31457280 | tf_op jit(solution)/shard_map/dot_general | solution.py:39
  544.7 7.7 %fusion.222 = (f32[512]{0:T(512)S(1)}, f32[512]{0:T(512)S(1)}, f32[512,1024]{1,0:T(8,128)}) fusion(f32[512]{0:T(512)S(1)} %copy-done.98, f32[512,1024]{1,0:T(8,128)S(1)} %copy-done.10, f32[512]{0:T(512)S(1)} %copy-done.94, f32[1024]{0:T(1024)S(1)} %copy-done.108, f32[512,1024]{1,0:T(8,128)} %fusion.176, bf16[512,4096]{1,0:T(8,128)(2,1)S(1)} %copy-done.16, ...), kind=kOutput, calls=%fused_computation.403 | convolution fusion | flops 4298636288 | bytes 18886656 | tf_op jit(solution)/shard_map/dot_general | solution.py:39
  555.6 4.0 add_convert_fusion.2
  559.6 4.0 reshape.1013
  563.6 3.6 copy.246
  567.3 5.8 fusion.60
  573.1 5.3 multiply_reduce_fusion
  615.0 10.0 %all-to-all-done.13 = f32[8,8,2176]{2,1,0:T(8,128)S(1)} async-done(((f32[8,8,2176]{2,1,0:T(8,128)}), f32[8,8,2176]{2,1,0:T(8,128)S(1)}, u32[]{:S(2)}, u32[]{:S(2)}) %all-to-all-start.13) | async-done | bytes 557088 | tf_op jit(solution)/shard_map/all_to_all | solution.py:319
  633.9 3.7 all-to-all-start.14
  638.3 9.3 %all-to-all-done.14 = f32[8,8,2176]{2,1,0:T(8,128)S(1)} async-done(((f32[8,8,2176]{2,1,0:T(8,128)}), f32[8,8,2176]{2,1,0:T(8,128)S(1)}, u32[]{:S(2)}, u32[]{:S(2)}) %all-to-all-start.14) | async-done | bytes 557088 | tf_op jit(solution)/shard_map/all_to_all | solution.py:311
  (632 shorter events, 303.7 us)
Async XLA Ops:
  3.4 68.2 %collective-permute-start.4 = (bf16[128,4096]{1,0:T(8,128)(2,1)}, bf16[128,4096]{1,0:T(8,128)(2,1)}, u32[]{:S(2)}, u32[]{:S(2)}) collective-permute-start(bf16[128,4096]{1,0:T(8,128)(2,1)} %get-tuple-element.340.refs_0_), channel_id=1, source_target_pairs={{0,2},{1,3},{2,0},{3,1},{4,6},{5,7},{6,4},{7,5},{8,10},{9,11},{10,... | collective-permute-start | bytes 3145736 | tf_op jit(solution)/shard_map/ppermute | solution.py:237
  6.4 65.3 %collective-permute-start.6 = (bf16[128,4096]{1,0:T(8,128)(2,1)}, bf16[128,4096]{1,0:T(8,128)(2,1)}, u32[]{:S(2)}, u32[]{:S(2)}) collective-permute-start(bf16[128,4096]{1,0:T(8,128)(2,1)} %get-tuple-element.340.refs_0_), channel_id=1, source_target_pairs={{0,4},{1,5},{2,6},{3,7},{4,0},{5,1},{6,2},{7,3},{8,12},{9,13},{10,... | collective-permute-start | bytes 3145736 | tf_op jit(solution)/shard_map/ppermute | solution.py:237
  7.9 105.6 %collective-permute-start.3 = (bf16[128,4096]{1,0:T(8,128)(2,1)}, bf16[128,4096]{1,0:T(8,128)(2,1)}, u32[]{:S(2)}, u32[]{:S(2)}) collective-permute-start(bf16[128,4096]{1,0:T(8,128)(2,1)} %get-tuple-element.340.refs_0_), channel_id=1, source_target_pairs={{0,1},{1,0},{2,3},{3,2},{4,5},{5,4},{6,7},{7,6},{8,9},{9,8},{10,11... | collective-permute-start | bytes 3145736 | tf_op jit(solution)/shard_map/ppermute | solution.py:237
  23.9 7.8 %all-to-all-start.2 = ((s32[8,1,81]{2,1,0:T(1,128)}), s32[8,1,81]{2,1,0:T(1,128)S(1)}, u32[]{:S(2)}, u32[]{:S(2)}) async-start(s32[8,1,81]{2,1,0:T(1,128)} %bitcast.3), calls=%async_computation.2 | async-start | bytes 8192 | tf_op jit(solution)/shard_map/all_to_all | solution.py:219
  33.2 14.1 %all-to-all-start.4 = ((bf16[8,2,1664]{2,1,0:T(2,128)(2,1)}), bf16[8,2,1664]{2,1,0:T(2,128)(2,1)S(1)}, u32[]{:S(2)}, u32[]{:S(2)}) async-start(bf16[8,2,1664]{2,1,0:T(2,128)(2,1)} %tile.23), calls=%async_computation.4 | async-start | bytes 106496 | tf_op jit(solution)/shard_map/all_to_all | solution.py:311
  47.4 32.3 %all-to-all-start.3 = ((bf16[8,80,1024]{2,1,0:T(8,128)(2,1)}), bf16[8,80,1024]{2,1,0:T(8,128)(2,1)}, u32[]{:S(2)}, u32[]{:S(2)}) async-start(bf16[8,80,1024]{2,1,0:T(8,128)(2,1)} %bitcast.306), calls=%async_computation.3 | async-start | bytes 2621440 | tf_op jit(solution)/shard_map/all_to_all | solution.py:221
  59.1 5.6 collective-permute-start
  60.7 7.1 %collective-permute-start.1 = (s32[]{:T(128)}, s32[]{:T(128)}, u32[]{:S(2)}, u32[]{:S(2)}) collective-permute-start(s32[]{:T(128)} %slice_reduce_fusion), channel_id=1, source_target_pairs={{0,16},{8,24},{16,0},{24,8},{1,17},{9,25},{17,1},{25,9},{2,18},{10... | collective-permute-start | bytes 20 | tf_op jit(solution)/shard_map/ppermute | solution.py:228
  71.7 39.8 %collective-permute-start.13 = (bf16[128,4096]{1,0:T(8,128)(2,1)S(1)}, bf16[128,4096]{1,0:T(8,128)(2,1)}, u32[]{:S(2)}, u32[]{:S(2)}) collective-permute-start(bf16[128,4096]{1,0:T(8,128)(2,1)S(1)} %get-tuple-element.178.refs_0_), channel_id=1, source_target_pairs={{0,2},{1,3},{2,0},{3,1},{4,6},{5,7},{6,4},{7,5},{8,10},{9,11},{10,... | collective-permute-start | bytes 3145736 | tf_op jit(solution)/shard_map/ppermute | solution.py:237
  73.6 38.0 %collective-permute-start.15 = (bf16[128,4096]{1,0:T(8,128)(2,1)S(1)}, bf16[128,4096]{1,0:T(8,128)(2,1)}, u32[]{:S(2)}, u32[]{:S(2)}) collective-permute-start(bf16[128,4096]{1,0:T(8,128)(2,1)S(1)} %get-tuple-element.178.refs_0_), channel_id=1, source_target_pairs={{0,4},{1,5},{2,6},{3,7},{4,0},{5,1},{6,2},{7,3},{8,12},{9,13},{10,... | collective-permute-start | bytes 3145736 | tf_op jit(solution)/shard_map/ppermute | solution.py:237
  77.0 31.8 %collective-permute-start.8 = (bf16[64,4096]{1,0:T(8,128)(2,1)}, bf16[64,4096]{1,0:T(8,128)(2,1)}, u32[]{:S(2)}, u32[]{:S(2)}) collective-permute-start(bf16[64,4096]{1,0:T(8,128)(2,1)} %slice.368), channel_id=1, source_target_pairs={{0,4},{1,5},{2,6},{3,7},{4,0},{5,1},{6,2},{7,3},{8,12},{9,13},{10,... | collective-permute-start | bytes 1572872 | tf_op jit(solution)/shard_map/ppermute | solution.py:237
  79.5 29.3 %collective-permute-start.9 = (bf16[64,4096]{1,0:T(8,128)(2,1)}, bf16[64,4096]{1,0:T(8,128)(2,1)}, u32[]{:S(2)}, u32[]{:S(2)}) collective-permute-start(bf16[64,4096]{1,0:T(8,128)(2,1)} %slice.369), channel_id=1, source_target_pairs={{0,2},{1,3},{2,0},{3,1},{4,6},{5,7},{6,4},{7,5},{8,10},{9,11},{10,... | collective-permute-start | bytes 1572872 | tf_op jit(solution)/shard_map/ppermute | solution.py:237
  108.8 7.4 %collective-permute-start.5 = (bf16[128,4096]{1,0:T(8,128)(2,1)}, bf16[128,4096]{1,0:T(8,128)(2,1)S(1)}, u32[]{:S(2)}, u32[]{:S(2)}) collective-permute-start(bf16[128,4096]{1,0:T(8,128)(2,1)} %collective-permute-done.4.refs_2_), channel_id=1, source_target_pairs={{0,1},{1,0},{2,3},{3,2},{4,5},{5,4},{6,7},{7,6},{8,9},{9,8},{10,11... | collective-permute-start | bytes 3145736 | tf_op jit(solution)/shard_map/ppermute | solution.py:237
  108.8 7.4 %collective-permute-start.7 = (bf16[128,4096]{1,0:T(8,128)(2,1)}, bf16[128,4096]{1,0:T(8,128)(2,1)S(1)}, u32[]{:S(2)}, u32[]{:S(2)}) collective-permute-start(bf16[128,4096]{1,0:T(8,128)(2,1)} %collective-permute-done.6.refs_4_), channel_id=1, source_target_pairs={{0,1},{1,0},{2,3},{3,2},{4,5},{5,4},{6,7},{7,6},{8,9},{9,8},{10,11... | collective-permute-start | bytes 3145736 | tf_op jit(solution)/shard_map/ppermute | solution.py:237
  113.5 78.0 %collective-permute-start.12 = (bf16[128,4096]{1,0:T(8,128)(2,1)S(1)}, bf16[128,4096]{1,0:T(8,128)(2,1)}, u32[]{:S(2)}, u32[]{:S(2)}) collective-permute-start(bf16[128,4096]{1,0:T(8,128)(2,1)S(1)} %get-tuple-element.178.refs_0_), channel_id=1, source_target_pairs={{0,1},{1,0},{2,3},{3,2},{4,5},{5,4},{6,7},{7,6},{8,9},{9,8},{10,11... | collective-permute-start | bytes 3145736 | tf_op jit(solution)/shard_map/ppermute | solution.py:237
  113.9 64.4 %collective-permute-start.22 = (bf16[512,1024]{1,0:T(8,128)(2,1)S(1)}, bf16[512,1024]{1,0:T(8,128)(2,1)}, u32[]{:S(2)}, u32[]{:S(2)}) collective-permute-start(bf16[512,1024]{1,0:T(8,128)(2,1)S(1)} %slice_bitcast_fusion.1.refs_0_), channel_id=1, source_target_pairs={{0,2},{1,3},{2,0},{3,1},{4,6},{5,7},{6,4},{7,5},{8,10},{9,11},{10,... | collective-permute-start | bytes 3145736 | tf_op jit(solution)/shard_map/ppermute | solution.py:237
  114.6 75.3 %collective-permute-start.24 = (bf16[512,1024]{1,0:T(8,128)(2,1)S(1)}, bf16[512,1024]{1,0:T(8,128)(2,1)}, u32[]{:S(2)}, u32[]{:S(2)}) collective-permute-start(bf16[512,1024]{1,0:T(8,128)(2,1)S(1)} %slice_bitcast_fusion.1.refs_0_), channel_id=1, source_target_pairs={{0,4},{1,5},{2,6},{3,7},{4,0},{5,1},{6,2},{7,3},{8,12},{9,13},{10,... | collective-permute-start | bytes 3145736 | tf_op jit(solution)/shard_map/ppermute | solution.py:237
  163.4 13.8 %collective-permute-start.17 = (bf16[64,4096]{1,0:T(8,128)(2,1)S(1)}, bf16[64,4096]{1,0:T(8,128)(2,1)S(1)}, u32[]{:S(2)}, u32[]{:S(2)}) collective-permute-start(bf16[64,4096]{1,0:T(8,128)(2,1)S(1)} %slice.382), channel_id=1, source_target_pairs={{0,4},{1,5},{2,6},{3,7},{4,0},{5,1},{6,2},{7,3},{8,12},{9,13},{10,... | collective-permute-start | bytes 1572872 | tf_op jit(solution)/shard_map/ppermute | solution.py:237
  164.0 28.2 %collective-permute-start.14 = (bf16[128,4096]{1,0:T(8,128)(2,1)}, bf16[128,4096]{1,0:T(8,128)(2,1)S(1)}, u32[]{:S(2)}, u32[]{:S(2)}) collective-permute-start(bf16[128,4096]{1,0:T(8,128)(2,1)} %collective-permute-done.13.refs_2_), channel_id=1, source_target_pairs={{0,1},{1,0},{2,3},{3,2},{4,5},{5,4},{6,7},{7,6},{8,9},{9,8},{10,11... | collective-permute-start | bytes 3145736 | tf_op jit(solution)/shard_map/ppermute | solution.py:237
  177.2 12.8 %collective-permute-start.18 = (bf16[64,4096]{1,0:T(8,128)(2,1)S(1)}, bf16[64,4096]{1,0:T(8,128)(2,1)S(1)}, u32[]{:S(2)}, u32[]{:S(2)}) collective-permute-start(bf16[64,4096]{1,0:T(8,128)(2,1)S(1)} %slice.383), channel_id=1, source_target_pairs={{0,2},{1,3},{2,0},{3,1},{4,6},{5,7},{6,4},{7,5},{8,10},{9,11},{10,... | collective-permute-start | bytes 1572872 | tf_op jit(solution)/shard_map/ppermute | solution.py:237
  178.3 19.8 %collective-permute-start.16 = (bf16[128,4096]{1,0:T(8,128)(2,1)}, bf16[128,4096]{1,0:T(8,128)(2,1)S(1)}, u32[]{:S(2)}, u32[]{:S(2)}) collective-permute-start(bf16[128,4096]{1,0:T(8,128)(2,1)} %collective-permute-done.15.refs_4_), channel_id=1, source_target_pairs={{0,1},{1,0},{2,3},{3,2},{4,5},{5,4},{6,7},{7,6},{8,9},{9,8},{10,11... | collective-permute-start | bytes 3145736 | tf_op jit(solution)/shard_map/ppermute | solution.py:237
  190.0 8.2 %collective-permute-start.19 = (bf16[64,4096]{1,0:T(8,128)(2,1)S(1)}, bf16[64,4096]{1,0:T(8,128)(2,1)S(1)}, u32[]{:S(2)}, u32[]{:S(2)}) collective-permute-start(bf16[64,4096]{1,0:T(8,128)(2,1)S(1)} %collective-permute-done.17.refs_6_), channel_id=1, source_target_pairs={{0,1},{1,0},{2,3},{3,2},{4,5},{5,4},{6,7},{7,6},{8,9},{9,8},{10,11... | collective-permute-start | bytes 1572872 | tf_op jit(solution)/shard_map/ppermute | solution.py:237
  190.0 9.4 %collective-permute-start.20 = (bf16[64,4096]{1,0:T(8,128)(2,1)S(1)}, bf16[64,4096]{1,0:T(8,128)(2,1)S(1)}, u32[]{:S(2)}, u32[]{:S(2)}) collective-permute-start(bf16[64,4096]{1,0:T(8,128)(2,1)S(1)} %collective-permute-done.18.refs_7_), channel_id=1, source_target_pairs={{0,1},{1,0},{2,3},{3,2},{4,5},{5,4},{6,7},{7,6},{8,9},{9,8},{10,11... | collective-permute-start | bytes 1572872 | tf_op jit(solution)/shard_map/ppermute | solution.py:237
  191.6 14.9 %collective-permute-start.26 = (bf16[256,1024]{1,0:T(8,128)(2,1)S(1)}, bf16[256,1024]{1,0:T(8,128)(2,1)S(1)}, u32[]{:S(2)}, u32[]{:S(2)}) collective-permute-start(bf16[256,1024]{1,0:T(8,128)(2,1)S(1)} %slice.387), channel_id=1, source_target_pairs={{0,4},{1,5},{2,6},{3,7},{4,0},{5,1},{6,2},{7,3},{8,12},{9,13},{10,... | collective-permute-start | bytes 1572872 | tf_op jit(solution)/shard_map/ppermute | solution.py:237
  192.2 14.8 %collective-permute-start.27 = (bf16[256,1024]{1,0:T(8,128)(2,1)S(1)}, bf16[256,1024]{1,0:T(8,128)(2,1)S(1)}, u32[]{:S(2)}, u32[]{:S(2)}) collective-permute-start(bf16[256,1024]{1,0:T(8,128)(2,1)S(1)} %slice.388), channel_id=1, source_target_pairs={{0,2},{1,3},{2,0},{3,1},{4,6},{5,7},{6,4},{7,5},{8,10},{9,11},{10,... | collective-permute-start | bytes 1572872 | tf_op jit(solution)/shard_map/ppermute | solution.py:237
  198.1 38.4 %collective-permute-start.21 = (bf16[512,1024]{1,0:T(8,128)(2,1)S(1)}, bf16[512,1024]{1,0:T(8,128)(2,1)S(1)}, u32[]{:S(2)}, u32[]{:S(2)}) collective-permute-start(bf16[512,1024]{1,0:T(8,128)(2,1)S(1)} %slice_bitcast_fusion.1.refs_0_), channel_id=1, source_target_pairs={{0,1},{1,0},{2,3},{3,2},{4,5},{5,4},{6,7},{7,6},{8,9},{9,8},{10,11... | collective-permute-start | bytes 3145736 | tf_op jit(solution)/shard_map/ppermute | solution.py:237
  198.2 30.1 %collective-permute-start.31 = (bf16[128,4096]{1,0:T(8,128)(2,1)S(1)}, bf16[128,4096]{1,0:T(8,128)(2,1)}, u32[]{:S(2)}, u32[]{:S(2)}) collective-permute-start(bf16[128,4096]{1,0:T(8,128)(2,1)S(1)} %get-tuple-element.180.refs_0_), channel_id=1, source_target_pairs={{0,2},{1,3},{2,0},{3,1},{4,6},{5,7},{6,4},{7,5},{8,10},{9,11},{10,... | collective-permute-start | bytes 3145736 | tf_op jit(solution)/shard_map/ppermute | solution.py:237
  199.4 28.9 %collective-permute-start.33 = (bf16[128,4096]{1,0:T(8,128)(2,1)S(1)}, bf16[128,4096]{1,0:T(8,128)(2,1)}, u32[]{:S(2)}, u32[]{:S(2)}) collective-permute-start(bf16[128,4096]{1,0:T(8,128)(2,1)S(1)} %get-tuple-element.180.refs_0_), channel_id=1, source_target_pairs={{0,4},{1,5},{2,6},{3,7},{4,0},{5,1},{6,2},{7,3},{8,12},{9,13},{10,... | collective-permute-start | bytes 3145736 | tf_op jit(solution)/shard_map/ppermute | solution.py:237
  206.4 32.6 %collective-permute-start.23 = (bf16[512,1024]{1,0:T(8,128)(2,1)}, bf16[512,1024]{1,0:T(8,128)(2,1)S(1)}, u32[]{:S(2)}, u32[]{:S(2)}) collective-permute-start(bf16[512,1024]{1,0:T(8,128)(2,1)} %collective-permute-done.22.refs_2_), channel_id=1, source_target_pairs={{0,1},{1,0},{2,3},{3,2},{4,5},{5,4},{6,7},{7,6},{8,9},{9,8},{10,11... | collective-permute-start | bytes 3145736 | tf_op jit(solution)/shard_map/ppermute | solution.py:237
  207.0 32.0 %collective-permute-start.25 = (bf16[512,1024]{1,0:T(8,128)(2,1)}, bf16[512,1024]{1,0:T(8,128)(2,1)S(1)}, u32[]{:S(2)}, u32[]{:S(2)}) collective-permute-start(bf16[512,1024]{1,0:T(8,128)(2,1)} %collective-permute-done.24.refs_4_), channel_id=1, source_target_pairs={{0,1},{1,0},{2,3},{3,2},{4,5},{5,4},{6,7},{7,6},{8,9},{9,8},{10,11... | collective-permute-start | bytes 3145736 | tf_op jit(solution)/shard_map/ppermute | solution.py:237
  228.3 8.3 %collective-permute-start.28 = (bf16[256,1024]{1,0:T(8,128)(2,1)S(1)}, bf16[256,1024]{1,0:T(8,128)(2,1)S(1)}, u32[]{:S(2)}, u32[]{:S(2)}) collective-permute-start(bf16[256,1024]{1,0:T(8,128)(2,1)S(1)} %collective-permute-done.26.refs_6_), channel_id=1, source_target_pairs={{0,1},{1,0},{2,3},{3,2},{4,5},{5,4},{6,7},{7,6},{8,9},{9,8},{10,11... | collective-permute-start | bytes 1572872 | tf_op jit(solution)/shard_map/ppermute | solution.py:237
  228.3 9.9 %collective-permute-start.29 = (bf16[256,1024]{1,0:T(8,128)(2,1)S(1)}, bf16[256,1024]{1,0:T(8,128)(2,1)S(1)}, u32[]{:S(2)}, u32[]{:S(2)}) collective-permute-start(bf16[256,1024]{1,0:T(8,128)(2,1)S(1)} %collective-permute-done.27.refs_7_), channel_id=1, source_target_pairs={{0,1},{1,0},{2,3},{3,2},{4,5},{5,4},{6,7},{7,6},{8,9},{9,8},{10,11... | collective-permute-start | bytes 1572872 | tf_op jit(solution)/shard_map/ppermute | solution.py:237
  236.5 27.0 %collective-permute-start.30 = (bf16[128,4096]{1,0:T(8,128)(2,1)S(1)}, bf16[128,4096]{1,0:T(8,128)(2,1)S(1)}, u32[]{:S(2)}, u32[]{:S(2)}) collective-permute-start(bf16[128,4096]{1,0:T(8,128)(2,1)S(1)} %get-tuple-element.180.refs_0_), channel_id=1, source_target_pairs={{0,1},{1,0},{2,3},{3,2},{4,5},{5,4},{6,7},{7,6},{8,9},{9,8},{10,11... | collective-permute-start | bytes 3145736 | tf_op jit(solution)/shard_map/ppermute | solution.py:237
  236.6 23.3 %collective-permute-start.35 = (bf16[64,4096]{1,0:T(8,128)(2,1)}, bf16[64,4096]{1,0:T(8,128)(2,1)}, u32[]{:S(2)}, u32[]{:S(2)}) collective-permute-start(bf16[64,4096]{1,0:T(8,128)(2,1)} %slice.395), channel_id=1, source_target_pairs={{0,4},{1,5},{2,6},{3,7},{4,0},{5,1},{6,2},{7,3},{8,12},{9,13},{10,... | collective-permute-start | bytes 1572872 | tf_op jit(solution)/shard_map/ppermute | solution.py:237
  238.2 22.2 %collective-permute-start.36 = (bf16[64,4096]{1,0:T(8,128)(2,1)}, bf16[64,4096]{1,0:T(8,128)(2,1)}, u32[]{:S(2)}, u32[]{:S(2)}) collective-permute-start(bf16[64,4096]{1,0:T(8,128)(2,1)} %slice.396), channel_id=1, source_target_pairs={{0,2},{1,3},{2,0},{3,1},{4,6},{5,7},{6,4},{7,5},{8,10},{9,11},{10,... | collective-permute-start | bytes 1572872 | tf_op jit(solution)/shard_map/ppermute | solution.py:237
  249.1 14.4 %collective-permute-start.32 = (bf16[128,4096]{1,0:T(8,128)(2,1)}, bf16[128,4096]{1,0:T(8,128)(2,1)S(1)}, u32[]{:S(2)}, u32[]{:S(2)}) collective-permute-start(bf16[128,4096]{1,0:T(8,128)(2,1)} %collective-permute-done.31.refs_2_), channel_id=1, source_target_pairs={{0,1},{1,0},{2,3},{3,2},{4,5},{5,4},{6,7},{7,6},{8,9},{9,8},{10,11... | collective-permute-start | bytes 3145736 | tf_op jit(solution)/shard_map/ppermute | solution.py:237
  249.1 14.4 %collective-permute-start.34 = (bf16[128,4096]{1,0:T(8,128)(2,1)}, bf16[128,4096]{1,0:T(8,128)(2,1)}, u32[]{:S(2)}, u32[]{:S(2)}) collective-permute-start(bf16[128,4096]{1,0:T(8,128)(2,1)} %collective-permute-done.33.refs_4_), channel_id=1, source_target_pairs={{0,1},{1,0},{2,3},{3,2},{4,5},{5,4},{6,7},{7,6},{8,9},{9,8},{10,11... | collective-permute-start | bytes 3145736 | tf_op jit(solution)/shard_map/ppermute | solution.py:237
  253.7 40.9 %all-to-all-start.6 = ((bf16[128,8,512]{0,2,1:T(8,128)(2,1)}), bf16[128,8,512]{0,2,1:T(8,128)(2,1)}, u32[]{:S(2)}, u32[]{:S(2)}) async-start(bf16[128,8,512]{0,2,1:T(8,128)(2,1)} %bitcast.309), calls=%async_computation.6 | async-start | bytes 2097152 | tf_op jit(solution)/shard_map/all_to_all | solution.py:442
  296.6 19.7 %all-to-all-start.5 = ((bf16[8,64,1024]{2,1,0:T(8,128)(2,1)}), bf16[8,64,1024]{2,1,0:T(8,128)(2,1)}, u32[]{:S(2)}, u32[]{:S(2)}) async-start(bf16[8,64,1024]{2,1,0:T(8,128)(2,1)} %tile.24), calls=%async_computation.5 | async-start | bytes 2097152 | tf_op jit(solution)/shard_map/all_to_all | solution.py:311
  326.4 20.1 %all-to-all-start.7 = ((bf16[8,64,1024]{2,1,0:T(8,128)(2,1)}), bf16[8,64,1024]{2,1,0:T(8,128)(2,1)}, u32[]{:S(2)}, u32[]{:S(2)}) async-start(bf16[8,64,1024]{2,1,0:T(8,128)(2,1)} %bitcast.312), calls=%async_computation.7 | async-start | bytes 2097152 | tf_op jit(solution)/shard_map/all_to_all | solution.py:319
  396.6 18.4 %all-to-all-start.10 = ((f32[8,1,128]{2,1,0:T(1,128)}), f32[8,1,128]{2,1,0:T(1,128)}, u32[]{:S(2)}, u32[]{:S(2)}) async-start(f32[8,1,128]{2,1,0:T(1,128)} %reshape.1036), calls=%async_computation.10 | async-start | bytes 8192 | tf_op jit(solution)/shard_map/all_to_all | solution.py:319
  415.0 19.7 %all-to-all-start.9 = ((bf16[8,64,1024]{2,1,0:T(8,128)(2,1)}), bf16[8,64,1024]{2,1,0:T(8,128)(2,1)}, u32[]{:S(2)}, u32[]{:S(2)}) async-start(bf16[8,64,1024]{2,1,0:T(8,128)(2,1)} %bitcast.328), calls=%async_computation.9 | async-start | bytes 2097152 | tf_op jit(solution)/shard_map/all_to_all | solution.py:319
  439.6 19.7 %all-to-all-start.11 = ((bf16[8,64,1024]{2,1,0:T(8,128)(2,1)}), bf16[8,64,1024]{2,1,0:T(8,128)(2,1)}, u32[]{:S(2)}, u32[]{:S(2)}) async-start(bf16[8,64,1024]{2,1,0:T(8,128)(2,1)} %tile.26), calls=%async_computation.11 | async-start | bytes 2097152 | tf_op jit(solution)/shard_map/all_to_all | solution.py:311
  468.8 19.7 %all-to-all-start.12 = ((bf16[8,64,1024]{2,1,0:T(8,128)(2,1)}), bf16[8,64,1024]{2,1,0:T(8,128)(2,1)}, u32[]{:S(2)}, u32[]{:S(2)}) async-start(bf16[8,64,1024]{2,1,0:T(8,128)(2,1)} %bitcast.310), calls=%async_computation.12 | async-start | bytes 2097152 | tf_op jit(solution)/shard_map/all_to_all | solution.py:319
  611.4 13.6 %all-to-all-start.13 = ((f32[8,8,2176]{2,1,0:T(8,128)}), f32[8,8,2176]{2,1,0:T(8,128)S(1)}, u32[]{:S(2)}, u32[]{:S(2)}) async-start(f32[8,8,2176]{2,1,0:T(8,128)} %pad_maximum_fusion), calls=%async_computation.13 | async-start | bytes 1114112 | tf_op jit(solution)/shard_map/all_to_all | solution.py:319
  625.0 6.3 collective-permute-start.39
  625.1 7.2 %collective-permute-start.40 = (f32[8,2176]{1,0:T(8,128)S(1)}, f32[8,2176]{1,0:T(8,128)S(1)}, u32[]{:S(2)}, u32[]{:S(2)}) collective-permute-start(f32[8,2176]{1,0:T(8,128)S(1)} %reduce_sum.363), channel_id=1, source_target_pairs={{0,16},{8,24},{16,0},{24,8},{1,17},{9,25},{17,1},{25,9},{2,18},{10... | collective-permute-start | bytes 208904 | tf_op jit(solution)/shard_map/ppermute | solution.py:370
  633.9 13.7 %all-to-all-start.14 = ((f32[8,8,2176]{2,1,0:T(8,128)}), f32[8,8,2176]{2,1,0:T(8,128)S(1)}, u32[]{:S(2)}, u32[]{:S(2)}) async-start(f32[8,8,2176]{2,1,0:T(8,128)} %tile.29), calls=%async_computation.14 | async-start | bytes 1114112 | tf_op jit(solution)/shard_map/all_to_all | solution.py:311
  (148 other events, 1624.7 us)

commit v2 on v1

v2 whole, which is shorter than its diff:
```python
import math
from functools import partial
from typing import NamedTuple

import jax
import jax.numpy as jnp
from jax import lax
from jax.experimental import pallas as pl
from jax.experimental.pallas import tpu as pltpu
from jax.sharding import PartitionSpec as P

MODEL_WIDTH = 1024
H = 16
HD = 64
HIDDEN_UNITS = 4096
ADAPTER_RANK = 4


ADAPTER_SCALE = 8.0
EPS_NORM = 1e-05
BETA_ONE = 0.9
BETA_TWO = 0.999
RATE = 0.02
DECAY = 0.01
EPS_ADAM = 1e-08
CLIP = 0.02
NEGATIVE = -1e30


def product_plain(left, right):
    return jnp.dot(left, right, preferred_element_type=jnp.float32)


def product_left_transposed(left, right):
    return lax.dot_general(
        left, right, (((0,), (0,)), ((), ())), preferred_element_type=jnp.float32
    )


def product_right_transposed(left, right):
    return lax.dot_general(
        left, right, (((1,), (1,)), ((), ())), preferred_element_type=jnp.float32
    )


def norm_fwd(hidden_rows, norm_gain, norm_shift):
    row_mean = jnp.mean(hidden_rows, axis=-1, keepdims=True)
    centered = hidden_rows - row_mean
    inverse_deviation = lax.rsqrt(jnp.mean(centered * centered, axis=-1, keepdims=True) + EPS_NORM)
    normalized_rows = centered * inverse_deviation
    return (normalized_rows * norm_gain + norm_shift, normalized_rows, inverse_deviation)


def norm_backward(gradient_value, normalized_rows, inverse_deviation, norm_gain):
    scaled_rows = gradient_value * norm_gain
    return inverse_deviation * (
        scaled_rows
        - jnp.mean(scaled_rows, axis=-1, keepdims=True)
        - normalized_rows * jnp.mean(scaled_rows * normalized_rows, axis=-1, keepdims=True)
    )


def moment_update(weight, first, second, gradient_value, scale_factor, step_number):
    clipped = gradient_value * scale_factor
    first_new = BETA_ONE * first + (1.0 - BETA_ONE) * clipped
    second_new = BETA_TWO * second + (1.0 - BETA_TWO) * clipped * clipped
    first_hat = first_new / (1.0 - BETA_ONE**step_number)
    second_hat = second_new / (1.0 - BETA_TWO**step_number)
    weight_new = weight - RATE * (first_hat / (jnp.sqrt(second_hat) + EPS_ADAM) + DECAY * weight)
    return (weight_new, first_new, second_new)


CAPACITY = 80


LANES = 16
HALF_TILE = 512
BLOCK = 1024
VMEM_BYTES = 63 * 2**20


def whole(array, *lead):
    shape = (None,) * len(lead) + array.shape[len(lead) :]
    place = lead + (0,) * (array.ndim - len(lead))
    return array, pl.BlockSpec(shape, lambda *_: place, pipeline_mode=pl.Buffered(1))


def strip(array, width, column, *lead):
    shape = (None,) * len(lead) + (array.shape[-2], width)
    if callable(column):
        return array, pl.BlockSpec(shape, lambda j, *_: lead + (0, column(j)))
    place = lead + (0, column)
    return array, pl.BlockSpec(shape, lambda *_: place, pipeline_mode=pl.Buffered(1))


def rows_strip(array, height, row, *lead):
    shape = (None,) * len(lead) + (height, array.shape[-1])
    return array, pl.BlockSpec(shape, lambda j, *_: lead + (row(j), 0))


def result(shape, dtype, block=None, place=None):
    kind = jax.ShapeDtypeStruct(shape, dtype)
    if block is None:
        block, zeros = shape, (0,) * len(shape)
        return kind, pl.BlockSpec(block, lambda *_: zeros)
    return kind, pl.BlockSpec(block, place)


def launch(kernel, grid, operands, results, scratch=(), scalars=(), flops=0):
    moved = sum(a.size * a.dtype.itemsize for a, _ in operands)
    return pl.pallas_call(
        kernel,
        out_shape=[kind for kind, _ in results],
        grid_spec=pltpu.PrefetchScalarGridSpec(
            num_scalar_prefetch=len(scalars),
            grid=grid,
            in_specs=[spec for _, spec in operands],
            out_specs=[spec for _, spec in results],
            scratch_shapes=list(scratch),
        ),
        compiler_params=pltpu.CompilerParams(vmem_limit_bytes=VMEM_BYTES),
        cost_estimate=pl.CostEstimate(flops=flops, bytes_accessed=moved, transcendentals=0),
    )(*scalars, *(a for a, _ in operands))


class Unit(NamedTuple):
    places: tuple
    arrays: tuple
    rows: int

    def operands(self):
        return [(array, pl.BlockSpec(memory_space=pltpu.HBM)) for array in self.arrays]


def shard_of(place):
    if isinstance(place, int):
        return place
    me = lax.axis_index("fsdp")
    return jnp.bitwise_xor(me, jnp.where(lax.rem(me, 2) == 0, *place))


def moves(unit, refs, target, sems, column, width):
    columns = pl.ds(pl.multiple_of(column * width, width), width)
    copies = []
    for n, (place, ref) in enumerate(zip(unit.places, refs)):
        start = pl.multiple_of(shard_of(place) * unit.rows, 16)
        copies.append(
            pltpu.make_async_copy(
                ref.at[:, columns], target.at[pl.ds(start, ref.shape[0]), :], sems.at[n]
            )
        )
    return copies


def begin(copies):
    for copy in copies:
        copy.start()


def finish(copies):
    for copy in copies:
        copy.wait()


def next_strip(unit, refs, slots, sems, width):
    j = pl.program_id(0)

    def strip_moves(step):
        slot = lax.rem(step, 2)
        return moves(unit, refs, slots.at[slot], sems.at[slot], step, width)

    pl.when(j == 0)(lambda: begin(strip_moves(j)))
    pl.when(j + 1 < pl.num_programs(0))(lambda: begin(strip_moves(j + 1)))
    finish(strip_moves(j))
    return slots.at[lax.rem(j, 2)]


def slots_for(unit, height, width):
    return [
        pltpu.VMEM((2, height, width), jnp.bfloat16),
        pltpu.SemaphoreType.DMA((2, len(unit.arrays))),
    ]


def one_slot_for(unit):
    return [
        pltpu.VMEM((MODEL_WIDTH, BLOCK), jnp.bfloat16),
        pltpu.SemaphoreType.DMA((len(unit.arrays),)),
    ]


def taken(refs, *units):
    groups = []
    for unit in units:
        groups.append(refs[: len(unit.arrays)])
        refs = refs[len(unit.arrays) :]
    return groups + [refs]


def over_rows(total, size, work):
    def turn(i, carry):
        work(pl.ds(pl.multiple_of(i * size, size), size))
        return carry

    lax.fori_loop(0, total // size, turn, 0)


def low(value):
    return value.astype(jnp.bfloat16)


def adapter(inner, up):
    return ADAPTER_SCALE * product_plain(inner, up)


def norm_into(out_ref, rows_ref, gain, shift):
    def part(rows):
        out_ref[rows, :] = low(norm_fwd(rows_ref[rows, :], gain, shift)[0])

    over_rows(rows_ref.shape[0], min(64, rows_ref.shape[0]), part)


def norm_back_into(out_ref, gradient_ref, rows_ref, gain, residual_ref=None):
    def part(rows):
        _, normalized, deviation = norm_fwd(rows_ref[rows, :], gain, 0.0)
        value = norm_backward(gradient_ref[rows, :], normalized, deviation, gain)
        if residual_ref is not None:
            value = value + residual_ref[rows, :]
        out_ref[rows, :] = value

    over_rows(rows_ref.shape[0], min(64, rows_ref.shape[0]), part)


def front_kernel(unit, *refs):
    pieces, refs = taken(refs, unit)
    x, gain, shift, bias, down, up, qkv, a, ua, slots, sems = refs
    weight = next_strip(unit, pieces, slots, sems, BLOCK)

    @pl.when(pl.program_id(0) == 0)
    def _():
        norm_into(a, x, gain[...], shift[...])
        ua[...] = low(product_right_transposed(a[...], down[...]))

    qkv[...] = low(product_plain(a[...], weight[...]) + bias[...] + adapter(ua[...], up[...]))


def front(x, unit, p, layer):
    tokens = x.shape[0]
    return launch(
        partial(front_kernel, unit),
        (3,),
        unit.operands()
        + [
            whole(x),
            strip(p["small"], BLOCK, 9, layer),
            strip(p["small"], BLOCK, 10, layer),
            strip(p["small"], BLOCK, lambda j: j, layer),
            whole(p["down_t"], layer, 0),
            strip(p["up"], BLOCK, lambda j: j, layer),
        ],
        [
            result((tokens, 3 * MODEL_WIDTH), jnp.bfloat16, (tokens, BLOCK), lambda j: (0, j)),
            result((tokens, MODEL_WIDTH), jnp.bfloat16),
            result((tokens, LANES), jnp.bfloat16),
        ],
        scratch=slots_for(unit, MODEL_WIDTH, BLOCK),
        flops=6 * tokens * MODEL_WIDTH**2,
    )


def pick_rows(index, source, target):
    def turn(i, carry):
        target[pl.ds(i, 1), :] = source[pl.ds(index[i], 1), :]
        return carry

    lax.fori_loop(0, target.shape[0], turn, 0)


def add_rows(index, source, target):
    def turn(i, carry):
        rows = pl.ds(index[i], 1)
        target[rows, :] = target[rows, :] + source[pl.ds(i, 1), :]
        return carry

    lax.fori_loop(0, source.shape[0], turn, 0)


def front_last_kernel(unit, index, *refs):
    pieces, refs = taken(refs, unit)
    x, gain, shift, bias, down, up, q, kv, a, a_sel, ua, ua_sel, x_sel, slots, sems = refs
    j = pl.program_id(0)
    weight = next_strip(unit, pieces, slots, sems, BLOCK)

    @pl.when(j == 0)
    def _():
        norm_into(a, x, gain[...], shift[...])
        ua[...] = low(product_right_transposed(a[...], down[...]))
        pick_rows(index, x, x_sel)
        norm_into(a_sel, x_sel, gain[...], shift[...])
        ua_sel[...] = low(product_right_transposed(a_sel[...], down[...]))

    @pl.when(j == 0)
    def _():
        q[...] = low(
            product_plain(a_sel[...], weight[...]) + bias[...] + adapter(ua_sel[...], up[...])
        )

    @pl.when(j > 0)
    def _():
        kv[...] = low(product_plain(a[...], weight[...]) + bias[...] + adapter(ua[...], up[...]))


def front_last(index, x, unit, p, layer):
    tokens, count = x.shape[0], index.shape[0]
    return launch(
        partial(front_last_kernel, unit),
        (3,),
        unit.operands()
        + [
            whole(x),
            strip(p["small"], BLOCK, 9, layer),
            strip(p["small"], BLOCK, 10, layer),
            strip(p["small"], BLOCK, lambda j: j, layer),
            whole(p["down_t"], layer, 0),
            strip(p["up"], BLOCK, lambda j: j, layer),
        ],
        [
            result((count, MODEL_WIDTH), jnp.bfloat16),
            result(
                (tokens, 2 * MODEL_WIDTH),
                jnp.bfloat16,
                (tokens, BLOCK),
                lambda j, *_: (0, jnp.maximum(j - 1, 0)),
            ),
            result((tokens, MODEL_WIDTH), jnp.bfloat16),
            result((count, MODEL_WIDTH), jnp.bfloat16),
            result((tokens, LANES), jnp.bfloat16),
            result((count, LANES), jnp.bfloat16),
            result((count, MODEL_WIDTH), jnp.float32),
        ],
        scratch=slots_for(unit, MODEL_WIDTH, BLOCK),
        scalars=(index,),
        flops=4 * tokens * MODEL_WIDTH**2,
    )


def attend_kernel(lengths, slots, query, key, value, out):
    length = lengths[pl.program_id(0)]
    kpos = lax.broadcasted_iota(jnp.int32, (query.shape[0], key.shape[0]), 1)
    allowed = (kpos <= slots[...]) & (kpos < length)
    heads = []
    for start in range(0, query.shape[1], HD):
        part = slice(start, start + HD)
        raw = product_right_transposed(query[:, part], key[:, part]) * HD ** (-0.5)
        raw = jnp.where(allowed, raw, NEGATIVE)
        prob = jnp.exp(raw - jnp.max(raw, axis=1, keepdims=True))
        prob = prob * (1.0 / jnp.sum(prob, axis=1, keepdims=True))
        heads.append(product_plain(low(prob), value[:, part]))
    out[...] = low(jnp.concatenate(heads, axis=1))


def own_lanes(count, heads):
    shape = (heads * count, heads * HD)
    row = lax.broadcasted_iota(jnp.int32, shape, 0) // count
    lane = lax.broadcasted_iota(jnp.int32, shape, 1) // HD
    return row == lane


def stacked_heads(rows, own):
    heads = own.shape[0] // rows.shape[0]
    tall = jnp.concatenate([rows.astype(jnp.float32)] * heads, axis=0)
    return low(jnp.where(own, tall, 0.0))


def own_heads(tall, own, count):
    tall = jnp.where(own, tall, 0.0)
    total = tall[:count]
    for start in range(count, tall.shape[0], count):
        total = total + tall[start : start + count]
    return total


def few_scores(length, slots, tall, key):
    raw = product_right_transposed(tall, key[...]) * HD ** (-0.5)
    kpos = lax.broadcasted_iota(jnp.int32, raw.shape, 1)
    places = jnp.concatenate([slots[...]] * (raw.shape[0] // slots.shape[0]), axis=0)
    raw = jnp.where((kpos <= places) & (kpos < length), raw, NEGATIVE)
    prob = jnp.exp(raw - jnp.max(raw, axis=1, keepdims=True))
    return prob * (1.0 / jnp.sum(prob, axis=1, keepdims=True))


def attend_few_kernel(lengths, slots, query, key, value, out):
    count = query.shape[0]
    own = own_lanes(count, query.shape[1] // HD)
    prob = few_scores(lengths[pl.program_id(0)], slots, stacked_heads(query[...], own), key)
    out[...] = low(own_heads(product_plain(low(prob), value[...]), own, count))


def attend_few_back_kernel(lengths, slots, query, key, value, d_out, d_query, d_key, d_value):
    count = query.shape[0]
    own = own_lanes(count, query.shape[1] // HD)
    tall = stacked_heads(query[...], own)
    d_tall = stacked_heads(d_out[...], own)
    prob = few_scores(lengths[pl.program_id(0)], slots, tall, key)
    d_prob = product_right_transposed(d_tall, value[...])
    d_raw = low(prob * (d_prob - jnp.sum(prob * d_prob, axis=1, keepdims=True)))
    d_value[...] = low(product_left_transposed(low(prob), d_tall))
    d_key[...] = low(product_left_transposed(d_raw, tall) * HD ** (-0.5))
    d_query[...] = low(own_heads(product_plain(d_raw, key[...]), own, count) * HD ** (-0.5))


def head_blocks(array, height, third, steps):
    offset = third * steps
    return array, pl.BlockSpec((height, MODEL_WIDTH // steps), lambda r, h, *_: (r, offset + h))


def head_steps(count):
    return 2 if count > 128 else 1


def attend(lengths, slots, query, key, value):
    rows, count = slots.shape
    seq = key[0].shape[0] // rows
    steps = head_steps(count)
    column = slots.reshape(-1, 1)
    (out,) = launch(
        attend_kernel if steps > 1 else attend_few_kernel,
        (rows, steps),
        [
            (column, pl.BlockSpec((count, 1), lambda r, h, *_: (r, 0))),
            head_blocks(query[0], count, query[1], steps),
            head_blocks(key[0], seq, key[1], steps),
            head_blocks(value[0], seq, value[1], steps),
        ],
        [
            result(
                (rows * count, MODEL_WIDTH),
                jnp.bfloat16,
                (count, MODEL_WIDTH // steps),
                lambda r, h, *_: (r, h),
            )
        ],
        scalars=(lengths,),
        flops=4 * rows * count * seq * MODEL_WIDTH,
    )
    return out


def attend_back_kernel(lengths, slots, query, key, value, d_out, d_query, d_key, d_value):
    length = lengths[pl.program_id(0)]
    kpos = lax.broadcasted_iota(jnp.int32, (key.shape[0], query.shape[0]), 0)
    allowed = (kpos <= slots[...]) & (kpos < length)
    parts = []
    for start in range(0, query.shape[1], HD):
        part = slice(start, start + HD)
        q, k, v, d_o = query[:, part], key[:, part], value[:, part], d_out[:, part]
        raw = product_right_transposed(k, q) * HD ** (-0.5)
        raw = jnp.where(allowed, raw, NEGATIVE)
        prob = jnp.exp(raw - jnp.max(raw, axis=0, keepdims=True))
        prob = prob * (1.0 / jnp.sum(prob, axis=0, keepdims=True))
        d_prob = product_right_transposed(v, d_o)
        d_raw = low(prob * (d_prob - jnp.sum(prob * d_prob, axis=0, keepdims=True)))
        parts.append(
            (
                product_left_transposed(d_raw, k) * HD ** (-0.5),
                product_plain(d_raw, q) * HD ** (-0.5),
                product_plain(low(prob), d_o),
            )
        )
    for n, ref in enumerate((d_query, d_key, d_value)):
        ref[...] = low(jnp.concatenate([part[n] for part in parts], axis=1))


def attend_back(lengths, slots, query, key, value, d_out):
    rows, count = slots.shape
    seq = key[0].shape[0] // rows
    steps = head_steps(count)
    heights = (count, seq, seq)
    return launch(
        attend_back_kernel if steps > 1 else attend_few_back_kernel,
        (rows, steps),
        [
            (
                slots.reshape(rows, 1, count),
                pl.BlockSpec((None, 1, count), lambda r, h, *_: (r, 0, 0)),
            )
            if steps > 1
            else (slots.reshape(-1, 1), pl.BlockSpec((count, 1), lambda r, h, *_: (r, 0))),
            head_blocks(query[0], count, query[1], steps),
            head_blocks(key[0], seq, key[1], steps),
            head_blocks(value[0], seq, value[1], steps),
            head_blocks(d_out, count, 0, steps),
        ],
        [
            result(
                (rows * height, MODEL_WIDTH),
                jnp.bfloat16,
                (height, MODEL_WIDTH // steps),
                lambda r, h, *_: (r, h),
            )
            for height in heights
        ],
        scalars=(lengths,),
        flops=10 * rows * count * seq * MODEL_WIDTH,
    )


def gelu_parts(value):
    root = 0.7978845608028654
    square = value * value
    bend = jnp.tanh(root * value * (1.0 + 0.044715 * square))
    half = 0.5 * (1.0 + bend)
    slope = half + 0.5 * value * (1.0 - bend * bend) * root * (1.0 + 3 * 0.044715 * square)
    return value * half, slope


def middle_into(x2, uo, x, o, w_o, c_o, d_o, u_o):
    uo[...] = low(product_right_transposed(o[...], d_o[...]))
    x2[...] = x[...] + (
        product_plain(o[...], w_o[...]) + c_o[...] + adapter(uo[...], u_o[...])
    )


FIRST_FEED = 4 * MODEL_WIDTH // BLOCK
FEED_STEPS = HIDDEN_UNITS // BLOCK
PIECES = 8
CHUNK = BLOCK // PIECES


def chunk_place(unit):
    part, rest = unit // (CHUNK * FEED_STEPS), unit % (CHUNK * FEED_STEPS)
    return pl.ds(pl.multiple_of(rest // CHUNK * BLOCK + part * CHUNK, CHUNK), CHUNK)


def chunked(part):
    return jnp.concatenate(jnp.split(part, FEED_STEPS), axis=1)


def feed_step(j):
    return jnp.minimum(j, FEED_STEPS - 1)


def late_step(j):
    return jnp.maximum(j - FEED_STEPS, 0)


def feed_in_kernel(unit, unit_fc, *refs):
    pieces, pieces_fc, refs = taken(refs, unit, unit_fc)
    x, o, c_o, d_o, u_o, gain, shift, c_fc, d_fc, u_fc = refs[:10]
    x2, uo, m, um, act, slope, weight_o, sems_o, slots, sems, pre = refs[10:]
    first = moves(unit, pieces, weight_o, sems_o, 3, BLOCK)
    pl.when(pl.program_id(0) == 0)(lambda: begin(first))
    weight = next_strip(unit_fc, pieces_fc, slots, sems, BLOCK)

    @pl.when(pl.program_id(0) == 0)
    def _():
        finish(first)
        middle_into(x2, uo, x, o, weight_o, c_o, d_o, u_o)
        norm_into(m, x2, gain[...], shift[...])
        um[...] = low(product_right_transposed(m[...], d_fc[...]))

    pre[...] = product_plain(m[...], weight[...]) + c_fc[...] + adapter(um[...], u_fc[...])
    j = pl.program_id(0)

    def part(rows):
        first, second = gelu_parts(pre[rows, :])
        slope[rows, :] = low(second)
        first = low(first)
        for start in range(0, BLOCK, CHUNK):
            act[rows, chunk_place(j * BLOCK + start)] = first[:, start : start + CHUNK]

    over_rows(pre.shape[0], 16, part)


def feed_in(x, o, unit, unit_fc, p, layer):
    tokens = x.shape[0]
    small, up = p["small"], p["up"]
    wide = (tokens, HIDDEN_UNITS), jnp.bfloat16, (tokens, BLOCK), lambda j: (0, j)
    return launch(
        partial(feed_in_kernel, unit, unit_fc),
        (FEED_STEPS,),
        unit.operands()
        + unit_fc.operands()
        + [
            whole(x),
            whole(o),
            strip(small, BLOCK, 3, layer),
            whole(p["down_t"], layer, 1),
            strip(up, BLOCK, 3, layer),
            strip(small, BLOCK, 11, layer),
            strip(small, BLOCK, 12, layer),
            strip(small, BLOCK, lambda j: FIRST_FEED + j, layer),
            whole(p["down_t"], layer, 2),
            strip(up, BLOCK, lambda j: FIRST_FEED + j, layer),
        ],
        [
            result((tokens, MODEL_WIDTH), jnp.float32),
            result((tokens, LANES), jnp.bfloat16),
            result((tokens, MODEL_WIDTH), jnp.bfloat16),
            result((tokens, LANES), jnp.bfloat16),
            result((tokens, HIDDEN_UNITS), jnp.bfloat16),
            result(*wide),
        ],
        scratch=one_slot_for(unit)
        + slots_for(unit_fc, MODEL_WIDTH, BLOCK)
        + [pltpu.VMEM((tokens, BLOCK), jnp.float32)],
        flops=2 * tokens * MODEL_WIDTH * (MODEL_WIDTH + HIDDEN_UNITS),
    )


def feed_out_kernel(unit_fp, *refs):
    pieces_fp, refs = taken(refs, unit_fp)
    x2, act, d_fp, c_fp, u_fp, final, x3, ug, h, slots, sems = refs
    j = pl.program_id(0)
    weight = next_strip(unit_fp, pieces_fp, slots, sems, BLOCK)

    @pl.when(j == 0)
    def _():
        ug[...] = jnp.zeros_like(ug)
        x3[...] = x2[...] + c_fp[...]

    columns = pl.ds(pl.multiple_of(j * BLOCK, BLOCK), BLOCK)
    taken_act = act[:, columns]
    x3[...] += product_plain(taken_act, weight[...])
    maps = [
        d_fp[:, pl.ds(pl.multiple_of((n * FEED_STEPS + j) * CHUNK, CHUNK), CHUNK)]
        for n in range(PIECES)
    ]
    ug[...] += product_right_transposed(taken_act, jnp.concatenate(maps, axis=1))

    @pl.when(j == pl.num_programs(0) - 1)
    def _():
        x3[...] += adapter(low(ug[...]), u_fp[...])
        gains = final[...].astype(jnp.float32)
        if h.shape == x3.shape:
            norm_into(h, x3, gains[0:1], gains[1:2])


def feed_out(x2, act, unit_fp, final, p, layer, with_norm):
    tokens = x2.shape[0]
    return launch(
        partial(feed_out_kernel, unit_fp),
        (FEED_STEPS,),
        unit_fp.operands()
        + [
            whole(x2),
            whole(act),
            whole(p["feed_t"], layer),
            strip(p["small"], BLOCK, 8, layer),
            strip(p["up"], BLOCK, 8, layer),
            whole(final),
        ],
        [
            result((tokens, MODEL_WIDTH), jnp.float32),
            result((tokens, LANES), jnp.float32),
            result((tokens if with_norm else 16, MODEL_WIDTH), jnp.bfloat16),
        ],
        scratch=slots_for(unit_fp, BLOCK, MODEL_WIDTH),
        flops=2 * tokens * MODEL_WIDTH * HIDDEN_UNITS,
    )


def three_parts(value):
    first = low(value)
    rest = value - first.astype(jnp.float32)
    second = low(rest)
    return [first, second, low(rest - second.astype(jnp.float32))]


def head_kernel(h, table, out, logits, total, top, bulk):
    j = pl.program_id(0)

    @pl.when(j == 0)
    def _():
        top[...] = jnp.full_like(top, NEGATIVE)
        bulk[...] = jnp.zeros_like(bulk)
        total[...] = jnp.zeros_like(total)

    def part(rows):
        logits[...] = product_right_transposed(h[rows, :], table[...])
        before = top[rows, :]
        now = jnp.maximum(before, jnp.max(logits[...], axis=1, keepdims=True))
        fade = jnp.exp(before - now)
        top[rows, :] = now
        weight = jnp.exp(logits[...] - now)
        bulk[rows, :] = bulk[rows, :] * fade + jnp.sum(weight, axis=1, keepdims=True)
        total[rows, :] = total[rows, :] * fade + product_plain(low(weight), table[...])

    over_rows(h.shape[0], logits.shape[0], part)

    @pl.when(j == pl.num_programs(0) - 1)
    def _():
        out[:, :MODEL_WIDTH] = low(total[...])
        columns = three_parts(top[...]) + three_parts(bulk[...])
        rest = jnp.zeros((h.shape[0], 128 - len(columns)), jnp.bfloat16)
        out[:, MODEL_WIDTH:] = jnp.concatenate(columns + [rest], axis=1)


def head(h, table):
    tokens, vocab = h.shape[0], table.shape[0]
    steps = 3 if vocab % 48 == 0 else 1
    tile = vocab // steps
    chunk = 256
    (out,) = launch(
        head_kernel,
        (steps,),
        [whole(h), rows_strip(table, tile, lambda j: j)],
        [result((tokens, MODEL_WIDTH + 128), jnp.bfloat16)],
        scratch=[
            pltpu.VMEM((chunk, tile), jnp.float32),
            pltpu.VMEM((tokens, MODEL_WIDTH), jnp.float32),
            pltpu.VMEM((tokens, 1), jnp.float32),
            pltpu.VMEM((tokens, 1), jnp.float32),
        ],
        flops=4 * tokens * vocab * MODEL_WIDTH,
    )
    return out


def head_back_kernel(parts, targets, h, x3, final, mask, terms, d_x3, d_hidden):
    tails = [
        parts[n, :, MODEL_WIDTH:].astype(jnp.float32) for n in range(parts.shape[0])
    ]
    tops = [tail[:, 0:1] + tail[:, 1:2] + tail[:, 2:3] for tail in tails]
    sums = [tail[:, 3:4] + tail[:, 4:5] + tail[:, 5:6] for tail in tails]
    top = tops[0]
    for other in tops[1:]:
        top = jnp.maximum(top, other)
    whole_sum = sum(s * jnp.exp(t - top) for t, s in zip(tops, sums))
    lse = top + jnp.log(whole_sum)
    wanted = targets[...]
    logit = jnp.sum(h[...].astype(jnp.float32) * wanted, axis=1, keepdims=True)
    terms[...] = (lse - logit) * mask[...]
    gathered = -wanted
    for n, t in enumerate(tops):
        gathered = gathered + parts[n, :, :MODEL_WIDTH].astype(jnp.float32) * jnp.exp(t - lse)
    d_hidden[...] = gathered * mask[...]
    norm_back_into(d_x3, d_hidden, x3, final[...].astype(jnp.float32)[0:1])


def head_back(parts, targets, h, x3, final, mask):
    count = h.shape[0]
    return launch(
        head_back_kernel,
        (1,),
        [whole(parts), whole(targets), whole(h), whole(x3), whole(final), whole(mask)],
        [
            result((count, 1), jnp.float32),
            result((count, MODEL_WIDTH), jnp.float32),
        ],
        scratch=[pltpu.VMEM((count, MODEL_WIDTH), jnp.float32)],
    )


def output_back(d_heads, grad_uo, grad_do, d_x2, o, uo, w_o, u_o, d_o):
    d_low = low(d_x2[...])
    grad_uo[...] = ADAPTER_SCALE * product_left_transposed(uo[...], d_low)
    duo = low(ADAPTER_SCALE * product_right_transposed(d_low, u_o[...]))
    grad_do[...] = product_left_transposed(duo, o[...])
    d_heads[...] = low(
        product_right_transposed(d_low, w_o[...]) + product_plain(duo, d_o[...])
    )


def front_last_back_kernel(unit, index, *refs):
    pieces, refs = taken(refs, unit)
    d_query, d_key, d_value, a, a_sel, ua, ua_sel, up, down, d_x2, x, gain = refs[:12]
    d_x, grad_up, grad_down, rows, rows_sel, inner, inner_sel, slots, sems = refs[12:]
    j = pl.program_id(0)
    weight = next_strip(unit, pieces, slots, sems, BLOCK)

    @pl.when(j == 0)
    def _():
        rows[...] = jnp.zeros_like(rows)
        inner[...] = jnp.zeros_like(inner)

    @pl.when(j == 0)
    def _():
        gradient = d_query[...]
        grad_up[...] = ADAPTER_SCALE * product_left_transposed(ua_sel[...], gradient)
        inner_sel[...] = ADAPTER_SCALE * product_right_transposed(gradient, up[...])
        rows_sel[...] = product_right_transposed(gradient, weight[...])

    def step(ref):
        gradient = ref[...]
        grad_up[...] = ADAPTER_SCALE * product_left_transposed(ua[...], gradient)
        inner[...] += ADAPTER_SCALE * product_right_transposed(gradient, up[...])
        rows[...] += product_right_transposed(gradient, weight[...])

    pl.when(j == 1)(lambda: step(d_key))
    pl.when(j == 2)(lambda: step(d_value))

    @pl.when(j == pl.num_programs(0) - 1)
    def _():
        last, last_sel = low(inner[...]), low(inner_sel[...])
        grad_down[...] = product_left_transposed(last, a[...]) + product_left_transposed(
            last_sel, a_sel[...]
        )
        rows[...] += product_plain(last, down[...])
        rows_sel[...] += product_plain(last_sel, down[...])
        add_rows(index, rows_sel, rows)
        norm_back_into(d_x, rows, x, gain[...])
        add_rows(index, d_x2, d_x)


def front_last_back(index, d_query, d_key, d_value, saved, d_x2, x, unit, p, layer):
    a, a_sel, ua, ua_sel = saved
    tokens, count = x.shape[0], index.shape[0]
    return launch(
        partial(front_last_back_kernel, unit),
        (3,),
        unit.operands()
        + [
            whole(d_query),
            whole(d_key),
            whole(d_value),
            whole(a),
            whole(a_sel),
            whole(ua),
            whole(ua_sel),
            strip(p["up"], BLOCK, lambda j: j, layer),
            whole(p["down_t"], layer, 0),
            whole(d_x2),
            whole(x),
            strip(p["small"], BLOCK, 9, layer),
        ],
        [
            result((tokens, MODEL_WIDTH), jnp.float32),
            result((LANES, 3 * MODEL_WIDTH), jnp.float32, (LANES, BLOCK), lambda j, *_: (0, j)),
            result((LANES, MODEL_WIDTH), jnp.float32),
        ],
        scratch=[
            pltpu.VMEM((tokens, MODEL_WIDTH), jnp.float32),
            pltpu.VMEM((count, MODEL_WIDTH), jnp.float32),
            pltpu.VMEM((tokens, LANES), jnp.float32),
            pltpu.VMEM((count, LANES), jnp.float32),
        ]
        + slots_for(unit, MODEL_WIDTH, BLOCK),
        scalars=(index,),
        flops=4 * tokens * MODEL_WIDTH**2,
    )


def feed_back_kernel(unit, unit_fc, unit_fp, *refs):
    pieces, pieces_fc, pieces_fp, refs = taken(refs, unit, unit_fc, unit_fp)
    d_x3, x2, m, um, ug, uo, o, act, slope, d_fp, u_fc, u_fp, d_fc, gain, u_o, d_o = refs[:16]
    d_x2, d_heads, grad_ufp, grad_dfp, grad_ufc, grad_dfc, grad_uo, grad_do = refs[16:24]
    d_out, dug, d_pre, inner, d_feed, weight_o, sems_o, slots, sems = refs[24:]
    j = pl.program_id(0)
    last = pl.num_programs(0) - 1
    out_moves = moves(unit, pieces, weight_o, sems_o, 3, BLOCK)

    def each(step, act):
        slot = lax.rem(step, 2)
        for some, refs, first in ((unit_fp, pieces_fp, 0), (unit_fc, pieces_fc, FEED_STEPS)):

            @pl.when((step >= first) & (step < first + FEED_STEPS))
            def _(some=some, refs=refs, first=first):
                column = jnp.clip(step - first, 0, FEED_STEPS - 1)
                act(moves(some, refs, slots.at[slot], sems.at[slot], column, BLOCK))

    pl.when(j == 0)(lambda: each(j, begin))
    pl.when(j < last)(lambda: each(j + 1, begin))
    pl.when(j == last)(lambda: begin(out_moves))

    @pl.when(j == 0)
    def _():
        d_out[...] = low(d_x3[...])
        dug[...] = low(ADAPTER_SCALE * product_right_transposed(d_out[...], u_fp[...]))
        grad_ufp[...] = ADAPTER_SCALE * product_left_transposed(low(ug[...]), d_out[...])
        inner[...] = jnp.zeros_like(inner)
        d_feed[...] = jnp.zeros_like(d_feed)

    each(j, finish)
    weight = slots.at[lax.rem(j, 2)]

    @pl.when(j < FEED_STEPS)
    def _():
        d_act = product_right_transposed(d_out[...], weight[...])
        from_act = product_left_transposed(dug[...], act[...])
        for n in range(PIECES):
            place = pl.ds(pl.multiple_of((n * FEED_STEPS + j) * CHUNK, CHUNK), CHUNK)
            part = slice(n * CHUNK, (n + 1) * CHUNK)
            value = d_act[:, part] + product_plain(dug[...], d_fp[:, place])
            d_pre[:, place] = low(value * slope[:, place].astype(jnp.float32))
            grad_dfp[:, place] = from_act[:, part]

    @pl.when(j >= FEED_STEPS)
    def _():
        columns = pl.ds(pl.multiple_of((j - FEED_STEPS) * BLOCK, BLOCK), BLOCK)
        gradient = d_pre[:, columns]
        grad_ufc[...] = ADAPTER_SCALE * product_left_transposed(um[...], gradient)
        inner[...] += ADAPTER_SCALE * product_right_transposed(gradient, u_fc[...])
        d_feed[...] += product_right_transposed(gradient, weight[...])

    @pl.when(j == last)
    def _():
        dum = low(inner[...])
        grad_dfc[...] = product_left_transposed(dum, m[...])
        d_feed[...] += product_plain(dum, d_fc[...])
        norm_back_into(d_x2, d_feed, x2, gain[...], d_x3)
        finish(out_moves)
        output_back(d_heads, grad_uo, grad_do, d_x2, o, uo, weight_o, u_o, d_o)


def feed_back(d_x3, saved, unit, unit_fc, unit_fp, p, layer):
    x2, m, um, ug, uo, o, act, slope = saved
    tokens = x2.shape[0]
    square = (LANES, MODEL_WIDTH), jnp.float32
    return launch(
        partial(feed_back_kernel, unit, unit_fc, unit_fp),
        (2 * FEED_STEPS,),
        unit.operands()
        + unit_fc.operands()
        + unit_fp.operands()
        + [
            whole(d_x3),
            whole(x2),
            whole(m),
            whole(um),
            whole(ug),
            whole(uo),
            whole(o),
            strip(act, BLOCK, feed_step),
            whole(slope),
            whole(p["feed_t"], layer),
            strip(p["up"], BLOCK, lambda j: FIRST_FEED + late_step(j), layer),
            strip(p["up"], BLOCK, 8, layer),
            whole(p["down_t"], layer, 2),
            strip(p["small"], BLOCK, 11, layer),
            strip(p["up"], BLOCK, 3, layer),
            whole(p["down_t"], layer, 1),
        ],
        [
            result((tokens, MODEL_WIDTH), jnp.float32),
            result((tokens, MODEL_WIDTH), jnp.bfloat16),
            result(*square),
            result((LANES, HIDDEN_UNITS), jnp.float32),
            result(
                (LANES, HIDDEN_UNITS), jnp.float32, (LANES, BLOCK), lambda j: (0, late_step(j))
            ),
            result(*square),
            result(*square),
            result(*square),
        ],
        scratch=[
            pltpu.VMEM((tokens, MODEL_WIDTH), jnp.bfloat16),
            pltpu.VMEM((tokens, LANES), jnp.bfloat16),
            pltpu.VMEM((tokens, HIDDEN_UNITS), jnp.bfloat16),
            pltpu.VMEM((tokens, LANES), jnp.float32),
            pltpu.VMEM((tokens, MODEL_WIDTH), jnp.float32),
        ]
        + one_slot_for(unit)
        + slots_for(unit_fc, MODEL_WIDTH, BLOCK),
        flops=2 * tokens * MODEL_WIDTH * (MODEL_WIDTH + 2 * HIDDEN_UNITS),
    )


def front_back_kernel(d_query, d_key, d_value, a, ua, up, grad_up, grad_down):
    inner = 0.0
    for n, ref in enumerate((d_query, d_key, d_value)):
        columns = slice(n * MODEL_WIDTH, (n + 1) * MODEL_WIDTH)
        grad_up[:, columns] = ADAPTER_SCALE * product_left_transposed(ua[...], ref[...])
        inner = inner + ADAPTER_SCALE * product_right_transposed(ref[...], up[:, columns])
    grad_down[...] = product_left_transposed(low(inner), a[...])


def front_back(d_query, d_key, d_value, a, ua, p, layer):
    return launch(
        front_back_kernel,
        (1,),
        [
            whole(d_query),
            whole(d_key),
            whole(d_value),
            whole(a),
            whole(ua),
            strip(p["up"], 3 * MODEL_WIDTH, 0, layer),
        ],
        [
            result((LANES, 3 * MODEL_WIDTH), jnp.float32),
            result((LANES, MODEL_WIDTH), jnp.float32),
        ],
    )


def pack_kernel(columns, *refs):
    extras, parts, out = refs[0], refs[1:-1], refs[-1]
    shards, width = out.shape[0], out.shape[2] - 128
    for n in range(shards):
        out[n, :, width:] = jnp.broadcast_to(extras[...], (out.shape[1], 128))
    for part, (row, start) in zip(parts, columns):
        values = part[0:ADAPTER_RANK, :]
        size = values.shape[1]
        done = 0
        while done < size:
            block, offset = divmod(start + done, width)
            step = min(width - offset, size - done)
            out[block, row : row + ADAPTER_RANK, offset : offset + step] = values[
                :, done : done + step
            ]
            done += step


def packed(by_layer, extras):
    shards = lax.axis_size("fsdp")
    columns, parts = [], []
    for layer, row in enumerate(by_layer):
        start = 0
        for part in row:
            parts.append(part)
            columns.append((layer * ADAPTER_RANK, start))
            start += part.shape[1]
    shape = (shards, len(by_layer) * ADAPTER_RANK, start // shards + 128)
    (out,) = launch(
        partial(pack_kernel, tuple(columns)),
        (1,),
        [whole(extras)] + [whole(part) for part in parts],
        [result(shape, jnp.float32)],
    )
    return out


def asking(table, ids, needed):
    shards = lax.axis_size("fsdp")
    total = ids.shape[0]
    order = jnp.arange(total, dtype=jnp.int32)
    owner = ids // table.shape[0]
    local = ids - owner * table.shape[0]
    same = (ids[:, None] == ids[None, :]) & needed[None, :]
    first = jnp.min(jnp.where(same, order[None, :], total), axis=1)
    leads = needed & (first == order)
    rank = jnp.sum(
        (leads & (owner[:, None] == owner[None, :]) & (order[None, :] < first[:, None])).astype(
            jnp.int32
        ),
        axis=1,
    )
    rounds = (jnp.max(jnp.where(needed, rank, 0)) + CAPACITY) // CAPACITY

    spots = jnp.arange(shards * CAPACITY, dtype=jnp.int32)

    def place_of(turn):
        return jnp.where(
            needed & (rank // CAPACITY == turn), owner * CAPACITY + rank % CAPACITY, -1
        )

    def ask(turn):
        place = place_of(turn)
        asked = jnp.sum(
            jnp.where(leads[:, None] & (place[:, None] == spots[None, :]), local[:, None], 0), axis=0
        )
        return asked.reshape(shards, CAPACITY)

    def sent_for(asked):
        return table.at[asked.reshape(-1)].get(mode="promise_in_bounds")

    def exchanged(part):
        return lax.all_to_all(part, "fsdp", 0, 0, tiled=True)

    def found(turn, back):
        pick = (place_of(turn)[:, None] == spots[None, :]).astype(jnp.bfloat16)
        return product_plain(pick, back)

    def later(first, most):
        def more(so_far):
            return lax.fori_loop(
                1,
                most,
                lambda turn, total: total
                + found(turn, exchanged(sent_for(exchanged(ask(turn))))),
                so_far,
            )

        return lax.cond(most > 1, more, lambda so_far: so_far, first)

    return ask, rounds, exchanged, sent_for, found, later


def as_low(numbers):
    return low(numbers // 256), low(numbers % 256)


def as_numbers(high, rest):
    return high.astype(jnp.int32) * 256 + rest.astype(jnp.int32)


def swap(part, bit):
    return lax.ppermute(part, "fsdp", [(i, i ^ bit) for i in range(lax.axis_size("fsdp"))])


def tie(parts, before):
    parts, _ = lax.optimization_barrier((parts, before))
    return parts


def hop(part):
    return lax.ppermute(
        part, "fsdp", [(i, i ^ (4 if i % 2 else 2)) for i in range(lax.axis_size("fsdp"))]
    )


class Gathering:
    PLACES = (0, 0), (1, 1), (2, 4), (3, 5), (5, 3), (4, 2), (7, 7), (6, 6)

    def __init__(self, shard, in_chunks=False):
        self.shard, self.in_chunks = shard, in_chunks
        self.direct = lax.axis_size("fsdp") == PIECES

    def begin(self, before=()):
        if self.direct:
            own = chunked(self.shard) if self.in_chunks else self.shard
            own = tie(own, before)
            other = swap(own, 1)
            self.arrays = own, other, hop(own), hop(other)

    def pass_on(self, value):
        if self.direct:
            own, other, first, second = self.arrays
            first, value = lax.optimization_barrier((first, value))
            handed = swap(first, 1)
            self.arrays = own, other, first, second, handed, swap(second, 1), hop(handed)
        return value

    def settle(self, value):
        if not self.direct:
            parts = jnp.split(lax.all_gather(self.shard, "fsdp", axis=0, tiled=True), PIECES)
            parts = [chunked(part) for part in parts] if self.in_chunks else parts
            return value, Unit(tuple(range(PIECES)), tuple(parts), parts[0].shape[0])
        far, value = lax.optimization_barrier((self.arrays[-1], value))
        arrays = self.arrays[:-1] + (far, swap(far, 1))
        return value, Unit(self.PLACES, arrays, arrays[0].shape[0])


def everywhere(part):
    shards = lax.axis_size("fsdp")
    return lax.all_to_all(
        jnp.tile(part, (shards,) + (1,) * (part.ndim - 1)), "fsdp", 0, 0, tiled=True
    )


def owned_parts(parts):
    shards = lax.axis_size("fsdp")
    rows = parts.shape[0] // shards
    return lax.all_to_all(parts, "fsdp", 0, 0, tiled=True).reshape(
        (shards, rows) + parts.shape[1:]
    )


def summed_everywhere(blocks):
    shards, rows, columns = blocks.shape
    groups = lax.axis_size("dp")
    width = columns - 128
    block = jnp.sum(owned_parts(blocks.reshape(shards * rows, columns)), axis=0)
    others = [
        lax.ppermute(block, "dp", [(i, (i + k) % groups) for i in range(groups)])
        for k in range(1, groups)
    ]
    stacked = jnp.stack([block] + others)
    order = (lax.axis_index("dp") - jnp.arange(groups)) % groups
    ranks = (order[None, :] == jnp.arange(groups)[:, None])[:, :, None, None]
    total = jnp.sum(jnp.sum(jnp.where(ranks, stacked[None], 0.0), axis=1), axis=0)
    gathered = everywhere(total).reshape(shards, rows, columns)
    return (
        gathered[:, :, :width].transpose(1, 0, 2).reshape(rows, shards * width),
        gathered[0, 0, width : width + 2],
    )


def body(
    input_token_ids,
    lengths,
    scored_slots,
    scored_targets,
    wte,
    wpe,
    frozen_attention,
    frozen_feed_input,
    frozen_feed_output,
    frozen_bias_gain,
    final_norm_params,
    adapter_down,
    adapter_down_feed,
    adapter_up,
    first_moment_down,
    first_moment_feed,
    first_moment_up,
    second_moment_down,
    second_moment_feed,
    second_moment_up,
    optimizer_step,
):
    micro, seqs, seq = input_token_ids.shape
    rows = micro * seqs
    picks = scored_slots.shape[2]
    layers = frozen_attention.shape[0]
    shards = lax.axis_size("fsdp")
    row_lengths = lengths.reshape(rows)
    slots = scored_slots.reshape(rows, picks)
    valid = slots < row_lengths[:, None]
    mask = valid.reshape(-1, 1).astype(jnp.float32)
    all_slots = jnp.tile(jnp.arange(seq, dtype=jnp.int32)[None], (rows, 1))

    useful = jnp.max(jnp.where(valid, slots, -1), axis=1)
    needed = jnp.concatenate([(all_slots <= useful[:, None]).reshape(-1), valid.reshape(-1)])
    ids = jnp.concatenate([input_token_ids.reshape(-1), scored_targets.reshape(-1)])
    attention_one, attention_two = Gathering(frozen_attention[0]), Gathering(frozen_attention[1])
    feed_in_one, feed_in_two = Gathering(frozen_feed_input[0]), Gathering(frozen_feed_input[1])
    feed_out_one = Gathering(frozen_feed_output[0], in_chunks=True)
    feed_out_two = Gathering(frozen_feed_output[1], in_chunks=True)
    attention_one.begin()
    ask, rounds, exchanged, sent_for, found, later = asking(wte, ids, needed)
    count = CAPACITY
    requests = as_low(jnp.concatenate([ask(0), jnp.full((shards, 1), rounds, jnp.int32)], 1))
    biases = jnp.tile(frozen_bias_gain.reshape(1, -1), (shards, 1))
    got = exchanged(jnp.concatenate([*requests, biases], 1))
    got = attention_one.pass_on(got)
    feed_in_one.begin(got)
    numbers = as_numbers(got[:, : count + 1], got[:, count + 1 : 2 * count + 2])
    small = (
        got[:, 2 * count + 2 :].reshape(shards, layers, -1).transpose(1, 0, 2).reshape(layers, 1, -1)
    )
    sent = sent_for(numbers[:, :count])
    most = jnp.max(numbers[:, count])
    extra = LANES - ADAPTER_RANK
    down_t = adapter_down.reshape(layers, MODEL_WIDTH, 3, ADAPTER_RANK).transpose(0, 2, 3, 1)
    p = {
        "small": small.astype(jnp.float32),
        "down_t": low(jnp.pad(down_t, ((0, 0), (0, 0), (0, extra), (0, 0)))),
        "feed_t": low(jnp.pad(adapter_down_feed.transpose(0, 2, 1), ((0, 0), (0, extra), (0, 0)))),
        "up": low(jnp.pad(adapter_up, ((0, 0), (0, extra), (0, 0)))),
    }
    back, p = lax.optimization_barrier((exchanged(sent), p))
    back, attention_one = attention_one.settle(back)
    back = feed_in_one.pass_on(back)
    feed_out_one.begin(back)
    looked_up = later(found(0, back), most)
    x0 = looked_up[: rows * seq] + jnp.tile(wpe.astype(jnp.float32), (rows, 1))
    targets = looked_up[rows * seq :]
    index = (slots + seq * jnp.arange(rows, dtype=jnp.int32)[:, None]).reshape(-1)

    qkv, a_one, ua_one = front(x0, attention_one, p, 0)
    qkv, feed_in_one = feed_in_one.settle(qkv)
    split_qkv = (qkv, 0), (qkv, 1), (qkv, 2)
    o_one = attend(row_lengths, all_slots, *split_qkv)
    o_one = feed_out_one.pass_on(o_one)
    attention_two.begin(o_one)
    x2_one, uo_one, m_one, um_one, act_one, slope_one = feed_in(
        x0, o_one, attention_one, feed_in_one, p, 0
    )
    act_one, feed_out_one = feed_out_one.settle(act_one)
    act_one = attention_two.pass_on(act_one)
    feed_in_two.begin(act_one)
    x1, ug_one, _ = feed_out(x2_one, act_one, feed_out_one, final_norm_params, p, 0, False)

    x1, attention_two = attention_two.settle(x1)
    query, kv, a_two, a_sel, ua_two, ua_sel, x_sel = front_last(index, x1, attention_two, p, 1)
    query = feed_in_two.pass_on(query)
    feed_out_two.begin(query)
    parts_two = (query, 0), (kv, 0), (kv, 1)
    o_two = attend(row_lengths, slots, *parts_two)
    o_two, feed_in_two = feed_in_two.settle(o_two)
    x2_two, uo_two, m_two, um_two, act_two, slope_two = feed_in(
        x_sel, o_two, attention_two, feed_in_two, p, 1
    )
    act_two = feed_out_two.pass_on(act_two)
    act_two, feed_out_two = feed_out_two.settle(act_two)
    x3, ug_two, h = feed_out(x2_two, act_two, feed_out_two, final_norm_params, p, 1, True)

    weighed = owned_parts(head(everywhere(h), wte))
    terms, d_x3 = head_back(weighed, targets, h, x3, final_norm_params, mask)

    d_x2, d_heads, grad_ufp, grad_dfp, grad_ufc, grad_dfc, grad_uo, grad_do = feed_back(
        d_x3,
        (x2_two, m_two, um_two, ug_two, uo_two, o_two, act_two, slope_two),
        attention_two,
        feed_in_two,
        feed_out_two,
        p,
        1,
    )
    d_parts = attend_back(row_lengths, slots, *parts_two, d_heads)
    d_x1, grad_uqkv, grad_dqkv = front_last_back(
        index, *d_parts, (a_two, a_sel, ua_two, ua_sel), d_x2, x1, attention_two, p, 1
    )
    grads_two = [
        grad_dqkv, grad_do, grad_dfc, grad_dfp, grad_uqkv, grad_uo, grad_ufc, grad_ufp
    ]

    _, d_heads, grad_ufp, grad_dfp, grad_ufc, grad_dfc, grad_uo, grad_do = feed_back(
        d_x1,
        (x2_one, m_one, um_one, ug_one, uo_one, o_one, act_one, slope_one),
        attention_one,
        feed_in_one,
        feed_out_one,
        p,
        0,
    )
    d_parts = attend_back(row_lengths, all_slots, *split_qkv, d_heads)
    grad_uqkv, grad_dqkv = front_back(*d_parts, a_one, ua_one, p, 0)
    grads_one = [
        grad_dqkv, grad_do, grad_dfc, grad_dfp, grad_uqkv, grad_uo, grad_ufc, grad_ufp
    ]

    tail = jnp.pad(jnp.stack([jnp.sum(terms), jnp.sum(mask)])[None], ((0, 0), (0, 126)))
    gradients, totals = summed_everywhere(packed((grads_one, grads_two), tail))
    loss_total, count = totals[0], totals[1]
    gradients = gradients / count
    norm = jnp.sqrt(jnp.sum(gradients * gradients))
    by_layer = gradients.reshape(layers, ADAPTER_RANK, -1)
    gradient_tree = [
        by_layer[:, :, : 3 * MODEL_WIDTH]
        .reshape(layers, ADAPTER_RANK, 3, MODEL_WIDTH)
        .transpose(0, 3, 2, 1)
        .reshape(layers, MODEL_WIDTH, 3 * ADAPTER_RANK),
        by_layer[:, :, 3 * MODEL_WIDTH : 3 * MODEL_WIDTH + HIDDEN_UNITS].transpose(0, 2, 1),
        by_layer[:, :, 3 * MODEL_WIDTH + HIDDEN_UNITS :],
    ]
    scale_factor = jnp.minimum(1.0, CLIP / (norm + 1e-06))
    step_number = optimizer_step[0].astype(jnp.float32)
    updated = [
        moment_update(weight, first, second, gradient_value, scale_factor, step_number)
        for weight, first, second, gradient_value in zip(
            (adapter_down, adapter_down_feed, adapter_up),
            (first_moment_down, first_moment_feed, first_moment_up),
            (second_moment_down, second_moment_feed, second_moment_up),
            gradient_tree,
        )
    ]
    return (
        loss_total / count,
        norm,
        *(part[0] for part in updated),
        *(part[1] for part in updated),
        *(part[2] for part in updated),
        terms.reshape(micro, seqs, picks),
    )


def solution(mesh):
    in_specs = (
        P(None, ("dp", "fsdp"), None),
        P(None, ("dp", "fsdp")),
        P(None, ("dp", "fsdp"), None),
        P(None, ("dp", "fsdp"), None),
        P("fsdp", None),
        P(),
        P(None, "fsdp", None),
        P(None, "fsdp", None),
        P(None, "fsdp", None),
        P(None, "fsdp"),
        P(),
        P(),
        P(),
        P(),
        P(),
        P(),
        P(),
        P(),
        P(),
        P(),
        P(),
    )
    out_specs = (
        P(),
        P(),
        P(),
        P(),
        P(),
        P(),
        P(),
        P(),
        P(),
        P(),
        P(),
        P(None, ("dp", "fsdp"), None),
    )
    return jax.shard_map(body, mesh=mesh, in_specs=in_specs, out_specs=out_specs, check_vma=False)
```

time: 669 us -> 528 us (0.79)
  Pallas kernels: 14.6 us -> 225 us
  matrix products: 204 us -> 3.86 us
  local copies, waits for them, and re-layouts: 136 us -> 39 us
  other arithmetic: 66.7 us -> 24.6 us
  starting transfers between devices: 80.5 us -> 52.3 us
  waiting for transfers between devices: 127 us -> 140 us
  loops' own time: 0.44 us -> 8.09 us
    pallas_call x4 -> x17, Pallas kernels: 14.6 us -> 225 us  [launch(): pl.pallas_call(kernel, out_shape=[kind for kind, _ in results], grid_spec...]
    dot_general x57 -> x0, matrix products: 125 us -> none  [the longest x25 75.8 us: product_right_transposed(): lax.dot_general(left, right, (((1,), (1,)), ((), ())), preferred_element_...]
    ppermute x3 -> x18, waiting for transfers between devices: 1.42 us -> 80 us  [hop(): lax.ppermute(part, 'fsdp', [(i, i ^ (4 if i % 2 else 2)) for i in range(l...]
    dot_general x29 -> x1, matrix products: 79 us -> 3.86 us  [product_plain(): return jnp.dot(left, right, preferred_element_type=jnp.float32)]
    reshape x16 -> x4, local copies, waits for them, and re-layouts: 43.6 us -> 2.08 us  [the longest x1 1.35 us: sent_for(): return table.at[asked.reshape(-1)].get(mode='promise_in_bounds')]
    ppermute x36 -> x24, waiting for transfers between devices: 51.7 us -> 10.8 us  [swap(): lax.ppermute(part, 'fsdp', [(i, i ^ bit) for i in range(lax.axis_size('fs...]
    reduce_sum x21 -> x3, other arithmetic: 28.5 us -> 1.05 us  [the longest x1 0.66 us: asking(): jnp.sum((leads & (owner[:, None] == owner[None, :]) & (order[None, :] < f...]
    all_to_all x4 -> x1, waiting for transfers between devices: 32.4 us -> 8.65 us  [everywhere(): lax.all_to_all(jnp.tile(part, (shards,) + (1,) * (part.ndim - 1)), 'fsdp'...]
  transfers between devices with their start and end apart: 54 -> 50, of which waited for: 20 -> 24; matrix products, arithmetic and copies ran while one was open for 32% -> 10% of each run, Pallas kernels for 2% -> 19%
where the time goes in v2:
time: 528 us; the launch traced here: 520 us
  Pallas kernels  225 us (43%)
  waiting for transfers between devices  140 us (27%)
  starting transfers between devices  52.3 us (10%)
  local copies, waits for them, and re-layouts  39 us (7%)
  other arithmetic  24.6 us (5%)
  blocking collectives  18.8 us (4%)
  loops' own time  8.09 us (2%)
  between operations  7.9 us (1%)
    pallas_call x17, Pallas kernels, launch(): pl.pallas_call(kernel, out_shape=[kind for kind, _ in results], grid_spec...  225 us
    ppermute x18, waiting for transfers between devices, hop(): lax.ppermute(part, 'fsdp', [(i, i ^ (4 if i % 2 else 2)) for i in range(l...  80 us
    all_to_all x2, waiting for transfers between devices, owned_parts(): lax.all_to_all(parts, 'fsdp', 0, 0, tiled=True)  23.7 us
    ppermute x18, starting transfers between devices, hop(): lax.ppermute(part, 'fsdp', [(i, i ^ (4 if i % 2 else 2)) for i in range(l...  23.6 us
    all_to_all x1, blocking collectives, everywhere(): lax.all_to_all(jnp.tile(part, (shards,) + (1,) * (part.ndim - 1)), 'fsdp'...  18.8 us
    all_to_all x2, waiting for transfers between devices, exchanged(): return lax.all_to_all(part, 'fsdp', 0, 0, tiled=True)  12.3 us
    gather x1, local copies, waits for them, and re-layouts, sent_for(): return table.at[asked.reshape(-1)].get(mode='promise_in_bounds')  10.9 us
    ppermute x24, waiting for transfers between devices, swap(): lax.ppermute(part, 'fsdp', [(i, i ^ bit) for i in range(lax.axis_size('fs...  10.8 us
  transfers between devices with their start and end apart: 50, of which 24 were waited for; matrix products, arithmetic and copies ran while one was open for 10% of the time, Pallas kernels for 19%

profile of v2, /device:TPU:0, one launch (start us, length us, event | category | flops | bytes accessed | tf_op | source)
XLA Modules:
  0.0 520.1 jit_solution(4795135476390207163)
XLA Ops:
  0.7 2.8 slice_bitcast_fusion
  3.5 2.9 collective-permute-start
  15.3 3.3 all-to-all-start.2
  20.6 3.0 all-to-all-done.2
  23.9 3.0 slice_bitcast_fusion.1
  30.3 10.9 %gather_fusion.1 = bf16[640,1024]{1,0:T(8,128)(2,1)} fusion(bf16[6288,1024]{1,0:T(8,128)(2,1)} %table.1, s32[1024]{0:T(1024)} %pad_clamp_fusion.1), kind=kCustom, calls=%fused_computation.1 | custom fusion | bytes 2624000 | tf_op jit(solution)/shard_map/gather | solution.py:1056
  41.2 4.3 all-to-all-start.3
  45.5 1.9 collective-permute-start.1
  49.3 1.8 pad.22.refs_13_.refs_20_.refs_25_.refs_12_.refs_34_.refs_35_.refs_38_.refs_15_.up
  52.7 1.8 collective-permute-start.8
  54.6 9.3 %all-to-all-done.3 = bf16[8,80,1024]{2,1,0:T(8,128)(2,1)} async-done(((bf16[8,80,1024]{2,1,0:T(8,128)(2,1)}), bf16[8,80,1024]{2,1,0:T(8,128)(2,1)}, u32[]{:S(2)}, u32[]{:S(2)}) %all-to-all-start.3) | async-done | bytes 1310752 | tf_op jit(solution)/shard_map/all_to_all | solution.py:1059
  63.8 21.5 %collective-permute-done.3.refs_6_ = bf16[128,4096]{1,0:T(8,128)(2,1)} collective-permute-done((bf16[128,4096]{1,0:T(8,128)(2,1)}, bf16[128,4096]{1,0:T(8,128)(2,1)}, u32[]{:S(2)}, u32[]{:S(2)}) %collective-permute-start.3) | collective-permute-done | bytes 1048608 | tf_op jit(solution)/shard_map/ppermute | solution.py:1098
  87.6 8.9 %collective-permute-done.8.refs_3_ = bf16[128,4096]{1,0:T(8,128)(2,1)} collective-permute-done((bf16[128,4096]{1,0:T(8,128)(2,1)}, bf16[128,4096]{1,0:T(8,128)(2,1)}, u32[]{:S(2)}, u32[]{:S(2)}) %collective-permute-start.8) | collective-permute-done | bytes 1048608 | tf_op jit(solution)/shard_map/ppermute | solution.py:1098
  103.7 3.9 fusion.11
  107.6 8.1 %conditional.1 = (f32[576,1024]{1,0:T(8,128)}) conditional(s32[]{:T(128)} %convert_element_type.72, f32[576,1024]{1,0:T(8,128)} %fusion.11, (s32[576]{0:T(1024)S(1)}, s32[576]{0:T(1024)S(1)}, pred[576]{0:T(1024)(128)(4,1)}, s32[576]{0:T(1024)S(1)}, s32[576]{0:T(1024)S(1)}, /*index=5*/s32[576]{0:T(1024)S(1)}, s32[]{:T(128)}, s32[640]{0:T(1024)S(1)}, ...), branch_computations={%region_6.7_spmd, %region_7.11_spmd} | conditional | flops 757422144 | bytes 12666021 | solution.py:1075
  115.7 3.3 slice_add_fusion.refs_8_.refs_16_
  119.0 11.5 %shard_map.292 = (bf16[512,3072]{1,0:T(8,128)(2,1)}, bf16[512,1024]{1,0:T(8,128)(2,1)}, bf16[512,16]{1,0:T(8,128)(2,1)}) custom-call(bf16[128,4096]{1,0:T(8,128)(2,1)} %copy-done, bf16[128,4096]{1,0:T(8,128)(2,1)} %collective-permute-done.7.refs_1_, bf16[128,4096]{1,0:T(8,128)(2,1)} %copy-done.7, bf16[128,4096]{1,0:T(8,128)(2,1)} %collective-permute-done.8.refs_3_, ...), custom_call_target="tpu_custom_call" | custom-call | flops 3221225472 | bytes 11591680 | tf_op jit(solution)/shard_map/pallas_call | solution.py:111
  130.5 13.6 %shard_map.293.refs_17_.refs_30_ = bf16[512,1024]{1,0:T(8,128)(2,1)} custom-call(s32[2]{0:T(128)} %bitcast.114, s32[512,1]{1,0:T(8,128)} %bitcast.100, bf16[512,3072]{1,0:T(8,128)(2,1)} %get-tuple-element.301.query.key.value, bf16[512,3072]{1,0:T(8,128)(2,1)} %get-tuple-element.301.query.key.value, bf16[512,3072]{1,0:T(8,128)(2,1)} %get-tuple-element.301.query.key.value), custom_call_target="tpu_custom_call" | custom-call | flops 536870912 | bytes 9439232 | tf_op jit(solution)/shard_map/pallas_call | solution.py:111
  145.1 2.0 collective-permute-done.12.refs_4_.refs_20_
  151.6 32.1 %shard_map.294 = (f32[512,1024]{1,0:T(8,128)}, bf16[512,16]{1,0:T(8,128)(2,1)}, bf16[512,1024]{1,0:T(8,128)(2,1)}, bf16[512,16]{1,0:T(8,128)(2,1)}, bf16[512,409...) custom-call(bf16[128,4096]{1,0:T(8,128)(2,1)} %copy-done, bf16[128,4096]{1,0:T(8,128)(2,1)} %collective-permute-done.7.refs_1_, ...), custom_call_target="tpu_custom_call" | custom-call | flops 5368709120 | bytes 21921792 | tf_op jit(solution)/shard_map/pallas_call | solution.py:111
  188.2 10.9 %collective-permute-done.20.refs_3_ = bf16[128,4096]{1,0:T(8,128)(2,1)} collective-permute-done((bf16[128,4096]{1,0:T(8,128)(2,1)}, bf16[128,4096]{1,0:T(8,128)(2,1)}, u32[]{:S(2)}, u32[]{:S(2)}) %collective-permute-start.20) | collective-permute-done | bytes 1048608 | tf_op jit(solution)/shard_map/ppermute | solution.py:1098
  199.1 13.0 %shard_map.295 = (f32[512,1024]{1,0:T(8,128)}, f32[512,16]{1,0:T(8,128)}, bf16[16,1024]{1,0:T(8,128)(2,1)}) custom-call(bf16[128,4096]{1,0:T(8,128)(2,1)} %get-tuple-element.294.refs_0_.refs_16_, bf16[128,4096]{1,0:T(8,128)(2,1)} %collective-permute-done.24.refs_1_.refs_17_, bf16[128,4096]{1,0:T(8,128)(2,1)} %collective-permute-done.4.refs_2_.refs_18_, ...), custom_call_target="tpu_custom_call" | custom-call | flops 4294967296 | bytes 15642624 | tf_op jit(solution)/shard_map/pallas_call | solution.py:111
  215.3 13.0 %shard_map.296 = (bf16[64,1024]{1,0:T(8,128)(2,1)}, bf16[512,2048]{1,0:T(8,128)(2,1)}, bf16[512,1024]{1,0:T(8,128)(2,1)}, bf16[64,1024]{1,0:T(8,128)(2,1)}, bf16...) custom-call(s32[64]{0:T(128)} %add.215.index, bf16[128,4096]{1,0:T(8,128)(2,1)} %get-tuple-element.303.refs_0_, ...), custom_call_target="tpu_custom_call" | custom-call | flops 2147483648 | bytes 11591680 | tf_op jit(solution)/shard_map/pallas_call | solution.py:111
  233.5 10.4 %collective-permute-done.32.refs_11_ = bf16[128,4096]{1,0:T(8,128)(2,1)} collective-permute-done((bf16[128,4096]{1,0:T(8,128)(2,1)}, bf16[128,4096]{1,0:T(8,128)(2,1)}, u32[]{:S(2)}, u32[]{:S(2)}) %collective-permute-start.32) | collective-permute-done | bytes 1048608 | tf_op jit(solution)/shard_map/ppermute | solution.py:1098
  243.9 5.6 %shard_map.297.refs_17_.refs_30_ = bf16[64,1024]{1,0:T(8,128)(2,1)} custom-call(s32[2]{0:T(128)} %bitcast.115, s32[64,1]{1,0:T(8,128)} %copy.89.slots, bf16[64,1024]{1,0:T(8,128)(2,1)} %get-tuple-element.318.query, bf16[512,2048]{1,0:T(8,128)(2,1)} %get-tuple-element.321.key.value, bf16[512,2048]{1,0:T(8,128)(2,1)} %get-tuple-element.321.key.value), custom_call_target="tpu_custom_call" | custom-call | flops 67108864 | bytes 4325632 | tf_op jit(solution)/shard_map/pallas_call | solution.py:111
  249.5 5.7 %collective-permute-done.35.refs_14_ = bf16[128,4096]{1,0:T(8,128)(2,1)} collective-permute-done((bf16[128,4096]{1,0:T(8,128)(2,1)}, bf16[128,4096]{1,0:T(8,128)(2,1)}, u32[]{:S(2)}, u32[]{:S(2)}) %collective-permute-start.35) | collective-permute-done | bytes 1048608 | tf_op jit(solution)/shard_map/ppermute | solution.py:1098
  258.1 10.5 %shard_map.298 = (f32[64,1024]{1,0:T(8,128)}, bf16[64,16]{1,0:T(8,128)(2,1)}, bf16[64,1024]{1,0:T(8,128)(2,1)}, bf16[64,16]{1,0:T(8,128)(2,1)}, bf16[64,4096]{1,0:T(8,128)(2,1)}, /*index=5*/bf16[64,4096]{1,0:T(8,128)(2,1)}) custom-call(bf16[128,4096]{1,0:T(8,128)(2,1)} %get-tuple-element.303.refs_0_, bf16[128,4096]{1,0:T(8,128)(2,1)} %collective-permute-done.19.refs_1_, ...), custom_call_target="tpu_custom_call" | custom-call | flops 671088640 | bytes 19169280 | tf_op jit(solution)/shard_map/pallas_call | solution.py:111
  275.5 9.8 %collective-permute-done.37.refs_3_.refs_19_ = bf16[128,4096]{1,0:T(8,128)(2,1)S(1)} collective-permute-done((bf16[128,4096]{1,0:T(8,128)(2,1)}, bf16[128,4096]{1,0:T(8,128)(2,1)S(1)}, u32[]{:S(2)}, u32[]{:S(2)}) %collective-permute-start.37) | collective-permute-done | bytes 1048608 | tf_op jit(solution)/shard_map/ppermute | solution.py:1098
  285.3 11.2 %collective-permute-done.40.refs_6_.refs_22_ = bf16[128,4096]{1,0:T(8,128)(2,1)S(1)} collective-permute-done((bf16[128,4096]{1,0:T(8,128)(2,1)S(1)}, bf16[128,4096]{1,0:T(8,128)(2,1)S(1)}, u32[]{:S(2)}, u32[]{:S(2)}) %collective-permute-start.40) | collective-permute-done | bytes 1048608 | tf_op jit(solution)/shard_map/ppermute | solution.py:1098
  300.2 7.4 %shard_map.299 = (f32[64,1024]{1,0:T(8,128)}, f32[64,16]{1,0:T(8,128)}, bf16[64,1024]{1,0:T(8,128)(2,1)}) custom-call(bf16[128,4096]{1,0:T(8,128)(2,1)} %get-tuple-element.319.refs_0_.refs_16_, bf16[128,4096]{1,0:T(8,128)(2,1)} %collective-permute-done.29.refs_1_.refs_17_, bf16[128,4096]{1,0:T(8,128)(2,1)} %collective-permute-done.30.refs_2_.refs_18_, ...), custom_call_target="tpu_custom_call" | custom-call | flops 536870912 | bytes 10137600 | tf_op jit(solution)/shard_map/pallas_call | solution.py:111
  308.6 18.8 %all_to_all.81 = bf16[8,64,1024]{2,1,0:T(8,128)(2,1)} all-to-all(bf16[8,64,1024]{2,1,0:T(8,128)(2,1)S(1)} %tile.22), channel_id=1, replica_groups=mesh['dp'=4,'fsdp'=8] {'fsdp'}, dimensions={0} | all-to-all | bytes 2097152 | tf_op jit(solution)/shard_map/all_to_all | solution.py:1137
  327.4 23.2 %shard_map.300 = bf16[512,1152]{1,0:T(8,128)(2,1)} custom-call(bf16[512,1024]{1,0:T(8,128)(2,1)} %bitcast.101, bf16[6288,1024]{1,0:T(8,128)(2,1)} %table.1), custom_call_target="tpu_custom_call" | custom-call | flops 13186891776 | bytes 13926400 | tf_op jit(solution)/shard_map/pallas_call | solution.py:111
  350.6 4.8 all-to-all-start.5
  358.6 13.6 %all-to-all-done.5.parts = bf16[8,64,1152]{2,1,0:T(8,128)(2,1)} async-done(((bf16[8,64,1152]{2,1,0:T(8,128)(2,1)}), bf16[8,64,1152]{2,1,0:T(8,128)(2,1)}, u32[]{:S(2)}, u32[]{:S(2)}) %all-to-all-start.5) | async-done | bytes 1179680 | tf_op jit(solution)/shard_map/all_to_all | solution.py:1145
  372.2 3.0 shard_map.301
  376.6 15.4 %shard_map.302 = (f32[64,1024]{1,0:T(8,128)}, bf16[64,1024]{1,0:T(8,128)(2,1)}, f32[16,1024]{1,0:T(8,128)}, f32[16,4096]{1,0:T(8,128)}, f32[16,4096]{1,0:T(8,128...) custom-call(bf16[128,4096]{1,0:T(8,128)(2,1)} %get-tuple-element.303.refs_0_, ...), custom_call_target="tpu_custom_call" | custom-call | flops 1207959552 | bytes 29540352 | tf_op jit(solution)/shard_map/pallas_call | solution.py:111
  392.0 6.7 %shard_map.303 = (bf16[64,1024]{1,0:T(8,128)(2,1)}, bf16[512,1024]{1,0:T(8,128)(2,1)}, bf16[512,1024]{1,0:T(8,128)(2,1)}) custom-call(s32[2]{0:T(128)} %bitcast.116, s32[64,1]{1,0:T(8,128)} %copy.89.slots, bf16[64,1024]{1,0:T(8,128)(2,1)} %get-tuple-element.318.query, bf16[512,2048]{1,0:T(8,128)(2,1)} %get-tuple-element.321.key.value, ...), custom_call_target="tpu_custom_call" | custom-call | flops 167772160 | bytes 4456704 | tf_op jit(solution)/shard_map/pallas_call | solution.py:111
  400.5 15.1 %shard_map.304 = (f32[512,1024]{1,0:T(8,128)}, f32[16,3072]{1,0:T(8,128)}, f32[16,1024]{1,0:T(8,128)}) custom-call(s32[64]{0:T(128)} %add.215.index, bf16[128,4096]{1,0:T(8,128)(2,1)} %get-tuple-element.303.refs_0_, bf16[128,4096]{1,0:T(8,128)(2,1)} %collective-permute-done.19.refs_1_, bf16[128,4096]{1,0:T(8,128)(2,1)} %collective-permute-done.11.refs_2_, ...), custom_call_target="tpu_custom_call" | custom-call | flops 2147483648 | bytes 15067136 | tf_op jit(solution)/shard_map/pallas_call | solution.py:111
  415.6 30.3 %shard_map.305 = (f32[512,1024]{1,0:T(8,128)}, bf16[512,1024]{1,0:T(8,128)(2,1)}, f32[16,1024]{1,0:T(8,128)}, f32[16,4096]{1,0:T(8,128)}, f32[16,4096]{1,0:T(8,1...) custom-call(bf16[128,4096]{1,0:T(8,128)(2,1)} %copy-done, ...), custom_call_target="tpu_custom_call" | custom-call | flops 9663676416 | bytes 42442752 | tf_op jit(solution)/shard_map/pallas_call | solution.py:111
  446.6 17.6 %shard_map.306 = (bf16[512,1024]{1,0:T(8,128)(2,1)}, bf16[512,1024]{1,0:T(8,128)(2,1)}, bf16[512,1024]{1,0:T(8,128)(2,1)}) custom-call(s32[2]{0:T(128)} %bitcast.117, s32[2,1,256]{2,1,0:T(1,128)} %reshape_tile.7.slots, bf16[512,3072]{1,0:T(8,128)(2,1)} %get-tuple-element.301.query.key.value, bf16[512,3072]{1,0:T(8,128)(2,1)} %get-tuple-element.301.query.key.value, ...), custom_call_target="tpu_custom_call" | custom-call | flops 1342177280 | bytes 10487808 | tf_op jit(solution)/shard_map/pallas_call | solution.py:111
  464.2 4.7 shard_map.307
  468.9 2.5 shard_map.308
  471.3 3.5 all-to-all-start.6
  474.9 10.0 %all-to-all-done.6 = f32[8,8,2176]{2,1,0:T(8,128)S(1)} async-done(((f32[8,8,2176]{2,1,0:T(8,128)}), f32[8,8,2176]{2,1,0:T(8,128)S(1)}, u32[]{:S(2)}, u32[]{:S(2)}) %all-to-all-start.6) | async-done | bytes 557088 | tf_op jit(solution)/shard_map/all_to_all | solution.py:1145
  484.9 3.7 collective-permute-start.44
  490.5 3.3 collective-permute-done.43
  495.8 3.7 all-to-all-start.7
  500.8 8.7 %all-to-all-done.7 = f32[8,8,2176]{2,1,0:T(8,128)S(1)} async-done(((f32[8,8,2176]{2,1,0:T(8,128)}), f32[8,8,2176]{2,1,0:T(8,128)S(1)}, u32[]{:S(2)}, u32[]{:S(2)}) %all-to-all-start.7) | async-done | bytes 557088 | tf_op jit(solution)/shard_map/all_to_all | solution.py:1137
  (226 shorter events, 76.3 us)
Async XLA Ops:
  3.5 20.2 %collective-permute-start = (bf16[128,4096]{1,0:T(8,128)(2,1)S(1)}, bf16[128,4096]{1,0:T(8,128)(2,1)S(1)}, u32[]{:S(2)}, u32[]{:S(2)}) collective-permute-start(bf16[128,4096]{1,0:T(8,128)(2,1)S(1)} %get-tuple-element.494.refs_0_), channel_id=1, source_target_pairs={{0,2},{1,5},{2,0},{3,7},{4,6},{5,1},{6,4},{7,3},{8,10},{9,13},{10,... | collective-permute-start | bytes 3145736 | tf_op jit(solution)/shard_map/ppermute | solution.py:1098
  15.3 8.3 %all-to-all-start.2 = ((bf16[8,2,1745]{2,1,0:T(2,128)(2,1)}), bf16[8,2,1745]{2,1,0:T(2,128)(2,1)S(1)}, u32[]{:S(2)}, u32[]{:S(2)}) async-start(bf16[8,2,1745]{2,1,0:T(2,128)(2,1)} %reshape.650), calls=%async_computation.2 | async-start | bytes 114688 | tf_op jit(solution)/shard_map/all_to_all | solution.py:1059
  18.7 34.0 %collective-permute-start.7 = (bf16[128,4096]{1,0:T(8,128)(2,1)S(1)}, bf16[128,4096]{1,0:T(8,128)(2,1)}, u32[]{:S(2)}, u32[]{:S(2)}) collective-permute-start(bf16[128,4096]{1,0:T(8,128)(2,1)S(1)} %get-tuple-element.494.refs_0_), channel_id=1, source_target_pairs={{0,1},{1,0},{2,3},{3,2},{4,5},{5,4},{6,7},{7,6},{8,9},{9,8},{10,11... | collective-permute-start | bytes 3145736 | tf_op jit(solution)/shard_map/ppermute | solution.py:1089
  23.8 23.6 %collective-permute-start.2 = (bf16[128,4096]{1,0:T(8,128)(2,1)S(1)}, bf16[128,4096]{1,0:T(8,128)(2,1)}, u32[]{:S(2)}, u32[]{:S(2)}) collective-permute-start(bf16[128,4096]{1,0:T(8,128)(2,1)S(1)} %collective-permute-done.refs_2_), channel_id=1, source_target_pairs={{0,1},{1,0},{2,3},{3,2},{4,5},{5,4},{6,7},{7,6},{8,9},{9,8},{10,11... | collective-permute-start | bytes 3145736 | tf_op jit(solution)/shard_map/ppermute | solution.py:1089
  41.2 22.6 %all-to-all-start.3 = ((bf16[8,80,1024]{2,1,0:T(8,128)(2,1)}), bf16[8,80,1024]{2,1,0:T(8,128)(2,1)}, u32[]{:S(2)}, u32[]{:S(2)}) async-start(bf16[8,80,1024]{2,1,0:T(8,128)(2,1)} %bitcast.18), calls=%async_computation.3 | async-start | bytes 2621440 | tf_op jit(solution)/shard_map/all_to_all | solution.py:1059
  45.5 39.8 %collective-permute-start.1 = (bf16[128,4096]{1,0:T(8,128)(2,1)S(1)}, bf16[128,4096]{1,0:T(8,128)(2,1)}, u32[]{:S(2)}, u32[]{:S(2)}) collective-permute-start(bf16[128,4096]{1,0:T(8,128)(2,1)S(1)} %get-tuple-element.289.refs_8_), channel_id=1, source_target_pairs={{0,2},{1,5},{2,0},{3,7},{4,6},{5,1},{6,4},{7,3},{8,10},{9,13},{10,... | collective-permute-start | bytes 3145736 | tf_op jit(solution)/shard_map/ppermute | solution.py:1098
  47.4 37.9 %collective-permute-start.3 = (bf16[128,4096]{1,0:T(8,128)(2,1)}, bf16[128,4096]{1,0:T(8,128)(2,1)}, u32[]{:S(2)}, u32[]{:S(2)}) collective-permute-start(bf16[128,4096]{1,0:T(8,128)(2,1)} %collective-permute-done.2.refs_4_), channel_id=1, source_target_pairs={{0,2},{1,5},{2,0},{3,7},{4,6},{5,1},{6,4},{7,3},{8,10},{9,13},{10,... | collective-permute-start | bytes 3145736 | tf_op jit(solution)/shard_map/ppermute | solution.py:1098
  52.7 43.8 %collective-permute-start.8 = (bf16[128,4096]{1,0:T(8,128)(2,1)}, bf16[128,4096]{1,0:T(8,128)(2,1)}, u32[]{:S(2)}, u32[]{:S(2)}) collective-permute-start(bf16[128,4096]{1,0:T(8,128)(2,1)} %collective-permute-done.7.refs_1_), channel_id=1, source_target_pairs={{0,2},{1,5},{2,0},{3,7},{4,6},{5,1},{6,4},{7,3},{8,10},{9,13},{10,... | collective-permute-start | bytes 3145736 | tf_op jit(solution)/shard_map/ppermute | solution.py:1098
  85.3 11.7 %collective-permute-start.5 = (bf16[128,4096]{1,0:T(8,128)(2,1)}, bf16[128,4096]{1,0:T(8,128)(2,1)}, u32[]{:S(2)}, u32[]{:S(2)}) collective-permute-start(bf16[128,4096]{1,0:T(8,128)(2,1)} %collective-permute-done.1.refs_10_), channel_id=1, source_target_pairs={{0,1},{1,0},{2,3},{3,2},{4,5},{5,4},{6,7},{7,6},{8,9},{9,8},{10,11... | collective-permute-start | bytes 3145736 | tf_op jit(solution)/shard_map/ppermute | solution.py:1089
  85.4 17.6 %collective-permute-start.14 = (bf16[128,4096]{1,0:T(8,128)(2,1)S(1)}, bf16[128,4096]{1,0:T(8,128)(2,1)}, u32[]{:S(2)}, u32[]{:S(2)}) collective-permute-start(bf16[128,4096]{1,0:T(8,128)(2,1)S(1)} %get-tuple-element.289.refs_8_), channel_id=1, source_target_pairs={{0,1},{1,0},{2,3},{3,2},{4,5},{5,4},{6,7},{7,6},{8,9},{9,8},{10,11... | collective-permute-start | bytes 3145736 | tf_op jit(solution)/shard_map/ppermute | solution.py:1089
  96.6 22.5 %collective-permute-start.9 = (bf16[128,4096]{1,0:T(8,128)(2,1)}, bf16[128,4096]{1,0:T(8,128)(2,1)}, u32[]{:S(2)}, u32[]{:S(2)}) collective-permute-start(bf16[128,4096]{1,0:T(8,128)(2,1)} %collective-permute-done.8.refs_3_), channel_id=1, source_target_pairs={{0,1},{1,0},{2,3},{3,2},{4,5},{5,4},{6,7},{7,6},{8,9},{9,8},{10,11... | collective-permute-start | bytes 3145736 | tf_op jit(solution)/shard_map/ppermute | solution.py:1089
  96.6 22.4 %collective-permute-start.10 = (bf16[128,4096]{1,0:T(8,128)(2,1)}, bf16[128,4096]{1,0:T(8,128)(2,1)}, u32[]{:S(2)}, u32[]{:S(2)}) collective-permute-start(bf16[128,4096]{1,0:T(8,128)(2,1)} %collective-permute-done.3.refs_6_), channel_id=1, source_target_pairs={{0,1},{1,0},{2,3},{3,2},{4,5},{5,4},{6,7},{7,6},{8,9},{9,8},{10,11... | collective-permute-start | bytes 3145736 | tf_op jit(solution)/shard_map/ppermute | solution.py:1089
  97.1 33.4 %collective-permute-start.6 = (bf16[128,4096]{1,0:T(8,128)(2,1)}, bf16[128,4096]{1,0:T(8,128)(2,1)}, u32[]{:S(2)}, u32[]{:S(2)}) collective-permute-start(bf16[128,4096]{1,0:T(8,128)(2,1)} %collective-permute-done.5.refs_12_), channel_id=1, source_target_pairs={{0,2},{1,5},{2,0},{3,7},{4,6},{5,1},{6,4},{7,3},{8,10},{9,13},{10,... | collective-permute-start | bytes 3145736 | tf_op jit(solution)/shard_map/ppermute | solution.py:1098
  99.3 44.8 %collective-permute-start.4 = (bf16[128,4096]{1,0:T(8,128)(2,1)}, bf16[128,4096]{1,0:T(8,128)(2,1)}, u32[]{:S(2)}, u32[]{:S(2)}) collective-permute-start(bf16[128,4096]{1,0:T(8,128)(2,1)} %get-tuple-element.294.refs_0_.refs_16_), channel_id=1, source_target_pairs={{0,2},{1,5},{2,0},{3,7},{4,6},{5,1},{6,4},{7,3},{8,10},{9,13},{10,... | collective-permute-start | bytes 3145736 | tf_op jit(solution)/shard_map/ppermute | solution.py:1098
  103.0 41.7 %collective-permute-start.15 = (bf16[128,4096]{1,0:T(8,128)(2,1)}, bf16[128,4096]{1,0:T(8,128)(2,1)}, u32[]{:S(2)}, u32[]{:S(2)}) collective-permute-start(bf16[128,4096]{1,0:T(8,128)(2,1)} %collective-permute-done.14.refs_9_), channel_id=1, source_target_pairs={{0,2},{1,5},{2,0},{3,7},{4,6},{5,1},{6,4},{7,3},{8,10},{9,13},{10,... | collective-permute-start | bytes 3145736 | tf_op jit(solution)/shard_map/ppermute | solution.py:1098
  144.1 3.0 collective-permute-start.12
  144.1 5.0 collective-permute-start.24
  144.6 5.8 %collective-permute-start.16 = (bf16[128,4096]{1,0:T(8,128)(2,1)}, bf16[128,4096]{1,0:T(8,128)(2,1)}, u32[]{:S(2)}, u32[]{:S(2)}) collective-permute-start(bf16[128,4096]{1,0:T(8,128)(2,1)} %collective-permute-done.15.refs_11_), channel_id=1, source_target_pairs={{0,1},{1,0},{2,3},{3,2},{4,5},{5,4},{6,7},{7,6},{8,9},{9,8},{10,11... | collective-permute-start | bytes 3145736 | tf_op jit(solution)/shard_map/ppermute | solution.py:1089
  144.7 6.9 %collective-permute-start.17 = (bf16[128,4096]{1,0:T(8,128)(2,1)}, bf16[128,4096]{1,0:T(8,128)(2,1)}, u32[]{:S(2)}, u32[]{:S(2)}) collective-permute-start(bf16[128,4096]{1,0:T(8,128)(2,1)} %collective-permute-done.6.refs_14_), channel_id=1, source_target_pairs={{0,1},{1,0},{2,3},{3,2},{4,5},{5,4},{6,7},{7,6},{8,9},{9,8},{10,11... | collective-permute-start | bytes 3145736 | tf_op jit(solution)/shard_map/ppermute | solution.py:1089
  147.1 36.6 %collective-permute-start.13 = (bf16[128,4096]{1,0:T(8,128)(2,1)}, bf16[128,4096]{1,0:T(8,128)(2,1)}, u32[]{:S(2)}, u32[]{:S(2)}) collective-permute-start(bf16[128,4096]{1,0:T(8,128)(2,1)} %collective-permute-done.12.refs_4_.refs_20_), channel_id=1, source_target_pairs={{0,2},{1,5},{2,0},{3,7},{4,6},{5,1},{6,4},{7,3},{8,10},{9,13},{10,... | collective-permute-start | bytes 3145736 | tf_op jit(solution)/shard_map/ppermute | solution.py:1098
  148.4 35.3 %collective-permute-start.11 = (bf16[128,4096]{1,0:T(8,128)(2,1)}, bf16[128,4096]{1,0:T(8,128)(2,1)}, u32[]{:S(2)}, u32[]{:S(2)}) collective-permute-start(bf16[128,4096]{1,0:T(8,128)(2,1)} %get-tuple-element.303.refs_0_), channel_id=1, source_target_pairs={{0,2},{1,5},{2,0},{3,7},{4,6},{5,1},{6,4},{7,3},{8,10},{9,13},{10,... | collective-permute-start | bytes 3145736 | tf_op jit(solution)/shard_map/ppermute | solution.py:1098
  149.1 36.1 %collective-permute-start.25 = (bf16[128,4096]{1,0:T(8,128)(2,1)}, bf16[128,4096]{1,0:T(8,128)(2,1)}, u32[]{:S(2)}, u32[]{:S(2)}) collective-permute-start(bf16[128,4096]{1,0:T(8,128)(2,1)} %collective-permute-done.24.refs_1_.refs_17_), channel_id=1, source_target_pairs={{0,2},{1,5},{2,0},{3,7},{4,6},{5,1},{6,4},{7,3},{8,10},{9,13},{10,... | collective-permute-start | bytes 3145736 | tf_op jit(solution)/shard_map/ppermute | solution.py:1098
  150.5 33.5 %collective-permute-start.19 = (bf16[128,4096]{1,0:T(8,128)(2,1)}, bf16[128,4096]{1,0:T(8,128)(2,1)}, u32[]{:S(2)}, u32[]{:S(2)}) collective-permute-start(bf16[128,4096]{1,0:T(8,128)(2,1)} %get-tuple-element.303.refs_0_), channel_id=1, source_target_pairs={{0,1},{1,0},{2,3},{3,2},{4,5},{5,4},{6,7},{7,6},{8,9},{9,8},{10,11... | collective-permute-start | bytes 3145736 | tf_op jit(solution)/shard_map/ppermute | solution.py:1089
  183.8 3.1 collective-permute-start.21
  184.0 15.1 %collective-permute-start.20 = (bf16[128,4096]{1,0:T(8,128)(2,1)}, bf16[128,4096]{1,0:T(8,128)(2,1)}, u32[]{:S(2)}, u32[]{:S(2)}) collective-permute-start(bf16[128,4096]{1,0:T(8,128)(2,1)} %collective-permute-done.19.refs_1_), channel_id=1, source_target_pairs={{0,2},{1,5},{2,0},{3,7},{4,6},{5,1},{6,4},{7,3},{8,10},{9,13},{10,... | collective-permute-start | bytes 3145736 | tf_op jit(solution)/shard_map/ppermute | solution.py:1098
  185.3 13.8 %collective-permute-start.26 = (bf16[128,4096]{1,0:T(8,128)(2,1)}, bf16[128,4096]{1,0:T(8,128)(2,1)}, u32[]{:S(2)}, u32[]{:S(2)}) collective-permute-start(bf16[128,4096]{1,0:T(8,128)(2,1)} %collective-permute-done.25.refs_3_.refs_19_), channel_id=1, source_target_pairs={{0,1},{1,0},{2,3},{3,2},{4,5},{5,4},{6,7},{7,6},{8,9},{9,8},{10,11... | collective-permute-start | bytes 3145736 | tf_op jit(solution)/shard_map/ppermute | solution.py:1089
  185.4 13.7 %collective-permute-start.27 = (bf16[128,4096]{1,0:T(8,128)(2,1)}, bf16[128,4096]{1,0:T(8,128)(2,1)}, u32[]{:S(2)}, u32[]{:S(2)}) collective-permute-start(bf16[128,4096]{1,0:T(8,128)(2,1)} %collective-permute-done.13.refs_6_.refs_22_), channel_id=1, source_target_pairs={{0,1},{1,0},{2,3},{3,2},{4,5},{5,4},{6,7},{7,6},{8,9},{9,8},{10,11... | collective-permute-start | bytes 3145736 | tf_op jit(solution)/shard_map/ppermute | solution.py:1089
  186.9 25.3 %collective-permute-start.23 = (bf16[128,4096]{1,0:T(8,128)(2,1)}, bf16[128,4096]{1,0:T(8,128)(2,1)}, u32[]{:S(2)}, u32[]{:S(2)}) collective-permute-start(bf16[128,4096]{1,0:T(8,128)(2,1)} %collective-permute-done.21.refs_4_), channel_id=1, source_target_pairs={{0,2},{1,5},{2,0},{3,7},{4,6},{5,1},{6,4},{7,3},{8,10},{9,13},{10,... | collective-permute-start | bytes 3145736 | tf_op jit(solution)/shard_map/ppermute | solution.py:1098
  199.1 15.6 %collective-permute-start.22 = (bf16[128,4096]{1,0:T(8,128)(2,1)}, bf16[128,4096]{1,0:T(8,128)(2,1)}, u32[]{:S(2)}, u32[]{:S(2)}) collective-permute-start(bf16[128,4096]{1,0:T(8,128)(2,1)} %collective-permute-done.20.refs_3_), channel_id=1, source_target_pairs={{0,1},{1,0},{2,3},{3,2},{4,5},{5,4},{6,7},{7,6},{8,9},{9,8},{10,11... | collective-permute-start | bytes 3145736 | tf_op jit(solution)/shard_map/ppermute | solution.py:1089
  212.1 3.2 collective-permute-start.28
  212.7 15.7 %collective-permute-start.18 = (bf16[128,4096]{1,0:T(8,128)(2,1)}, bf16[128,4096]{1,0:T(8,128)(2,1)}, u32[]{:S(2)}, u32[]{:S(2)}) collective-permute-start(bf16[128,4096]{1,0:T(8,128)(2,1)} %get-tuple-element.309.refs_8_), channel_id=1, source_target_pairs={{0,2},{1,5},{2,0},{3,7},{4,6},{5,1},{6,4},{7,3},{8,10},{9,13},{10,... | collective-permute-start | bytes 3145736 | tf_op jit(solution)/shard_map/ppermute | solution.py:1098
  214.7 14.1 %collective-permute-start.31 = (bf16[128,4096]{1,0:T(8,128)(2,1)}, bf16[128,4096]{1,0:T(8,128)(2,1)}, u32[]{:S(2)}, u32[]{:S(2)}) collective-permute-start(bf16[128,4096]{1,0:T(8,128)(2,1)} %get-tuple-element.309.refs_8_), channel_id=1, source_target_pairs={{0,1},{1,0},{2,3},{3,2},{4,5},{5,4},{6,7},{7,6},{8,9},{9,8},{10,11... | collective-permute-start | bytes 3145736 | tf_op jit(solution)/shard_map/ppermute | solution.py:1089
  228.4 3.1 collective-permute-start.33
  228.8 15.1 %collective-permute-start.32 = (bf16[128,4096]{1,0:T(8,128)(2,1)}, bf16[128,4096]{1,0:T(8,128)(2,1)}, u32[]{:S(2)}, u32[]{:S(2)}) collective-permute-start(bf16[128,4096]{1,0:T(8,128)(2,1)} %collective-permute-done.31.refs_9_), channel_id=1, source_target_pairs={{0,2},{1,5},{2,0},{3,7},{4,6},{5,1},{6,4},{7,3},{8,10},{9,13},{10,... | collective-permute-start | bytes 3145736 | tf_op jit(solution)/shard_map/ppermute | solution.py:1098
  231.4 23.7 %collective-permute-start.35 = (bf16[128,4096]{1,0:T(8,128)(2,1)}, bf16[128,4096]{1,0:T(8,128)(2,1)}, u32[]{:S(2)}, u32[]{:S(2)}) collective-permute-start(bf16[128,4096]{1,0:T(8,128)(2,1)} %collective-permute-done.33.refs_12_), channel_id=1, source_target_pairs={{0,2},{1,5},{2,0},{3,7},{4,6},{5,1},{6,4},{7,3},{8,10},{9,13},{10,... | collective-permute-start | bytes 3145736 | tf_op jit(solution)/shard_map/ppermute | solution.py:1098
  243.9 12.8 %collective-permute-start.34 = (bf16[128,4096]{1,0:T(8,128)(2,1)}, bf16[128,4096]{1,0:T(8,128)(2,1)}, u32[]{:S(2)}, u32[]{:S(2)}) collective-permute-start(bf16[128,4096]{1,0:T(8,128)(2,1)} %collective-permute-done.32.refs_11_), channel_id=1, source_target_pairs={{0,1},{1,0},{2,3},{3,2},{4,5},{5,4},{6,7},{7,6},{8,9},{9,8},{10,11... | collective-permute-start | bytes 3145736 | tf_op jit(solution)/shard_map/ppermute | solution.py:1089
  255.1 3.0 collective-permute-start.36
  255.1 15.1 %collective-permute-start.30 = (bf16[128,4096]{1,0:T(8,128)(2,1)}, bf16[128,4096]{1,0:T(8,128)(2,1)}, u32[]{:S(2)}, u32[]{:S(2)}) collective-permute-start(bf16[128,4096]{1,0:T(8,128)(2,1)} %get-tuple-element.319.refs_0_.refs_16_), channel_id=1, source_target_pairs={{0,2},{1,5},{2,0},{3,7},{4,6},{5,1},{6,4},{7,3},{8,10},{9,13},{10,... | collective-permute-start | bytes 3145736 | tf_op jit(solution)/shard_map/ppermute | solution.py:1098
  256.5 13.8 %collective-permute-start.29 = (bf16[128,4096]{1,0:T(8,128)(2,1)}, bf16[128,4096]{1,0:T(8,128)(2,1)}, u32[]{:S(2)}, u32[]{:S(2)}) collective-permute-start(bf16[128,4096]{1,0:T(8,128)(2,1)} %get-tuple-element.319.refs_0_.refs_16_), channel_id=1, source_target_pairs={{0,1},{1,0},{2,3},{3,2},{4,5},{5,4},{6,7},{7,6},{8,9},{9,8},{10,11... | collective-permute-start | bytes 3145736 | tf_op jit(solution)/shard_map/ppermute | solution.py:1089
  270.3 15.0 %collective-permute-start.37 = (bf16[128,4096]{1,0:T(8,128)(2,1)}, bf16[128,4096]{1,0:T(8,128)(2,1)S(1)}, u32[]{:S(2)}, u32[]{:S(2)}) collective-permute-start(bf16[128,4096]{1,0:T(8,128)(2,1)} %collective-permute-done.29.refs_1_.refs_17_), channel_id=1, source_target_pairs={{0,2},{1,5},{2,0},{3,7},{4,6},{5,1},{6,4},{7,3},{8,10},{9,13},{10,... | collective-permute-start | bytes 3145736 | tf_op jit(solution)/shard_map/ppermute | solution.py:1098
  274.1 22.4 %collective-permute-start.40 = (bf16[128,4096]{1,0:T(8,128)(2,1)S(1)}, bf16[128,4096]{1,0:T(8,128)(2,1)S(1)}, u32[]{:S(2)}, u32[]{:S(2)}) collective-permute-start(bf16[128,4096]{1,0:T(8,128)(2,1)S(1)} %collective-permute-done.38.refs_4_.refs_20_), channel_id=1, source_target_pairs={{0,2},{1,5},{2,0},{3,7},{4,6},{5,1},{6,4},{7,3},{8,10},{9,13},{10,... | collective-permute-start | bytes 3145736 | tf_op jit(solution)/shard_map/ppermute | solution.py:1098
  285.3 11.2 %collective-permute-start.39 = (bf16[128,4096]{1,0:T(8,128)(2,1)S(1)}, bf16[128,4096]{1,0:T(8,128)(2,1)S(1)}, u32[]{:S(2)}, u32[]{:S(2)}) collective-permute-start(bf16[128,4096]{1,0:T(8,128)(2,1)S(1)} %collective-permute-done.37.refs_3_.refs_19_), channel_id=1, source_target_pairs={{0,1},{1,0},{2,3},{3,2},{4,5},{5,4},{6,7},{7,6},{8,9},{9,8},{10,11... | collective-permute-start | bytes 3145736 | tf_op jit(solution)/shard_map/ppermute | solution.py:1089
  350.6 21.6 %all-to-all-start.5 = ((bf16[8,64,1152]{2,1,0:T(8,128)(2,1)}), bf16[8,64,1152]{2,1,0:T(8,128)(2,1)}, u32[]{:S(2)}, u32[]{:S(2)}) async-start(bf16[8,64,1152]{2,1,0:T(8,128)(2,1)} %bitcast.99), calls=%async_computation.5 | async-start | bytes 2359296 | tf_op jit(solution)/shard_map/all_to_all | solution.py:1145
  471.3 13.6 %all-to-all-start.6 = ((f32[8,8,2176]{2,1,0:T(8,128)}), f32[8,8,2176]{2,1,0:T(8,128)S(1)}, u32[]{:S(2)}, u32[]{:S(2)}) async-start(f32[8,8,2176]{2,1,0:T(8,128)} %shard_map.308), calls=%async_computation.6 | async-start | bytes 1114112 | tf_op jit(solution)/shard_map/all_to_all | solution.py:1145
  484.9 5.6 %collective-permute-start.44 = (f32[8,2176]{1,0:T(8,128)S(1)}, f32[8,2176]{1,0:T(8,128)S(1)}, u32[]{:S(2)}, u32[]{:S(2)}) collective-permute-start(f32[8,2176]{1,0:T(8,128)S(1)} %reduce_sum.83), channel_id=1, source_target_pairs={{0,24},{8,0},{16,8},{24,16},{1,25},{9,1},{17,9},{25,17},{2,26},{10... | collective-permute-start | bytes 208904 | tf_op jit(solution)/shard_map/ppermute | solution.py:1156
  488.6 5.2 %collective-permute-start.43 = (f32[8,2176]{1,0:T(8,128)S(1)}, f32[8,2176]{1,0:T(8,128)S(1)}, u32[]{:S(2)}, u32[]{:S(2)}) collective-permute-start(f32[8,2176]{1,0:T(8,128)S(1)} %reduce_sum.83), channel_id=1, source_target_pairs={{0,16},{8,24},{16,0},{24,8},{1,17},{9,25},{17,1},{25,9},{2,18},{10... | collective-permute-start | bytes 208904 | tf_op jit(solution)/shard_map/ppermute | solution.py:1156
  488.6 6.1 %collective-permute-start.42 = (f32[8,2176]{1,0:T(8,128)S(1)}, f32[8,2176]{1,0:T(8,128)S(1)}, u32[]{:S(2)}, u32[]{:S(2)}) collective-permute-start(f32[8,2176]{1,0:T(8,128)S(1)} %reduce_sum.83), channel_id=1, source_target_pairs={{0,8},{8,16},{16,24},{24,0},{1,9},{9,17},{17,25},{25,1},{2,10},{10... | collective-permute-start | bytes 208904 | tf_op jit(solution)/shard_map/ppermute | solution.py:1156
  495.8 13.7 %all-to-all-start.7 = ((f32[8,8,2176]{2,1,0:T(8,128)}), f32[8,8,2176]{2,1,0:T(8,128)S(1)}, u32[]{:S(2)}, u32[]{:S(2)}) async-start(f32[8,8,2176]{2,1,0:T(8,128)} %tile.46), calls=%async_computation.7 | async-start | bytes 1114112 | tf_op jit(solution)/shard_map/all_to_all | solution.py:1137
  (35 other events, 316.2 us)

commit v3 on v2

--- a/solution.py
+++ b/solution.py
@@ -83,6 +83,11 @@
     shape = (None,) * len(lead) + array.shape[len(lead) :]
     place = lead + (0,) * (array.ndim - len(lead))
     return array, pl.BlockSpec(shape, lambda *_: place, pipeline_mode=pl.Buffered(1))
+
+
+def some_rows(array, count, row=0):
+    shape = (count, array.shape[1])
+    return array, pl.BlockSpec(shape, lambda *_: (row, 0), pipeline_mode=pl.Buffered(1))
 
 
 def strip(array, width, column, *lead):
@@ -244,14 +249,13 @@
     qkv[...] = low(product_plain(a[...], weight[...]) + bias[...] + adapter(ua[...], up[...]))
 
 
-def front(x, unit, p, layer):
-    tokens = x.shape[0]
+def front(x, tokens, unit, p, layer):
     return launch(
         partial(front_kernel, unit),
         (3,),
         unit.operands()
         + [
-            whole(x),
+            some_rows(x, tokens),
             strip(p["small"], BLOCK, 9, layer),
             strip(p["small"], BLOCK, 10, layer),
             strip(p["small"], BLOCK, lambda j: j, layer),
@@ -573,7 +577,7 @@
 
 
 def feed_in(x, o, unit, unit_fc, p, layer):
-    tokens = x.shape[0]
+    tokens = o.shape[0]
     small, up = p["small"], p["up"]
     wide = (tokens, HIDDEN_UNITS), jnp.bfloat16, (tokens, BLOCK), lambda j: (0, j)
     return launch(
@@ -582,7 +586,7 @@
         unit.operands()
         + unit_fc.operands()
         + [
-            whole(x),
+            some_rows(x, tokens),
             whole(o),
             strip(small, BLOCK, 3, layer),
             whole(p["down_t"], layer, 1),
@@ -743,7 +747,7 @@
     return launch(
         head_back_kernel,
         (1,),
-        [whole(parts), whole(targets), whole(h), whole(x3), whole(final), whole(mask)],
+        [whole(parts), some_rows(targets, count, targets.shape[0] // count - 1), whole(h), whole(x3), whole(final), whole(mask)],
         [
             result((count, 1), jnp.float32),
             result((count, MODEL_WIDTH), jnp.float32),
@@ -1062,7 +1066,7 @@
         pick = (place_of(turn)[:, None] == spots[None, :]).astype(jnp.bfloat16)
         return product_plain(pick, back)
 
-    def later(first, most):
+    def with_rounds(most, added):
         def more(so_far):
             return lax.fori_loop(
                 1,
@@ -1072,9 +1076,9 @@
                 so_far,
             )
 
-        return lax.cond(most > 1, more, lambda so_far: so_far, first)
-
-    return ask, rounds, exchanged, sent_for, found, later
+        return lax.cond(most > 1, more, lambda so_far: so_far, added)
+
+    return ask, rounds, exchanged, sent_for, found, with_rounds
 
 
 def as_low(numbers):
@@ -1113,6 +1117,12 @@
             own = tie(own, before)
             other = swap(own, 1)
             self.arrays = own, other, hop(own), hop(other)
+
+    def after_first(self, value):
+        return tie(value, self.arrays[1]) if self.direct else value
+
+    def after_last(self, value):
+        return tie(value, self.arrays[4]) if self.direct else value
 
     def pass_on(self, value):
         if self.direct:
@@ -1209,18 +1219,19 @@
     feed_out_one = Gathering(frozen_feed_output[0], in_chunks=True)
     feed_out_two = Gathering(frozen_feed_output[1], in_chunks=True)
     attention_one.begin()
-    ask, rounds, exchanged, sent_for, found, later = asking(wte, ids, needed)
+    ask, rounds, exchanged, sent_for, found, with_rounds = asking(wte, ids, needed)
     count = CAPACITY
     requests = as_low(jnp.concatenate([ask(0), jnp.full((shards, 1), rounds, jnp.int32)], 1))
     biases = jnp.tile(frozen_bias_gain.reshape(1, -1), (shards, 1))
-    got = exchanged(jnp.concatenate([*requests, biases], 1))
+    message = jnp.concatenate([*requests, biases], 1)
+    got = exchanged(attention_one.after_first(message))
     got = attention_one.pass_on(got)
     feed_in_one.begin(got)
     numbers = as_numbers(got[:, : count + 1], got[:, count + 1 : 2 * count + 2])
     small = (
         got[:, 2 * count + 2 :].reshape(shards, layers, -1).transpose(1, 0, 2).reshape(layers, 1, -1)
     )
-    sent = sent_for(numbers[:, :count])
+    sent = sent_for(attention_one.after_last(numbers[:, :count]))
     most = jnp.max(numbers[:, count])
     extra = LANES - ADAPTER_RANK
     down_t = adapter_down.reshape(layers, MODEL_WIDTH, 3, ADAPTER_RANK).transpose(0, 2, 3, 1)
@@ -1230,45 +1241,46 @@
         "feed_t": low(jnp.pad(adapter_down_feed.transpose(0, 2, 1), ((0, 0), (0, extra), (0, 0)))),
         "up": low(jnp.pad(adapter_up, ((0, 0), (0, extra), (0, 0)))),
     }
-    back, p = lax.optimization_barrier((exchanged(sent), p))
+    places = jnp.concatenate([wpe.astype(jnp.float32)] * rows)
+    places = jnp.pad(places, ((0, rows * picks), (0, 0)))
+    places = with_rounds(most, places)
+    back, p, places = lax.optimization_barrier((exchanged(sent), p, places))
     back, attention_one = attention_one.settle(back)
     back = feed_in_one.pass_on(back)
     feed_out_one.begin(back)
-    looked_up = later(found(0, back), most)
-    x0 = looked_up[: rows * seq] + jnp.tile(wpe.astype(jnp.float32), (rows, 1))
-    targets = looked_up[rows * seq :]
+    x0 = found(0, back) + places
     index = (slots + seq * jnp.arange(rows, dtype=jnp.int32)[:, None]).reshape(-1)
 
-    qkv, a_one, ua_one = front(x0, attention_one, p, 0)
-    qkv, feed_in_one = feed_in_one.settle(qkv)
+    qkv, a_one, ua_one = front(x0, rows * seq, attention_one, p, 0)
+    qkv = feed_out_one.pass_on(qkv)
+    attention_two.begin(qkv)
     split_qkv = (qkv, 0), (qkv, 1), (qkv, 2)
     o_one = attend(row_lengths, all_slots, *split_qkv)
-    o_one = feed_out_one.pass_on(o_one)
-    attention_two.begin(o_one)
+    o_one, feed_in_one = feed_in_one.settle(o_one)
+    o_one = attention_two.pass_on(o_one)
+    feed_in_two.begin(o_one)
     x2_one, uo_one, m_one, um_one, act_one, slope_one = feed_in(
         x0, o_one, attention_one, feed_in_one, p, 0
     )
     act_one, feed_out_one = feed_out_one.settle(act_one)
-    act_one = attention_two.pass_on(act_one)
-    feed_in_two.begin(act_one)
+    act_one = feed_in_two.pass_on(act_one)
+    feed_out_two.begin(act_one)
     x1, ug_one, _ = feed_out(x2_one, act_one, feed_out_one, final_norm_params, p, 0, False)
-
     x1, attention_two = attention_two.settle(x1)
+    x1 = feed_out_two.pass_on(x1)
+
     query, kv, a_two, a_sel, ua_two, ua_sel, x_sel = front_last(index, x1, attention_two, p, 1)
-    query = feed_in_two.pass_on(query)
-    feed_out_two.begin(query)
+    query, feed_in_two = feed_in_two.settle(query)
     parts_two = (query, 0), (kv, 0), (kv, 1)
     o_two = attend(row_lengths, slots, *parts_two)
-    o_two, feed_in_two = feed_in_two.settle(o_two)
     x2_two, uo_two, m_two, um_two, act_two, slope_two = feed_in(
         x_sel, o_two, attention_two, feed_in_two, p, 1
     )
-    act_two = feed_out_two.pass_on(act_two)
     act_two, feed_out_two = feed_out_two.settle(act_two)
     x3, ug_two, h = feed_out(x2_two, act_two, feed_out_two, final_norm_params, p, 1, True)
 
     weighed = owned_parts(head(everywhere(h), wte))
-    terms, d_x3 = head_back(weighed, targets, h, x3, final_norm_params, mask)
+    terms, d_x3 = head_back(weighed, x0, h, x3, final_norm_params, mask)
 
     d_x2, d_heads, grad_ufp, grad_dfp, grad_ufc, grad_dfc, grad_uo, grad_do = feed_back(
         d_x3,

time: 528 us -> 483 us (0.915)
  waiting for transfers between devices: 140 us -> 116 us
  loops' own time: 8.09 us -> 0.01 us
  local copies, waits for them, and re-layouts: 39 us -> 32.8 us
    ppermute x18, waiting for transfers between devices: 80 us -> 65.1 us  [hop(): lax.ppermute(part, 'fsdp', [(i, i ^ (4 if i % 2 else 2)) for i in range(l...]
    another operation x1, loops' own time: 8.09 us -> 0.01 us  [with_rounds(): return lax.cond(most > 1, more, lambda so_far: so_far, added)]
    ppermute x24, waiting for transfers between devices: 10.8 us -> 3.18 us  [swap(): lax.ppermute(part, 'fsdp', [(i, i ^ bit) for i in range(lax.axis_size('fs...]
  transfers between devices with their start and end apart: 50 -> 50, of which waited for: 24 -> 18; matrix products, arithmetic and copies ran while one was open for 10% -> 9% of each run, Pallas kernels for 19% -> 21%
where the time goes in v3:
time: 483 us; the launch traced here: 473 us
  Pallas kernels  225 us (47%)
  waiting for transfers between devices  116 us (24%)
  starting transfers between devices  49 us (10%)
  local copies, waits for them, and re-layouts  32.8 us (7%)
  other arithmetic  19.5 us (4%)
  blocking collectives  18.7 us (4%)
  between operations  7.88 us (2%)
    pallas_call x17, Pallas kernels, launch(): pl.pallas_call(kernel, out_shape=[kind for kind, _ in results], grid_spec...  225 us
    ppermute x18, waiting for transfers between devices, hop(): lax.ppermute(part, 'fsdp', [(i, i ^ (4 if i % 2 else 2)) for i in range(l...  65.1 us
    all_to_all x2, waiting for transfers between devices, owned_parts(): lax.all_to_all(parts, 'fsdp', 0, 0, tiled=True)  25.3 us
    ppermute x18, starting transfers between devices, hop(): lax.ppermute(part, 'fsdp', [(i, i ^ (4 if i % 2 else 2)) for i in range(l...  19.1 us
    all_to_all x1, blocking collectives, everywhere(): lax.all_to_all(jnp.tile(part, (shards,) + (1,) * (part.ndim - 1)), 'fsdp'...  18.7 us
    all_to_all x2, waiting for transfers between devices, exchanged(): return lax.all_to_all(part, 'fsdp', 0, 0, tiled=True)  11 us
    gather x1, local copies, waits for them, and re-layouts, sent_for(): return table.at[asked.reshape(-1)].get(mode='promise_in_bounds')  10.8 us
  transfers between devices with their start and end apart: 50, of which 18 were waited for; matrix products, arithmetic and copies ran while one was open for 9% of the time, Pallas kernels for 21%

profile of v3, /device:TPU:0, one launch (start us, length us, event | category | flops | bytes accessed | tf_op | source)
XLA Modules:
  0.0 473.3 jit_solution(4842769332370812263)
XLA Ops:
  0.7 2.8 slice_bitcast_fusion
  3.9 2.5 collective-permute-start
  14.1 3.3 all-to-all-start.2
  19.1 3.2 all-to-all-done.2
  22.6 2.7 slice_bitcast_fusion.1
  27.5 10.8 %gather_fusion.1 = bf16[640,1024]{1,0:T(8,128)(2,1)} fusion(bf16[6288,1024]{1,0:T(8,128)(2,1)} %table.1, s32[1024]{0:T(1024)S(1)} %pad_clamp_fusion.1), kind=kCustom, calls=%fused_computation.1 | custom fusion | bytes 2624000 | tf_op jit(solution)/shard_map/gather | solution.py:1060
  38.3 3.9 all-to-all-start.3
  42.2 2.0 collective-permute-start.4
  44.4 2.8 slice_bitcast_fusion.7
  52.7 7.8 %all-to-all-done.3 = bf16[8,80,1024]{2,1,0:T(8,128)(2,1)S(1)} async-done(((bf16[8,80,1024]{2,1,0:T(8,128)(2,1)}), bf16[8,80,1024]{2,1,0:T(8,128)(2,1)S(1)}, u32[]{:S(2)}, u32[]{:S(2)}) %all-to-all-start.3) | async-done | bytes 1310752 | tf_op jit(solution)/shard_map/all_to_all | solution.py:1063
  60.5 10.4 %collective-permute-done.4.refs_6_ = bf16[128,4096]{1,0:T(8,128)(2,1)} collective-permute-done((bf16[128,4096]{1,0:T(8,128)(2,1)}, bf16[128,4096]{1,0:T(8,128)(2,1)}, u32[]{:S(2)}, u32[]{:S(2)}) %collective-permute-start.4) | collective-permute-done | bytes 1048608 | tf_op jit(solution)/shard_map/ppermute | solution.py:1102
  70.8 3.1 pad_maximum_fusion
  73.9 8.1 %collective-permute-done.2.refs_10_ = bf16[128,4096]{1,0:T(8,128)(2,1)} collective-permute-done((bf16[128,4096]{1,0:T(8,128)(2,1)S(1)}, bf16[128,4096]{1,0:T(8,128)(2,1)}, u32[]{:S(2)}, u32[]{:S(2)}) %collective-permute-start.2) | collective-permute-done | bytes 1048608 | tf_op jit(solution)/shard_map/ppermute | solution.py:1102
  82.4 1.7 collective-permute-start.16
  84.1 4.2 convolution_add_fusion.refs_8_.refs_16_.targets
  88.6 11.5 %shard_map.292 = (bf16[512,3072]{1,0:T(8,128)(2,1)}, bf16[512,1024]{1,0:T(8,128)(2,1)}, bf16[512,16]{1,0:T(8,128)(2,1)}) custom-call(bf16[128,4096]{1,0:T(8,128)(2,1)} %copy-done, bf16[128,4096]{1,0:T(8,128)(2,1)} %copy-done.2, bf16[128,4096]{1,0:T(8,128)(2,1)} %collective-permute-done.refs_2_, bf16[128,4096]{1,0:T(8,128)(2,1)} %collective-permute-done.6.refs_3_, ...), custom_call_target="tpu_custom_call" | custom-call | flops 3221225472 | bytes 11853824 | tf_op jit(solution)/shard_map/pallas_call | solution.py:116
  103.0 5.4 %collective-permute-done.16.refs_11_ = bf16[128,4096]{1,0:T(8,128)(2,1)} collective-permute-done((bf16[128,4096]{1,0:T(8,128)(2,1)}, bf16[128,4096]{1,0:T(8,128)(2,1)}, u32[]{:S(2)}, u32[]{:S(2)}) %collective-permute-start.16) | collective-permute-done | bytes 1048608 | tf_op jit(solution)/shard_map/ppermute | solution.py:1102
  108.4 13.6 %shard_map.293.refs_17_.refs_30_ = bf16[512,1024]{1,0:T(8,128)(2,1)} custom-call(s32[2]{0:T(128)} %bitcast.114, s32[512,1]{1,0:T(8,128)} %bitcast.100, bf16[512,3072]{1,0:T(8,128)(2,1)} %get-tuple-element.298.query.key.value, bf16[512,3072]{1,0:T(8,128)(2,1)} %get-tuple-element.298.query.key.value, bf16[512,3072]{1,0:T(8,128)(2,1)} %get-tuple-element.298.query.key.value), custom_call_target="tpu_custom_call" | custom-call | flops 536870912 | bytes 9439232 | tf_op jit(solution)/shard_map/pallas_call | solution.py:116
  122.9 8.0 %collective-permute-done.9.refs_2_ = bf16[128,4096]{1,0:T(8,128)(2,1)} collective-permute-done((bf16[128,4096]{1,0:T(8,128)(2,1)}, bf16[128,4096]{1,0:T(8,128)(2,1)}, u32[]{:S(2)}, u32[]{:S(2)}) %collective-permute-start.9) | collective-permute-done | bytes 1048608 | tf_op jit(solution)/shard_map/ppermute | solution.py:1102
  131.2 1.7 collective-permute-start.12
  132.9 9.2 %collective-permute-done.24.refs_3_.refs_19_ = bf16[128,4096]{1,0:T(8,128)(2,1)} collective-permute-done((bf16[128,4096]{1,0:T(8,128)(2,1)}, bf16[128,4096]{1,0:T(8,128)(2,1)}, u32[]{:S(2)}, u32[]{:S(2)}) %collective-permute-start.24) | collective-permute-done | bytes 1048608 | tf_op jit(solution)/shard_map/ppermute | solution.py:1102
  143.0 32.1 %shard_map.294 = (f32[512,1024]{1,0:T(8,128)}, bf16[512,16]{1,0:T(8,128)(2,1)}, bf16[512,1024]{1,0:T(8,128)(2,1)}, bf16[512,16]{1,0:T(8,128)(2,1)}, bf16[512,409...) custom-call(bf16[128,4096]{1,0:T(8,128)(2,1)} %copy-done, bf16[128,4096]{1,0:T(8,128)(2,1)} %copy-done.2, ...), custom_call_target="tpu_custom_call" | custom-call | flops 5368709120 | bytes 22183936 | tf_op jit(solution)/shard_map/pallas_call | solution.py:116
  179.1 13.2 %shard_map.295 = (f32[512,1024]{1,0:T(8,128)}, f32[512,16]{1,0:T(8,128)}, bf16[16,1024]{1,0:T(8,128)(2,1)}) custom-call(bf16[128,4096]{1,0:T(8,128)(2,1)} %get-tuple-element.291.refs_0_.refs_16_, bf16[128,4096]{1,0:T(8,128)(2,1)} %collective-permute-done.23.refs_1_.refs_17_, bf16[128,4096]{1,0:T(8,128)(2,1)} %collective-permute-done.5.refs_2_.refs_18_, ...), custom_call_target="tpu_custom_call" | custom-call | flops 4294967296 | bytes 15642624 | tf_op jit(solution)/shard_map/pallas_call | solution.py:116
  193.6 8.9 %collective-permute-done.20.refs_2_.refs_18_ = bf16[128,4096]{1,0:T(8,128)(2,1)} collective-permute-done((bf16[128,4096]{1,0:T(8,128)(2,1)}, bf16[128,4096]{1,0:T(8,128)(2,1)}, u32[]{:S(2)}, u32[]{:S(2)}) %collective-permute-start.20) | collective-permute-done | bytes 1048608 | tf_op jit(solution)/shard_map/ppermute | solution.py:1102
  204.6 9.1 %collective-permute-done.36.refs_11_ = bf16[128,4096]{1,0:T(8,128)(2,1)} collective-permute-done((bf16[128,4096]{1,0:T(8,128)(2,1)}, bf16[128,4096]{1,0:T(8,128)(2,1)}, u32[]{:S(2)}, u32[]{:S(2)}) %collective-permute-start.36) | collective-permute-done | bytes 1048608 | tf_op jit(solution)/shard_map/ppermute | solution.py:1102
  215.0 12.8 %shard_map.296 = (bf16[64,1024]{1,0:T(8,128)(2,1)}, bf16[512,2048]{1,0:T(8,128)(2,1)}, bf16[512,1024]{1,0:T(8,128)(2,1)}, bf16[64,1024]{1,0:T(8,128)(2,1)}, bf16...) custom-call(s32[64]{0:T(128)} %add.217.index, bf16[128,4096]{1,0:T(8,128)(2,1)} %get-tuple-element.299.refs_0_, ...), custom_call_target="tpu_custom_call" | custom-call | flops 2147483648 | bytes 11591680 | tf_op jit(solution)/shard_map/pallas_call | solution.py:116
  230.3 5.9 %collective-permute-done.27.refs_3_.refs_19_ = bf16[128,4096]{1,0:T(8,128)(2,1)} collective-permute-done((bf16[128,4096]{1,0:T(8,128)(2,1)}, bf16[128,4096]{1,0:T(8,128)(2,1)}, u32[]{:S(2)}, u32[]{:S(2)}) %collective-permute-start.27) | collective-permute-done | bytes 1048608 | tf_op jit(solution)/shard_map/ppermute | solution.py:1102
  236.2 5.6 %shard_map.297.refs_17_.refs_30_ = bf16[64,1024]{1,0:T(8,128)(2,1)} custom-call(s32[2]{0:T(128)} %bitcast.115, s32[64,1]{1,0:T(8,128)} %copy.89.slots, bf16[64,1024]{1,0:T(8,128)(2,1)} %get-tuple-element.323.query, bf16[512,2048]{1,0:T(8,128)(2,1)} %get-tuple-element.324.key.value, bf16[512,2048]{1,0:T(8,128)(2,1)} %get-tuple-element.324.key.value), custom_call_target="tpu_custom_call" | custom-call | flops 67108864 | bytes 4325632 | tf_op jit(solution)/shard_map/pallas_call | solution.py:116
  241.8 10.6 %shard_map.298 = (f32[64,1024]{1,0:T(8,128)}, bf16[64,16]{1,0:T(8,128)(2,1)}, bf16[64,1024]{1,0:T(8,128)(2,1)}, bf16[64,16]{1,0:T(8,128)(2,1)}, bf16[64,4096]{1,0:T(8,128)(2,1)}, /*index=5*/bf16[64,4096]{1,0:T(8,128)(2,1)}) custom-call(bf16[128,4096]{1,0:T(8,128)(2,1)} %get-tuple-element.299.refs_0_, bf16[128,4096]{1,0:T(8,128)(2,1)} %collective-permute-done.31.refs_1_, ...), custom_call_target="tpu_custom_call" | custom-call | flops 671088640 | bytes 19169280 | tf_op jit(solution)/shard_map/pallas_call | solution.py:116
  253.1 2.6 collective-permute-done.41.refs_7_.refs_23_
  255.7 7.4 %shard_map.299 = (f32[64,1024]{1,0:T(8,128)}, f32[64,16]{1,0:T(8,128)}, bf16[64,1024]{1,0:T(8,128)(2,1)}) custom-call(bf16[128,4096]{1,0:T(8,128)(2,1)} %get-tuple-element.309.refs_0_.refs_16_, bf16[128,4096]{1,0:T(8,128)(2,1)} %collective-permute-done.19.refs_1_.refs_17_, bf16[128,4096]{1,0:T(8,128)(2,1)} %collective-permute-done.20.refs_2_.refs_18_, ...), custom_call_target="tpu_custom_call" | custom-call | flops 536870912 | bytes 10137600 | tf_op jit(solution)/shard_map/pallas_call | solution.py:116
  264.1 18.7 %all_to_all.81 = bf16[8,64,1024]{2,1,0:T(8,128)(2,1)} all-to-all(bf16[8,64,1024]{2,1,0:T(8,128)(2,1)S(1)} %tile.16), channel_id=1, replica_groups=mesh['dp'=4,'fsdp'=8] {'fsdp'}, dimensions={0} | all-to-all | bytes 2097152 | tf_op jit(solution)/shard_map/all_to_all | solution.py:1147
  282.8 23.2 %shard_map.300 = bf16[512,1152]{1,0:T(8,128)(2,1)} custom-call(bf16[512,1024]{1,0:T(8,128)(2,1)} %bitcast.101, bf16[6288,1024]{1,0:T(8,128)(2,1)} %table.1), custom_call_target="tpu_custom_call" | custom-call | flops 13186891776 | bytes 13926400 | tf_op jit(solution)/shard_map/pallas_call | solution.py:116
  306.0 4.8 %all-to-all-start.5 = ((bf16[8,64,1152]{2,1,0:T(8,128)(2,1)}), bf16[8,64,1152]{2,1,0:T(8,128)(2,1)}, u32[]{:S(2)}, u32[]{:S(2)}) async-start(bf16[8,64,1152]{2,1,0:T(8,128)(2,1)} %bitcast.99), calls=%async_computation.5 | async-start | bytes 2359296 | tf_op jit(solution)/shard_map/all_to_all | solution.py:1155
  312.2 15.3 %all-to-all-done.5.parts = bf16[8,64,1152]{2,1,0:T(8,128)(2,1)} async-done(((bf16[8,64,1152]{2,1,0:T(8,128)(2,1)}), bf16[8,64,1152]{2,1,0:T(8,128)(2,1)}, u32[]{:S(2)}, u32[]{:S(2)}) %all-to-all-start.5) | async-done | bytes 1179680 | tf_op jit(solution)/shard_map/all_to_all | solution.py:1155
  327.6 3.0 shard_map.301
  330.6 15.4 %shard_map.302 = (f32[64,1024]{1,0:T(8,128)}, bf16[64,1024]{1,0:T(8,128)(2,1)}, f32[16,1024]{1,0:T(8,128)}, f32[16,4096]{1,0:T(8,128)}, f32[16,4096]{1,0:T(8,128...) custom-call(bf16[128,4096]{1,0:T(8,128)(2,1)} %get-tuple-element.299.refs_0_, ...), custom_call_target="tpu_custom_call" | custom-call | flops 1207959552 | bytes 29540352 | tf_op jit(solution)/shard_map/pallas_call | solution.py:116
  346.0 6.6 %shard_map.303 = (bf16[64,1024]{1,0:T(8,128)(2,1)}, bf16[512,1024]{1,0:T(8,128)(2,1)}, bf16[512,1024]{1,0:T(8,128)(2,1)}) custom-call(s32[2]{0:T(128)} %bitcast.116, s32[64,1]{1,0:T(8,128)} %copy.89.slots, bf16[64,1024]{1,0:T(8,128)(2,1)} %get-tuple-element.323.query, bf16[512,2048]{1,0:T(8,128)(2,1)} %get-tuple-element.324.key.value, ...), custom_call_target="tpu_custom_call" | custom-call | flops 167772160 | bytes 4456704 | tf_op jit(solution)/shard_map/pallas_call | solution.py:116
  353.2 15.1 %shard_map.304 = (f32[512,1024]{1,0:T(8,128)}, f32[16,3072]{1,0:T(8,128)}, f32[16,1024]{1,0:T(8,128)}) custom-call(s32[64]{0:T(128)} %add.217.index, bf16[128,4096]{1,0:T(8,128)(2,1)} %get-tuple-element.299.refs_0_, bf16[128,4096]{1,0:T(8,128)(2,1)} %collective-permute-done.31.refs_1_, bf16[128,4096]{1,0:T(8,128)(2,1)} %collective-permute-done.9.refs_2_, ...), custom_call_target="tpu_custom_call" | custom-call | flops 2147483648 | bytes 15067136 | tf_op jit(solution)/shard_map/pallas_call | solution.py:116
  368.3 30.4 %shard_map.305 = (f32[512,1024]{1,0:T(8,128)}, bf16[512,1024]{1,0:T(8,128)(2,1)}, f32[16,1024]{1,0:T(8,128)}, f32[16,4096]{1,0:T(8,128)}, f32[16,4096]{1,0:T(8,1...) custom-call(bf16[128,4096]{1,0:T(8,128)(2,1)} %copy-done, bf16[128,4096]{1,0:T(8,128)(2,1)} %copy-done.2, ...), custom_call_target="tpu_custom_call" | custom-call | flops 9663676416 | bytes 42442752 | tf_op jit(solution)/shard_map/pallas_call | solution.py:116
  399.2 17.6 %shard_map.306 = (bf16[512,1024]{1,0:T(8,128)(2,1)}, bf16[512,1024]{1,0:T(8,128)(2,1)}, bf16[512,1024]{1,0:T(8,128)(2,1)}) custom-call(s32[2]{0:T(128)} %bitcast.117, s32[2,1,256]{2,1,0:T(1,128)} %reshape_tile.7.slots, bf16[512,3072]{1,0:T(8,128)(2,1)} %get-tuple-element.298.query.key.value, bf16[512,3072]{1,0:T(8,128)(2,1)} %get-tuple-element.298.query.key.value, ...), custom_call_target="tpu_custom_call" | custom-call | flops 1342177280 | bytes 10487808 | tf_op jit(solution)/shard_map/pallas_call | solution.py:116
  418.8 4.7 shard_map.307
  423.4 2.5 shard_map.308
  425.9 3.5 all-to-all-start.6
  429.4 10.0 %all-to-all-done.6 = f32[8,8,2176]{2,1,0:T(8,128)S(1)} async-done(((f32[8,8,2176]{2,1,0:T(8,128)}), f32[8,8,2176]{2,1,0:T(8,128)S(1)}, u32[]{:S(2)}, u32[]{:S(2)}) %all-to-all-start.6) | async-done | bytes 557088 | tf_op jit(solution)/shard_map/all_to_all | solution.py:1155
  441.1 2.6 collective-permute-start.43
  449.0 3.7 all-to-all-start.7
  454.1 8.7 %all-to-all-done.7 = f32[8,8,2176]{2,1,0:T(8,128)S(1)} async-done(((f32[8,8,2176]{2,1,0:T(8,128)}), f32[8,8,2176]{2,1,0:T(8,128)S(1)}, u32[]{:S(2)}, u32[]{:S(2)}) %all-to-all-start.7) | async-done | bytes 557088 | tf_op jit(solution)/shard_map/all_to_all | solution.py:1147
  (210 shorter events, 53.0 us)
Async XLA Ops:
  3.5 8.6 %collective-permute-start.1 = (bf16[128,4096]{1,0:T(8,128)(2,1)S(1)}, bf16[128,4096]{1,0:T(8,128)(2,1)S(1)}, u32[]{:S(2)}, u32[]{:S(2)}) collective-permute-start(bf16[128,4096]{1,0:T(8,128)(2,1)S(1)} %get-tuple-element.492.refs_0_), channel_id=1, source_target_pairs={{0,1},{1,0},{2,3},{3,2},{4,5},{5,4},{6,7},{7,6},{8,9},{9,8},{10,11... | collective-permute-start | bytes 3145736 | tf_op jit(solution)/shard_map/ppermute | solution.py:1093
  3.9 18.6 %collective-permute-start = (bf16[128,4096]{1,0:T(8,128)(2,1)S(1)}, bf16[128,4096]{1,0:T(8,128)(2,1)}, u32[]{:S(2)}, u32[]{:S(2)}) collective-permute-start(bf16[128,4096]{1,0:T(8,128)(2,1)S(1)} %get-tuple-element.492.refs_0_), channel_id=1, source_target_pairs={{0,2},{1,5},{2,0},{3,7},{4,6},{5,1},{6,4},{7,3},{8,10},{9,13},{10,... | collective-permute-start | bytes 3145736 | tf_op jit(solution)/shard_map/ppermute | solution.py:1102
  14.1 8.3 %all-to-all-start.2 = ((bf16[8,2,1745]{2,1,0:T(2,128)(2,1)}), bf16[8,2,1745]{2,1,0:T(2,128)(2,1)S(1)}, u32[]{:S(2)}, u32[]{:S(2)}) async-start(bf16[8,2,1745]{2,1,0:T(2,128)(2,1)} %reshape.646), calls=%async_computation.2 | async-start | bytes 114688 | tf_op jit(solution)/shard_map/all_to_all | solution.py:1063
  22.5 4.9 %collective-permute-start.3 = (bf16[128,4096]{1,0:T(8,128)(2,1)}, bf16[128,4096]{1,0:T(8,128)(2,1)}, u32[]{:S(2)}, u32[]{:S(2)}) collective-permute-start(bf16[128,4096]{1,0:T(8,128)(2,1)} %collective-permute-done.refs_2_), channel_id=1, source_target_pairs={{0,1},{1,0},{2,3},{3,2},{4,5},{5,4},{6,7},{7,6},{8,9},{9,8},{10,11... | collective-permute-start | bytes 3145736 | tf_op jit(solution)/shard_map/ppermute | solution.py:1093
  25.3 26.9 %collective-permute-start.6 = (bf16[128,4096]{1,0:T(8,128)(2,1)S(1)}, bf16[128,4096]{1,0:T(8,128)(2,1)}, u32[]{:S(2)}, u32[]{:S(2)}) collective-permute-start(bf16[128,4096]{1,0:T(8,128)(2,1)S(1)} %collective-permute-done.1.refs_1_), channel_id=1, source_target_pairs={{0,2},{1,5},{2,0},{3,7},{4,6},{5,1},{6,4},{7,3},{8,10},{9,13},{10,... | collective-permute-start | bytes 3145736 | tf_op jit(solution)/shard_map/ppermute | solution.py:1102
  38.3 22.1 %all-to-all-start.3 = ((bf16[8,80,1024]{2,1,0:T(8,128)(2,1)}), bf16[8,80,1024]{2,1,0:T(8,128)(2,1)S(1)}, u32[]{:S(2)}, u32[]{:S(2)}) async-start(bf16[8,80,1024]{2,1,0:T(8,128)(2,1)} %bitcast.98), calls=%async_computation.3 | async-start | bytes 2621440 | tf_op jit(solution)/shard_map/all_to_all | solution.py:1063
  42.2 28.6 %collective-permute-start.4 = (bf16[128,4096]{1,0:T(8,128)(2,1)}, bf16[128,4096]{1,0:T(8,128)(2,1)}, u32[]{:S(2)}, u32[]{:S(2)}) collective-permute-start(bf16[128,4096]{1,0:T(8,128)(2,1)} %collective-permute-done.3.refs_4_), channel_id=1, source_target_pairs={{0,2},{1,5},{2,0},{3,7},{4,6},{5,1},{6,4},{7,3},{8,10},{9,13},{10,... | collective-permute-start | bytes 3145736 | tf_op jit(solution)/shard_map/ppermute | solution.py:1102
  44.3 37.7 %collective-permute-start.2 = (bf16[128,4096]{1,0:T(8,128)(2,1)S(1)}, bf16[128,4096]{1,0:T(8,128)(2,1)}, u32[]{:S(2)}, u32[]{:S(2)}) collective-permute-start(bf16[128,4096]{1,0:T(8,128)(2,1)S(1)} %get-tuple-element.285.refs_8_), channel_id=1, source_target_pairs={{0,2},{1,5},{2,0},{3,7},{4,6},{5,1},{6,4},{7,3},{8,10},{9,13},{10,... | collective-permute-start | bytes 3145736 | tf_op jit(solution)/shard_map/ppermute | solution.py:1102
  49.8 32.6 %collective-permute-start.15 = (bf16[128,4096]{1,0:T(8,128)(2,1)S(1)}, bf16[128,4096]{1,0:T(8,128)(2,1)}, u32[]{:S(2)}, u32[]{:S(2)}) collective-permute-start(bf16[128,4096]{1,0:T(8,128)(2,1)S(1)} %get-tuple-element.285.refs_8_), channel_id=1, source_target_pairs={{0,1},{1,0},{2,3},{3,2},{4,5},{5,4},{6,7},{7,6},{8,9},{9,8},{10,11... | collective-permute-start | bytes 3145736 | tf_op jit(solution)/shard_map/ppermute | solution.py:1093
  52.2 36.1 %collective-permute-start.7 = (bf16[128,4096]{1,0:T(8,128)(2,1)}, bf16[128,4096]{1,0:T(8,128)(2,1)}, u32[]{:S(2)}, u32[]{:S(2)}) collective-permute-start(bf16[128,4096]{1,0:T(8,128)(2,1)} %collective-permute-done.6.refs_3_), channel_id=1, source_target_pairs={{0,1},{1,0},{2,3},{3,2},{4,5},{5,4},{6,7},{7,6},{8,9},{9,8},{10,11... | collective-permute-start | bytes 3145736 | tf_op jit(solution)/shard_map/ppermute | solution.py:1093
  70.8 17.8 %collective-permute-start.8 = (bf16[128,4096]{1,0:T(8,128)(2,1)}, bf16[128,4096]{1,0:T(8,128)(2,1)}, u32[]{:S(2)}, u32[]{:S(2)}) collective-permute-start(bf16[128,4096]{1,0:T(8,128)(2,1)} %collective-permute-done.4.refs_6_), channel_id=1, source_target_pairs={{0,1},{1,0},{2,3},{3,2},{4,5},{5,4},{6,7},{7,6},{8,9},{9,8},{10,11... | collective-permute-start | bytes 3145736 | tf_op jit(solution)/shard_map/ppermute | solution.py:1093
  82.0 18.0 %collective-permute-start.5 = (bf16[128,4096]{1,0:T(8,128)(2,1)}, bf16[128,4096]{1,0:T(8,128)(2,1)}, u32[]{:S(2)}, u32[]{:S(2)}) collective-permute-start(bf16[128,4096]{1,0:T(8,128)(2,1)} %get-tuple-element.291.refs_0_.refs_16_), channel_id=1, source_target_pairs={{0,2},{1,5},{2,0},{3,7},{4,6},{5,1},{6,4},{7,3},{8,10},{9,13},{10,... | collective-permute-start | bytes 3145736 | tf_op jit(solution)/shard_map/ppermute | solution.py:1102
  82.4 17.6 %collective-permute-start.10 = (bf16[128,4096]{1,0:T(8,128)(2,1)}, bf16[128,4096]{1,0:T(8,128)(2,1)}, u32[]{:S(2)}, u32[]{:S(2)}) collective-permute-start(bf16[128,4096]{1,0:T(8,128)(2,1)} %collective-permute-done.2.refs_10_), channel_id=1, source_target_pairs={{0,1},{1,0},{2,3},{3,2},{4,5},{5,4},{6,7},{7,6},{8,9},{9,8},{10,11... | collective-permute-start | bytes 3145736 | tf_op jit(solution)/shard_map/ppermute | solution.py:1093
  82.4 26.0 %collective-permute-start.16 = (bf16[128,4096]{1,0:T(8,128)(2,1)}, bf16[128,4096]{1,0:T(8,128)(2,1)}, u32[]{:S(2)}, u32[]{:S(2)}) collective-permute-start(bf16[128,4096]{1,0:T(8,128)(2,1)} %collective-permute-done.15.refs_9_), channel_id=1, source_target_pairs={{0,2},{1,5},{2,0},{3,7},{4,6},{5,1},{6,4},{7,3},{8,10},{9,13},{10,... | collective-permute-start | bytes 3145736 | tf_op jit(solution)/shard_map/ppermute | solution.py:1102
  88.3 33.7 %collective-permute-start.23 = (bf16[128,4096]{1,0:T(8,128)(2,1)}, bf16[128,4096]{1,0:T(8,128)(2,1)}, u32[]{:S(2)}, u32[]{:S(2)}) collective-permute-start(bf16[128,4096]{1,0:T(8,128)(2,1)} %get-tuple-element.291.refs_0_.refs_16_), channel_id=1, source_target_pairs={{0,1},{1,0},{2,3},{3,2},{4,5},{5,4},{6,7},{7,6},{8,9},{9,8},{10,11... | collective-permute-start | bytes 3145736 | tf_op jit(solution)/shard_map/ppermute | solution.py:1093
  100.0 22.5 %collective-permute-start.11 = (bf16[128,4096]{1,0:T(8,128)(2,1)}, bf16[128,4096]{1,0:T(8,128)(2,1)}, u32[]{:S(2)}, u32[]{:S(2)}) collective-permute-start(bf16[128,4096]{1,0:T(8,128)(2,1)} %collective-permute-done.10.refs_12_), channel_id=1, source_target_pairs={{0,2},{1,5},{2,0},{3,7},{4,6},{5,1},{6,4},{7,3},{8,10},{9,13},{10,... | collective-permute-start | bytes 3145736 | tf_op jit(solution)/shard_map/ppermute | solution.py:1102
  101.6 29.3 %collective-permute-start.9 = (bf16[128,4096]{1,0:T(8,128)(2,1)}, bf16[128,4096]{1,0:T(8,128)(2,1)}, u32[]{:S(2)}, u32[]{:S(2)}) collective-permute-start(bf16[128,4096]{1,0:T(8,128)(2,1)} %get-tuple-element.299.refs_0_), channel_id=1, source_target_pairs={{0,2},{1,5},{2,0},{3,7},{4,6},{5,1},{6,4},{7,3},{8,10},{9,13},{10,... | collective-permute-start | bytes 3145736 | tf_op jit(solution)/shard_map/ppermute | solution.py:1102
  102.1 28.7 %collective-permute-start.13 = (bf16[128,4096]{1,0:T(8,128)(2,1)}, bf16[128,4096]{1,0:T(8,128)(2,1)}, u32[]{:S(2)}, u32[]{:S(2)}) collective-permute-start(bf16[128,4096]{1,0:T(8,128)(2,1)} %collective-permute-done.5.refs_2_.refs_18_), channel_id=1, source_target_pairs={{0,1},{1,0},{2,3},{3,2},{4,5},{5,4},{6,7},{7,6},{8,9},{9,8},{10,11... | collective-permute-start | bytes 3145736 | tf_op jit(solution)/shard_map/ppermute | solution.py:1093
  108.4 22.8 %collective-permute-start.17 = (bf16[128,4096]{1,0:T(8,128)(2,1)}, bf16[128,4096]{1,0:T(8,128)(2,1)}, u32[]{:S(2)}, u32[]{:S(2)}) collective-permute-start(bf16[128,4096]{1,0:T(8,128)(2,1)} %collective-permute-done.16.refs_11_), channel_id=1, source_target_pairs={{0,1},{1,0},{2,3},{3,2},{4,5},{5,4},{6,7},{7,6},{8,9},{9,8},{10,11... | collective-permute-start | bytes 3145736 | tf_op jit(solution)/shard_map/ppermute | solution.py:1093
  122.0 20.1 %collective-permute-start.31 = (bf16[128,4096]{1,0:T(8,128)(2,1)}, bf16[128,4096]{1,0:T(8,128)(2,1)}, u32[]{:S(2)}, u32[]{:S(2)}) collective-permute-start(bf16[128,4096]{1,0:T(8,128)(2,1)} %get-tuple-element.299.refs_0_), channel_id=1, source_target_pairs={{0,1},{1,0},{2,3},{3,2},{4,5},{5,4},{6,7},{7,6},{8,9},{9,8},{10,11... | collective-permute-start | bytes 3145736 | tf_op jit(solution)/shard_map/ppermute | solution.py:1093
  122.5 19.6 %collective-permute-start.24 = (bf16[128,4096]{1,0:T(8,128)(2,1)}, bf16[128,4096]{1,0:T(8,128)(2,1)}, u32[]{:S(2)}, u32[]{:S(2)}) collective-permute-start(bf16[128,4096]{1,0:T(8,128)(2,1)} %collective-permute-done.23.refs_1_.refs_17_), channel_id=1, source_target_pairs={{0,2},{1,5},{2,0},{3,7},{4,6},{5,1},{6,4},{7,3},{8,10},{9,13},{10,... | collective-permute-start | bytes 3145736 | tf_op jit(solution)/shard_map/ppermute | solution.py:1102
  130.9 11.8 %collective-permute-start.18 = (bf16[128,4096]{1,0:T(8,128)(2,1)}, bf16[128,4096]{1,0:T(8,128)(2,1)}, u32[]{:S(2)}, u32[]{:S(2)}) collective-permute-start(bf16[128,4096]{1,0:T(8,128)(2,1)} %collective-permute-done.11.refs_14_), channel_id=1, source_target_pairs={{0,1},{1,0},{2,3},{3,2},{4,5},{5,4},{6,7},{7,6},{8,9},{9,8},{10,11... | collective-permute-start | bytes 3145736 | tf_op jit(solution)/shard_map/ppermute | solution.py:1093
  130.9 44.2 %collective-permute-start.14 = (bf16[128,4096]{1,0:T(8,128)(2,1)}, bf16[128,4096]{1,0:T(8,128)(2,1)}, u32[]{:S(2)}, u32[]{:S(2)}) collective-permute-start(bf16[128,4096]{1,0:T(8,128)(2,1)} %collective-permute-done.13.refs_4_.refs_20_), channel_id=1, source_target_pairs={{0,2},{1,5},{2,0},{3,7},{4,6},{5,1},{6,4},{7,3},{8,10},{9,13},{10,... | collective-permute-start | bytes 3145736 | tf_op jit(solution)/shard_map/ppermute | solution.py:1102
  131.2 44.9 %collective-permute-start.12 = (bf16[128,4096]{1,0:T(8,128)(2,1)}, bf16[128,4096]{1,0:T(8,128)(2,1)}, u32[]{:S(2)}, u32[]{:S(2)}) collective-permute-start(bf16[128,4096]{1,0:T(8,128)(2,1)} %get-tuple-element.303.refs_8_), channel_id=1, source_target_pairs={{0,2},{1,5},{2,0},{3,7},{4,6},{5,1},{6,4},{7,3},{8,10},{9,13},{10,... | collective-permute-start | bytes 3145736 | tf_op jit(solution)/shard_map/ppermute | solution.py:1102
  142.1 34.1 %collective-permute-start.21 = (bf16[128,4096]{1,0:T(8,128)(2,1)}, bf16[128,4096]{1,0:T(8,128)(2,1)}, u32[]{:S(2)}, u32[]{:S(2)}) collective-permute-start(bf16[128,4096]{1,0:T(8,128)(2,1)} %collective-permute-done.9.refs_2_), channel_id=1, source_target_pairs={{0,1},{1,0},{2,3},{3,2},{4,5},{5,4},{6,7},{7,6},{8,9},{9,8},{10,11... | collective-permute-start | bytes 3145736 | tf_op jit(solution)/shard_map/ppermute | solution.py:1093
  142.1 35.3 %collective-permute-start.25 = (bf16[128,4096]{1,0:T(8,128)(2,1)}, bf16[128,4096]{1,0:T(8,128)(2,1)}, u32[]{:S(2)}, u32[]{:S(2)}) collective-permute-start(bf16[128,4096]{1,0:T(8,128)(2,1)} %collective-permute-done.24.refs_3_.refs_19_), channel_id=1, source_target_pairs={{0,1},{1,0},{2,3},{3,2},{4,5},{5,4},{6,7},{7,6},{8,9},{9,8},{10,11... | collective-permute-start | bytes 3145736 | tf_op jit(solution)/shard_map/ppermute | solution.py:1093
  142.6 35.6 %collective-permute-start.32 = (bf16[128,4096]{1,0:T(8,128)(2,1)}, bf16[128,4096]{1,0:T(8,128)(2,1)}, u32[]{:S(2)}, u32[]{:S(2)}) collective-permute-start(bf16[128,4096]{1,0:T(8,128)(2,1)} %collective-permute-done.31.refs_1_), channel_id=1, source_target_pairs={{0,2},{1,5},{2,0},{3,7},{4,6},{5,1},{6,4},{7,3},{8,10},{9,13},{10,... | collective-permute-start | bytes 3145736 | tf_op jit(solution)/shard_map/ppermute | solution.py:1102
  176.1 16.2 %collective-permute-start.35 = (bf16[128,4096]{1,0:T(8,128)(2,1)}, bf16[128,4096]{1,0:T(8,128)(2,1)}, u32[]{:S(2)}, u32[]{:S(2)}) collective-permute-start(bf16[128,4096]{1,0:T(8,128)(2,1)} %get-tuple-element.303.refs_8_), channel_id=1, source_target_pairs={{0,1},{1,0},{2,3},{3,2},{4,5},{5,4},{6,7},{7,6},{8,9},{9,8},{10,11... | collective-permute-start | bytes 3145736 | tf_op jit(solution)/shard_map/ppermute | solution.py:1093
  176.2 16.3 %collective-permute-start.22 = (bf16[128,4096]{1,0:T(8,128)(2,1)}, bf16[128,4096]{1,0:T(8,128)(2,1)}, u32[]{:S(2)}, u32[]{:S(2)}) collective-permute-start(bf16[128,4096]{1,0:T(8,128)(2,1)} %collective-permute-done.21.refs_4_), channel_id=1, source_target_pairs={{0,2},{1,5},{2,0},{3,7},{4,6},{5,1},{6,4},{7,3},{8,10},{9,13},{10,... | collective-permute-start | bytes 3145736 | tf_op jit(solution)/shard_map/ppermute | solution.py:1102
  177.4 25.2 %collective-permute-start.20 = (bf16[128,4096]{1,0:T(8,128)(2,1)}, bf16[128,4096]{1,0:T(8,128)(2,1)}, u32[]{:S(2)}, u32[]{:S(2)}) collective-permute-start(bf16[128,4096]{1,0:T(8,128)(2,1)} %get-tuple-element.309.refs_0_.refs_16_), channel_id=1, source_target_pairs={{0,2},{1,5},{2,0},{3,7},{4,6},{5,1},{6,4},{7,3},{8,10},{9,13},{10,... | collective-permute-start | bytes 3145736 | tf_op jit(solution)/shard_map/ppermute | solution.py:1102
  178.2 24.3 %collective-permute-start.37 = (bf16[128,4096]{1,0:T(8,128)(2,1)}, bf16[128,4096]{1,0:T(8,128)(2,1)}, u32[]{:S(2)}, u32[]{:S(2)}) collective-permute-start(bf16[128,4096]{1,0:T(8,128)(2,1)} %collective-permute-done.12.refs_10_), channel_id=1, source_target_pairs={{0,1},{1,0},{2,3},{3,2},{4,5},{5,4},{6,7},{7,6},{8,9},{9,8},{10,11... | collective-permute-start | bytes 3145736 | tf_op jit(solution)/shard_map/ppermute | solution.py:1093
  178.7 25.0 %collective-permute-start.33 = (bf16[128,4096]{1,0:T(8,128)(2,1)}, bf16[128,4096]{1,0:T(8,128)(2,1)}, u32[]{:S(2)}, u32[]{:S(2)}) collective-permute-start(bf16[128,4096]{1,0:T(8,128)(2,1)} %collective-permute-done.32.refs_3_), channel_id=1, source_target_pairs={{0,1},{1,0},{2,3},{3,2},{4,5},{5,4},{6,7},{7,6},{8,9},{9,8},{10,11... | collective-permute-start | bytes 3145736 | tf_op jit(solution)/shard_map/ppermute | solution.py:1093
  192.3 21.5 %collective-permute-start.19 = (bf16[128,4096]{1,0:T(8,128)(2,1)}, bf16[128,4096]{1,0:T(8,128)(2,1)}, u32[]{:S(2)}, u32[]{:S(2)}) collective-permute-start(bf16[128,4096]{1,0:T(8,128)(2,1)} %get-tuple-element.309.refs_0_.refs_16_), channel_id=1, source_target_pairs={{0,1},{1,0},{2,3},{3,2},{4,5},{5,4},{6,7},{7,6},{8,9},{9,8},{10,11... | collective-permute-start | bytes 3145736 | tf_op jit(solution)/shard_map/ppermute | solution.py:1093
  192.5 21.3 %collective-permute-start.36 = (bf16[128,4096]{1,0:T(8,128)(2,1)}, bf16[128,4096]{1,0:T(8,128)(2,1)}, u32[]{:S(2)}, u32[]{:S(2)}) collective-permute-start(bf16[128,4096]{1,0:T(8,128)(2,1)} %collective-permute-done.35.refs_9_), channel_id=1, source_target_pairs={{0,2},{1,5},{2,0},{3,7},{4,6},{5,1},{6,4},{7,3},{8,10},{9,13},{10,... | collective-permute-start | bytes 3145736 | tf_op jit(solution)/shard_map/ppermute | solution.py:1102
  202.5 12.4 %collective-permute-start.34 = (bf16[128,4096]{1,0:T(8,128)(2,1)}, bf16[128,4096]{1,0:T(8,128)(2,1)}, u32[]{:S(2)}, u32[]{:S(2)}) collective-permute-start(bf16[128,4096]{1,0:T(8,128)(2,1)} %collective-permute-done.22.refs_6_), channel_id=1, source_target_pairs={{0,1},{1,0},{2,3},{3,2},{4,5},{5,4},{6,7},{7,6},{8,9},{9,8},{10,11... | collective-permute-start | bytes 3145736 | tf_op jit(solution)/shard_map/ppermute | solution.py:1093
  202.5 25.2 %collective-permute-start.39 = (bf16[128,4096]{1,0:T(8,128)(2,1)}, bf16[128,4096]{1,0:T(8,128)(2,1)}, u32[]{:S(2)}, u32[]{:S(2)}) collective-permute-start(bf16[128,4096]{1,0:T(8,128)(2,1)} %collective-permute-done.37.refs_12_), channel_id=1, source_target_pairs={{0,2},{1,5},{2,0},{3,7},{4,6},{5,1},{6,4},{7,3},{8,10},{9,13},{10,... | collective-permute-start | bytes 3145736 | tf_op jit(solution)/shard_map/ppermute | solution.py:1102
  203.7 24.4 %collective-permute-start.28 = (bf16[128,4096]{1,0:T(8,128)(2,1)}, bf16[128,4096]{1,0:T(8,128)(2,1)}, u32[]{:S(2)}, u32[]{:S(2)}) collective-permute-start(bf16[128,4096]{1,0:T(8,128)(2,1)} %collective-permute-done.20.refs_2_.refs_18_), channel_id=1, source_target_pairs={{0,1},{1,0},{2,3},{3,2},{4,5},{5,4},{6,7},{7,6},{8,9},{9,8},{10,11... | collective-permute-start | bytes 3145736 | tf_op jit(solution)/shard_map/ppermute | solution.py:1093
  213.8 28.1 %collective-permute-start.38 = (bf16[128,4096]{1,0:T(8,128)(2,1)}, bf16[128,4096]{1,0:T(8,128)(2,1)}, u32[]{:S(2)}, u32[]{:S(2)}) collective-permute-start(bf16[128,4096]{1,0:T(8,128)(2,1)} %collective-permute-done.36.refs_11_), channel_id=1, source_target_pairs={{0,1},{1,0},{2,3},{3,2},{4,5},{5,4},{6,7},{7,6},{8,9},{9,8},{10,11... | collective-permute-start | bytes 3145736 | tf_op jit(solution)/shard_map/ppermute | solution.py:1093
  213.8 22.5 %collective-permute-start.27 = (bf16[128,4096]{1,0:T(8,128)(2,1)}, bf16[128,4096]{1,0:T(8,128)(2,1)}, u32[]{:S(2)}, u32[]{:S(2)}) collective-permute-start(bf16[128,4096]{1,0:T(8,128)(2,1)} %collective-permute-done.19.refs_1_.refs_17_), channel_id=1, source_target_pairs={{0,2},{1,5},{2,0},{3,7},{4,6},{5,1},{6,4},{7,3},{8,10},{9,13},{10,... | collective-permute-start | bytes 3145736 | tf_op jit(solution)/shard_map/ppermute | solution.py:1102
  227.8 14.1 %collective-permute-start.40 = (bf16[128,4096]{1,0:T(8,128)(2,1)}, bf16[128,4096]{1,0:T(8,128)(2,1)}, u32[]{:S(2)}, u32[]{:S(2)}) collective-permute-start(bf16[128,4096]{1,0:T(8,128)(2,1)} %collective-permute-done.39.refs_14_), channel_id=1, source_target_pairs={{0,1},{1,0},{2,3},{3,2},{4,5},{5,4},{6,7},{7,6},{8,9},{9,8},{10,11... | collective-permute-start | bytes 3145736 | tf_op jit(solution)/shard_map/ppermute | solution.py:1093
  228.1 24.4 %collective-permute-start.30 = (bf16[128,4096]{1,0:T(8,128)(2,1)}, bf16[128,4096]{1,0:T(8,128)(2,1)}, u32[]{:S(2)}, u32[]{:S(2)}) collective-permute-start(bf16[128,4096]{1,0:T(8,128)(2,1)} %collective-permute-done.28.refs_4_.refs_20_), channel_id=1, source_target_pairs={{0,2},{1,5},{2,0},{3,7},{4,6},{5,1},{6,4},{7,3},{8,10},{9,13},{10,... | collective-permute-start | bytes 3145736 | tf_op jit(solution)/shard_map/ppermute | solution.py:1102
  236.2 16.8 %collective-permute-start.29 = (bf16[128,4096]{1,0:T(8,128)(2,1)}, bf16[128,4096]{1,0:T(8,128)(2,1)}, u32[]{:S(2)}, u32[]{:S(2)}) collective-permute-start(bf16[128,4096]{1,0:T(8,128)(2,1)} %collective-permute-done.27.refs_3_.refs_19_), channel_id=1, source_target_pairs={{0,1},{1,0},{2,3},{3,2},{4,5},{5,4},{6,7},{7,6},{8,9},{9,8},{10,11... | collective-permute-start | bytes 3145736 | tf_op jit(solution)/shard_map/ppermute | solution.py:1093
  306.0 21.6 %all-to-all-start.5 = ((bf16[8,64,1152]{2,1,0:T(8,128)(2,1)}), bf16[8,64,1152]{2,1,0:T(8,128)(2,1)}, u32[]{:S(2)}, u32[]{:S(2)}) async-start(bf16[8,64,1152]{2,1,0:T(8,128)(2,1)} %bitcast.99), calls=%async_computation.5 | async-start | bytes 2359296 | tf_op jit(solution)/shard_map/all_to_all | solution.py:1155
  425.9 13.6 %all-to-all-start.6 = ((f32[8,8,2176]{2,1,0:T(8,128)}), f32[8,8,2176]{2,1,0:T(8,128)S(1)}, u32[]{:S(2)}, u32[]{:S(2)}) async-start(f32[8,8,2176]{2,1,0:T(8,128)} %shard_map.308), calls=%async_computation.6 | async-start | bytes 1114112 | tf_op jit(solution)/shard_map/all_to_all | solution.py:1155
  439.5 6.2 %collective-permute-start.42 = (f32[8,2176]{1,0:T(8,128)S(1)}, f32[8,2176]{1,0:T(8,128)S(1)}, u32[]{:S(2)}, u32[]{:S(2)}) collective-permute-start(f32[8,2176]{1,0:T(8,128)S(1)} %reduce_sum.83), channel_id=1, source_target_pairs={{0,8},{8,16},{16,24},{24,0},{1,9},{9,17},{17,25},{25,1},{2,10},{10... | collective-permute-start | bytes 208904 | tf_op jit(solution)/shard_map/ppermute | solution.py:1166
  441.1 5.3 %collective-permute-start.43 = (f32[8,2176]{1,0:T(8,128)S(1)}, f32[8,2176]{1,0:T(8,128)S(1)}, u32[]{:S(2)}, u32[]{:S(2)}) collective-permute-start(f32[8,2176]{1,0:T(8,128)S(1)} %reduce_sum.83), channel_id=1, source_target_pairs={{0,16},{8,24},{16,0},{24,8},{1,17},{9,25},{17,1},{25,9},{2,18},{10... | collective-permute-start | bytes 208904 | tf_op jit(solution)/shard_map/ppermute | solution.py:1166
  443.7 4.3 collective-permute-start.44
  449.0 13.7 %all-to-all-start.7 = ((f32[8,8,2176]{2,1,0:T(8,128)}), f32[8,8,2176]{2,1,0:T(8,128)S(1)}, u32[]{:S(2)}, u32[]{:S(2)}) async-start(f32[8,8,2176]{2,1,0:T(8,128)} %tile.17), calls=%async_computation.7 | async-start | bytes 1114112 | tf_op jit(solution)/shard_map/all_to_all | solution.py:1147
  (28 other events, 261.7 us)
